TPU v7x, 256 devices: a whole 4x4x8 slice. The times are simulated.
256 devices in a mesh: lat: 8 (over y, x_hi), lon: 32 (over x_lo, z, core).
Axes of the slice: x: 4 (x_hi: 2, x_lo: 2; x = x_hi * 2 + x_lo), y: 4, z: 8, core: 2. Of those that a mesh axis runs over, the one named last changes fastest.
Arguments:
- features: bfloat16 [128, 384, 2048], P('lat', 'lon'), may hold values from -6 to 6
- atrous_kernel_weight: bfloat16 [9, 2048, 256], replicated, may hold values from -0.046875 to 0.046875
- point_weight: bfloat16 [2048, 256], replicated, may hold values from -0.125 to 0.125
- project_weight: bfloat16 [2, 256, 256], replicated, may hold values from -0.25 to 0.25
- upstream: bfloat16 [128, 384, 256], P('lat', 'lon'), may hold values from -6 to 6
- labels: int32 [128, 384], P('lat', 'lon'), may hold values from 0 to 2
- class_weights: float32 [3], replicated, may hold values from 0.5 to 4
Outputs:
- head_out: bfloat16 [128, 384, 256], P('lat', 'lon')
- input_grad: bfloat16 [128, 384, 2048], P('lat', 'lon')
- weight_grads: float32 [20992, 256], P('lon')
All inputs are finite; a program needn't handle non-finite values.
Results may differ from a plain program's by a relative error of at most 0.006.
Values may be sent and summed in bfloat16 or wider, within the bound.
No kernel may reach another device: no remote copies, remote signals or barrier semaphores. Data moves between devices by JAX's collectives and lax.ppermute only.
A program may use at most 128 MiB of HBM per device.

v0:
```python
import jax
import jax.numpy as jnp
from jax import lax
from jax.sharding import PartitionSpec as P

ATROUS_DILATION = 36


def shifted(value, axis, by):
    count = lax.axis_size(axis)
    pairs = [(i, i + by) for i in range(count) if 0 <= i + by < count]
    return lax.ppermute(value, axis, pairs)


def shifted_2(block, axis, distance):
    devices = range(lax.axis_size(axis))
    route = [((i - distance) % len(devices), i) for i in devices]
    return lax.ppermute(block, axis, route)


def contract_row_axes(left, right):
    return lax.dot_general(
        left, right, (((0,), (0,)), ((), ())), preferred_element_type=jnp.float32
    )


def multiply_transposed(left, right):
    return lax.dot_general(
        left, right, (((1,), (1,)), ((), ())), preferred_element_type=jnp.float32
    )


def silu_slope(value):
    sigmoid_value = jax.nn.sigmoid(value)
    return sigmoid_value * (1.0 + value * (1.0 - sigmoid_value))


def roll_tensor(entry_bytesize, tensor_mode, step_distance, holder_tensor):
    if step_distance == 0:
        return entry_bytesize
    tile_size = entry_bytesize.shape[tensor_mode]
    whole_patches, leftover_rows = divmod(abs(step_distance), tile_size)
    segment_sequence = []
    if step_distance > 0:
        closest_edge = lax.slice_in_dim(entry_bytesize, leftover_rows, tile_size, axis=tensor_mode)
        segment_sequence.append(holder_tensor(closest_edge, -whole_patches))
        if leftover_rows > 0:
            segment_sequence.append(
                holder_tensor(
                    lax.slice_in_dim(entry_bytesize, 0, leftover_rows, axis=tensor_mode),
                    -(whole_patches + 1),
                )
            )
    else:
        if leftover_rows > 0:
            segment_sequence.append(
                holder_tensor(
                    lax.slice_in_dim(
                        entry_bytesize, tile_size - leftover_rows, tile_size, axis=tensor_mode
                    ),
                    whole_patches + 1,
                )
            )
        closest_edge = lax.slice_in_dim(
            entry_bytesize, 0, tile_size - leftover_rows, axis=tensor_mode
        )
        segment_sequence.append(holder_tensor(closest_edge, whole_patches))
    if len(segment_sequence) == 1:
        return segment_sequence[0]
    return jnp.concatenate(segment_sequence, axis=tensor_mode)


def neighbour_window(
    entry_bytesize, hole_stride, north_south_holder, east_west_holder, direction_choice
):
    last_width = entry_bytesize.shape[-1]
    shifted_taps = {}
    for upward_direction in (-1, 0, 1):
        displaced_field = roll_tensor(
            entry_bytesize, 0, direction_choice * upward_direction * hole_stride, north_south_holder
        )
        for across_axis in (-1, 0, 1):
            shifted_taps[upward_direction, across_axis] = roll_tensor(
                displaced_field, 1, direction_choice * across_axis * hole_stride, east_west_holder
            )
    return [
        shifted_taps[upward_direction, across_axis].reshape(-1, last_width)
        for upward_direction in (-1, 0, 1)
        for across_axis in (-1, 0, 1)
    ]


def shards(
    features, atrous_kernel_weight, point_weight, project_weight, upstream, labels, class_weights
):
    tile_rows, tile_cols, in_width = features.shape
    channel_count = point_weight.shape[1]

    def shift_feature_row_list(portion, step_distance):
        return shifted(portion, "lat", step_distance)

    def shift_feature_columns(portion, step_distance):
        return shifted_2(portion, "lon", step_distance)

    def shift_cotangent_row_list(portion, step_distance):
        return shifted(portion, "lat", step_distance)

    def shift_cotangent_columns(portion, step_distance):
        return shifted_2(portion, "lon", step_distance)

    feature_tap_list = neighbour_window(
        features, ATROUS_DILATION, shift_feature_row_list, shift_feature_columns, 1
    )
    flattened = features.reshape(-1, in_width)
    point_pre = jnp.dot(flattened, point_weight, preferred_element_type=jnp.float32)
    running_total = jnp.zeros((tile_rows * tile_cols, channel_count), jnp.float32)
    for kernel_tap_index in range(9):
        running_total = running_total + jnp.dot(
            feature_tap_list[kernel_tap_index],
            atrous_kernel_weight[kernel_tap_index],
            preferred_element_type=jnp.float32,
        )
    pre_list = [point_pre, running_total]
    activations = [jax.nn.silu(pre).astype(jnp.bfloat16) for pre in pre_list]
    mixed_sum = jnp.dot(activations[0], project_weight[0], preferred_element_type=jnp.float32)
    mixed_sum = mixed_sum + jnp.dot(
        activations[1], project_weight[1], preferred_element_type=jnp.float32
    )
    head_out = jax.nn.silu(mixed_sum).astype(jnp.bfloat16)
    class_index = jnp.arange(3, dtype=jnp.int32)
    pixel_weight = jnp.sum(
        jnp.where(labels[..., None] == class_index, class_weights, 0.0), axis=-1
    ).reshape(-1, 1)
    out_grad = (
        upstream.reshape(-1, channel_count).astype(jnp.float32)
        * pixel_weight
        * silu_slope(mixed_sum)
    ).astype(jnp.bfloat16)
    branch_gradient_list = [
        (
            multiply_transposed(out_grad, project_weight[branch]) * silu_slope(pre_list[branch])
        ).astype(jnp.bfloat16)
        for branch in range(2)
    ]
    gradient_field = branch_gradient_list[1].reshape(tile_rows, tile_cols, channel_count)
    cotangent_tap_list = neighbour_window(
        gradient_field, ATROUS_DILATION, shift_cotangent_row_list, shift_cotangent_columns, -1
    )
    gradient_blocks = []
    summed_input = multiply_transposed(branch_gradient_list[0], point_weight)
    for kernel_tap_index in range(9):
        gradient_blocks.append(
            contract_row_axes(feature_tap_list[kernel_tap_index], branch_gradient_list[1])
        )
        summed_input = summed_input + multiply_transposed(
            cotangent_tap_list[kernel_tap_index], atrous_kernel_weight[kernel_tap_index]
        )
    for branch in range(2):
        gradient_blocks.append(contract_row_axes(activations[branch], out_grad))
    gradient_blocks.append(contract_row_axes(flattened, branch_gradient_list[0]))
    local_terms = jnp.concatenate(gradient_blocks, axis=0)
    longitude_sum = lax.psum_scatter(local_terms, "lon", scatter_dimension=0, tiled=True)
    weight_grads = lax.psum(longitude_sum, "lat")
    head_tile = head_out.reshape(tile_rows, tile_cols, channel_count)
    grad_tile = summed_input.astype(jnp.bfloat16).reshape(tile_rows, tile_cols, in_width)
    return (head_tile, grad_tile, weight_grads)


def solution(mesh):
    placed = (P("lat", "lon", None), P(), P(), P(), P("lat", "lon", None), P("lat", "lon"), P())
    return jax.shard_map(
        shards,
        mesh=mesh,
        in_specs=placed,
        out_specs=(P("lat", "lon", None), P("lat", "lon", None), P("lon", None)),
        check_vma=False,
    )
```

profile of v0, /device:TPU:32, one launch (start us, length us, event | category | flops | bytes accessed | tf_op | source)
XLA Modules:
  0.0 409.9 jit_solution(15401529797206073239)
XLA Ops:
  8.7 4.5 %collective-permute-start.5 = (bf16[16,12,2048]{2,0,1:T(8,128)(2,1)}, bf16[16,12,2048]{2,0,1:T(8,128)(2,1)}, u32[]{:S(2)}, u32[]{:S(2)}) collective-permute-start(bf16[16,12,2048]{2,0,1:T(8,128)(2,1)} %param.7), channel_id=1, source_target_pairs={{3,0},{4,1},{5,2},{6,3},{7,4},{8,5},{9,6},{10,7},{11,8},{12,9},{13... | collective-permute-start | bytes 2359304 | tf_op jit(solution)/shard_map/ppermute | solution.py:18
  13.2 2.9 fusion.76
  16.1 4.4 %collective-permute-start.1 = (bf16[12,12,2048]{2,0,1:T(8,128)(2,1)}, bf16[12,12,2048]{2,0,1:T(8,128)(2,1)}, u32[]{:S(2)}, u32[]{:S(2)}) collective-permute-start(bf16[12,12,2048]{2,0,1:T(8,128)(2,1)} %get-tuple-element.14), channel_id=1, source_target_pairs={{0,64},{32,96},{64,128},{96,160},{128,192},{160,224},{1,65},{33,97... | collective-permute-start | bytes 1769480 | tf_op jit(solution)/shard_map/ppermute | solution.py:12
  21.8 4.8 %collective-permute-start = (bf16[4,12,2048]{2,0,1:T(4,128)(2,1)S(1)}, bf16[4,12,2048]{2,0,1:T(4,128)(2,1)S(1)}, u32[]{:S(2)}, u32[]{:S(2)}) collective-permute-start(bf16[4,12,2048]{2,0,1:T(4,128)(2,1)S(1)} %get-tuple-element.12), channel_id=1, source_target_pairs={{0,96},{32,128},{64,160},{96,192},{128,224},{1,97},{33,129},{65,16... | collective-permute-start | bytes 589832 | tf_op jit(solution)/shard_map/ppermute | solution.py:12
  31.3 2.3 fusion.33
  38.6 2.4 pad_maximum_fusion
  43.5 2.5 collective-permute-done.7
  46.5 5.2 %collective-permute-done.6 = bf16[12,12,2048]{2,0,1:T(8,128)(2,1)} collective-permute-done((bf16[12,12,2048]{2,0,1:T(8,128)(2,1)}, bf16[12,12,2048]{2,0,1:T(8,128)(2,1)}, u32[]{:S(2)}, u32[]{:S(2)}) %collective-permute-start.6) | collective-permute-done | bytes 589856 | tf_op jit(solution)/shard_map/ppermute | solution.py:12
  54.4 2.6 copy.40
  59.5 2.8 fusion.44
  64.5 4.3 %collective-permute-start.9 = (bf16[16,12,2048]{2,0,1:T(8,128)(2,1)}, bf16[16,12,2048]{2,0,1:T(8,128)(2,1)}, u32[]{:S(2)}, u32[]{:S(2)}) collective-permute-start(bf16[16,12,2048]{2,0,1:T(8,128)(2,1)} %pad_maximum_fusion.1), channel_id=1, source_target_pairs={{3,0},{4,1},{5,2},{6,3},{7,4},{8,5},{9,6},{10,7},{11,8},{12,9},{13... | collective-permute-start | bytes 2359304 | tf_op jit(solution)/shard_map/ppermute | solution.py:18
  71.4 2.6 copy.38
  75.3 2.5 fusion.37
  77.9 2.6 copy.36
  82.6 2.6 copy.34
  86.5 14.1 %collective-permute-done.8 = bf16[16,12,2048]{2,0,1:T(8,128)(2,1)} collective-permute-done((bf16[16,12,2048]{2,0,1:T(8,128)(2,1)}, bf16[16,12,2048]{2,0,1:T(8,128)(2,1)}, u32[]{:S(2)}, u32[]{:S(2)}) %collective-permute-start.8) | collective-permute-done | bytes 786464 | tf_op jit(solution)/shard_map/ppermute | solution.py:18
  100.6 2.6 copy.39
  105.3 2.5 fusion.41
  107.9 2.5 fusion.27
  110.4 2.6 copy.41
  144.0 7.5 %collective-permute-start.16 = (bf16[4,12,256]{2,1,0:T(8,128)(2,1)S(1)}, bf16[4,12,256]{2,1,0:T(8,128)(2,1)S(1)}, u32[]{:S(2)}, u32[]{:S(2)}) collective-permute-start(bf16[4,12,256]{2,1,0:T(8,128)(2,1)S(1)} %slice.100), channel_id=1, source_target_pairs={{0,96},{32,128},{64,160},{96,192},{128,224},{1,97},{33,129},{65,16... | collective-permute-start | bytes 73736 | tf_op jit(solution)/shard_map/ppermute | solution.py:12
  152.0 2.9 fusion.31
  162.9 4.5 %collective-permute-start.17 = (bf16[12,12,256]{2,1,0:T(8,128)(2,1)}, bf16[12,12,256]{2,1,0:T(8,128)(2,1)S(1)}, u32[]{:S(2)}, u32[]{:S(2)}) collective-permute-start(bf16[12,12,256]{2,1,0:T(8,128)(2,1)} %slice.102), channel_id=1, source_target_pairs={{0,64},{32,96},{64,128},{96,160},{128,192},{160,224},{1,65},{33,97... | collective-permute-start | bytes 221192 | tf_op jit(solution)/shard_map/ppermute | solution.py:12
  169.3 2.7 collective-permute-start.12
  172.0 3.2 collective-permute-start.19
  175.1 2.9 fusion.21
  179.9 2.9 fusion.35
  188.6 2.9 fusion.18
  193.2 3.1 fusion.6
  196.3 108.5 %reduce-scatter.2.cloned.1.call-done = f32[656,256]{1,0:T(8,128)} async-done(((f32[20992,256]{1,0:T(8,128)}), f32[656,256]{1,0:T(8,128)}) %reduce-scatter.2.cloned.1.call-update) | async-done | bytes 671760 | tf_op jit(solution)/shard_map/reduce_scatter | solution.py:162
  306.6 2.8 fusion.10
  311.0 90.2 %all-reduce.2.cloned.1.call-done = f32[656,256]{1,0:T(8,128)} async-done(((f32[656,256]{1,0:T(8,128)}), f32[656,256]{1,0:T(8,128)}) %all-reduce.2.cloned.1.call-update) | async-done | bytes 671760 | tf_op jit(solution)/shard_map/psum | solution.py:163
  (140 shorter events, 88.0 us)
Async XLA Ops:
  7.2 26.4 %copy-start = (bf16[2048,256]{1,0:T(8,128)(2,1)S(1)}, bf16[2048,256]{1,0:T(8,128)(2,1)}, u32[]{:S(2)}) copy-start(bf16[2048,256]{1,0:T(8,128)(2,1)} %param.9) | copy-start | bytes 3145732
  7.2 26.8 %copy-start.17 = (s32[16,12]{1,0:T(8,128)S(1)}, s32[16,12]{1,0:T(8,128)}, u32[]{:S(2)}) copy-start(s32[16,12]{1,0:T(8,128)} %param.12) | copy-start | bytes 2308
  7.2 26.8 %copy-start.18 = (f32[3]{0:T(128)S(1)}, f32[3]{0:T(128)}, u32[]{:S(2)}) copy-start(f32[3]{0:T(128)} %param.13) | copy-start | bytes 40
  7.2 297.7 %reduce-scatter.2.cloned.1.call-start = ((), (), s32[]{:S(2)}) async-start(), calls=%async_computation.1 | async-start | bytes 22167552 | tf_op jit(solution)/shard_map/reduce_scatter | solution.py:162
  7.2 57.3 %collective-permute-start.4 = (bf16[16,12,2048]{2,0,1:T(8,128)(2,1)}, bf16[16,12,2048]{2,0,1:T(8,128)(2,1)}, u32[]{:S(2)}, u32[]{:S(2)}) collective-permute-start(bf16[16,12,2048]{2,0,1:T(8,128)(2,1)} %param.7), channel_id=1, source_target_pairs={{29,0},{30,1},{31,2},{0,3},{1,4},{2,5},{3,6},{4,7},{5,8},{6,9},{7,... | collective-permute-start | bytes 2359304 | tf_op jit(solution)/shard_map/ppermute | solution.py:18
  8.7 62.8 %collective-permute-start.5 = (bf16[16,12,2048]{2,0,1:T(8,128)(2,1)}, bf16[16,12,2048]{2,0,1:T(8,128)(2,1)}, u32[]{:S(2)}, u32[]{:S(2)}) collective-permute-start(bf16[16,12,2048]{2,0,1:T(8,128)(2,1)} %param.7), channel_id=1, source_target_pairs={{3,0},{4,1},{5,2},{6,3},{7,4},{8,5},{9,6},{10,7},{11,8},{12,9},{13... | collective-permute-start | bytes 2359304 | tf_op jit(solution)/shard_map/ppermute | solution.py:18
  16.1 22.5 %collective-permute-start.1 = (bf16[12,12,2048]{2,0,1:T(8,128)(2,1)}, bf16[12,12,2048]{2,0,1:T(8,128)(2,1)}, u32[]{:S(2)}, u32[]{:S(2)}) collective-permute-start(bf16[12,12,2048]{2,0,1:T(8,128)(2,1)} %get-tuple-element.14), channel_id=1, source_target_pairs={{0,64},{32,96},{64,128},{96,160},{128,192},{160,224},{1,65},{33,97... | collective-permute-start | bytes 1769480 | tf_op jit(solution)/shard_map/ppermute | solution.py:12
  21.8 14.2 %collective-permute-start = (bf16[4,12,2048]{2,0,1:T(4,128)(2,1)S(1)}, bf16[4,12,2048]{2,0,1:T(4,128)(2,1)S(1)}, u32[]{:S(2)}, u32[]{:S(2)}) collective-permute-start(bf16[4,12,2048]{2,0,1:T(4,128)(2,1)S(1)} %get-tuple-element.12), channel_id=1, source_target_pairs={{0,96},{32,128},{64,160},{96,192},{128,224},{1,97},{33,129},{65,16... | collective-permute-start | bytes 589832 | tf_op jit(solution)/shard_map/ppermute | solution.py:12
  26.6 25.2 %collective-permute-start.6 = (bf16[12,12,2048]{2,0,1:T(8,128)(2,1)}, bf16[12,12,2048]{2,0,1:T(8,128)(2,1)}, u32[]{:S(2)}, u32[]{:S(2)}) collective-permute-start(bf16[12,12,2048]{2,0,1:T(8,128)(2,1)} %get-tuple-element.15), channel_id=1, source_target_pairs={{64,0},{96,32},{128,64},{160,96},{192,128},{224,160},{65,1},{97,33... | collective-permute-start | bytes 1769480 | tf_op jit(solution)/shard_map/ppermute | solution.py:12
  36.0 10.1 %collective-permute-start.7 = (bf16[4,12,2048]{2,0,1:T(4,128)(2,1)S(1)}, bf16[4,12,2048]{2,0,1:T(4,128)(2,1)S(1)}, u32[]{:S(2)}, u32[]{:S(2)}) collective-permute-start(bf16[4,12,2048]{2,0,1:T(4,128)(2,1)S(1)} %get-tuple-element.13), channel_id=1, source_target_pairs={{96,0},{128,32},{160,64},{192,96},{224,128},{97,1},{129,33},{161,6... | collective-permute-start | bytes 589832 | tf_op jit(solution)/shard_map/ppermute | solution.py:12
  40.9 36.9 %collective-permute-start.3 = (bf16[16,12,2048]{2,0,1:T(8,128)(2,1)}, bf16[16,12,2048]{2,0,1:T(8,128)(2,1)}, u32[]{:S(2)}, u32[]{:S(2)}) collective-permute-start(bf16[16,12,2048]{2,0,1:T(8,128)(2,1)} %pad_maximum_fusion), channel_id=1, source_target_pairs={{3,0},{4,1},{5,2},{6,3},{7,4},{8,5},{9,6},{10,7},{11,8},{12,9},{13... | collective-permute-start | bytes 2359304 | tf_op jit(solution)/shard_map/ppermute | solution.py:18
  46.0 36.6 %collective-permute-start.2 = (bf16[16,12,2048]{2,0,1:T(8,128)(2,1)}, bf16[16,12,2048]{2,0,1:T(8,128)(2,1)}, u32[]{:S(2)}, u32[]{:S(2)}) collective-permute-start(bf16[16,12,2048]{2,0,1:T(8,128)(2,1)} %pad_maximum_fusion), channel_id=1, source_target_pairs={{29,0},{30,1},{31,2},{0,3},{1,4},{2,5},{3,6},{4,7},{5,8},{6,9},{7,... | collective-permute-start | bytes 2359304 | tf_op jit(solution)/shard_map/ppermute | solution.py:18
  54.0 46.7 %collective-permute-start.8 = (bf16[16,12,2048]{2,0,1:T(8,128)(2,1)}, bf16[16,12,2048]{2,0,1:T(8,128)(2,1)}, u32[]{:S(2)}, u32[]{:S(2)}) collective-permute-start(bf16[16,12,2048]{2,0,1:T(8,128)(2,1)} %pad_maximum_fusion.1), channel_id=1, source_target_pairs={{29,0},{30,1},{31,2},{0,3},{1,4},{2,5},{3,6},{4,7},{5,8},{6,9},{7,... | collective-permute-start | bytes 2359304 | tf_op jit(solution)/shard_map/ppermute | solution.py:18
  64.5 45.9 %collective-permute-start.9 = (bf16[16,12,2048]{2,0,1:T(8,128)(2,1)}, bf16[16,12,2048]{2,0,1:T(8,128)(2,1)}, u32[]{:S(2)}, u32[]{:S(2)}) collective-permute-start(bf16[16,12,2048]{2,0,1:T(8,128)(2,1)} %pad_maximum_fusion.1), channel_id=1, source_target_pairs={{3,0},{4,1},{5,2},{6,3},{7,4},{8,5},{9,6},{10,7},{11,8},{12,9},{13... | collective-permute-start | bytes 2359304 | tf_op jit(solution)/shard_map/ppermute | solution.py:18
  115.1 11.8 %copy-start.8 = (bf16[192,2048]{1,0:T(8,128)(2,1)S(1)}, bf16[192,2048]{1,0:T(8,128)(2,1)}, u32[]{:S(2)}) copy-start(bf16[192,2048]{1,0:T(8,128)(2,1)} %reshape.80) | copy-start | bytes 2359300
  117.1 11.7 %copy-start.7 = (bf16[192,2048]{1,0:T(8,128)(2,1)S(1)}, bf16[192,2048]{1,0:T(8,128)(2,1)}, u32[]{:S(2)}) copy-start(bf16[192,2048]{1,0:T(8,128)(2,1)} %reshape.81) | copy-start | bytes 2359300
  123.0 11.6 %copy-start.9 = (bf16[192,2048]{1,0:T(8,128)(2,1)S(1)}, bf16[192,2048]{1,0:T(8,128)(2,1)}, u32[]{:S(2)}) copy-start(bf16[192,2048]{1,0:T(8,128)(2,1)} %reshape.83) | copy-start | bytes 2359300
  123.2 18.8 %copy-start.11 = (bf16[192,256]{1,0:T(8,128)(2,1)}, bf16[192,256]{1,0:T(8,128)(2,1)S(1)}, u32[]{:S(2)}) copy-start(bf16[192,256]{1,0:T(8,128)(2,1)S(1)} %fusion.16) | copy-start | bytes 294916
  125.1 11.3 %copy-start.5 = (bf16[192,2048]{1,0:T(8,128)(2,1)S(1)}, bf16[192,2048]{1,0:T(8,128)(2,1)}, u32[]{:S(2)}) copy-start(bf16[192,2048]{1,0:T(8,128)(2,1)} %copy-done.4) | copy-start | bytes 2359300
  143.9 17.7 %copy-start.15 = (bf16[192,256]{1,0:T(8,128)(2,1)S(1)}, bf16[192,256]{1,0:T(8,128)(2,1)}, u32[]{:S(2)}) copy-start(bf16[192,256]{1,0:T(8,128)(2,1)} %get-tuple-element.17) | copy-start | bytes 294916
  143.9 257.2 %all-reduce.2.cloned.1.call-start = ((), (), s32[]{:S(2)}) async-start(), calls=%async_computation.2 | async-start | bytes 1343488 | tf_op jit(solution)/shard_map/psum | solution.py:163
  144.0 18.3 %collective-permute-start.16 = (bf16[4,12,256]{2,1,0:T(8,128)(2,1)S(1)}, bf16[4,12,256]{2,1,0:T(8,128)(2,1)S(1)}, u32[]{:S(2)}, u32[]{:S(2)}) collective-permute-start(bf16[4,12,256]{2,1,0:T(8,128)(2,1)S(1)} %slice.100), channel_id=1, source_target_pairs={{0,96},{32,128},{64,160},{96,192},{128,224},{1,97},{33,129},{65,16... | collective-permute-start | bytes 73736 | tf_op jit(solution)/shard_map/ppermute | solution.py:12
  155.0 23.1 %collective-permute-start.14 = (bf16[16,12,256]{2,1,0:T(8,128)(2,1)S(1)}, bf16[16,12,256]{2,1,0:T(8,128)(2,1)S(1)}, u32[]{:S(2)}, u32[]{:S(2)}) collective-permute-start(bf16[16,12,256]{2,1,0:T(8,128)(2,1)S(1)} %reshape.90), channel_id=1, source_target_pairs={{3,0},{4,1},{5,2},{6,3},{7,4},{8,5},{9,6},{10,7},{11,8},{12,9},{13... | collective-permute-start | bytes 294920 | tf_op jit(solution)/shard_map/ppermute | solution.py:18
  155.3 27.5 %collective-permute-start.15 = (bf16[16,12,256]{2,1,0:T(8,128)(2,1)S(1)}, bf16[16,12,256]{2,1,0:T(8,128)(2,1)S(1)}, u32[]{:S(2)}, u32[]{:S(2)}) collective-permute-start(bf16[16,12,256]{2,1,0:T(8,128)(2,1)S(1)} %reshape.90), channel_id=1, source_target_pairs={{29,0},{30,1},{31,2},{0,3},{1,4},{2,5},{3,6},{4,7},{5,8},{6,9},{7,... | collective-permute-start | bytes 294920 | tf_op jit(solution)/shard_map/ppermute | solution.py:18
  157.7 10.5 %collective-permute-start.10 = (bf16[12,12,256]{2,1,0:T(8,128)(2,1)}, bf16[12,12,256]{2,1,0:T(8,128)(2,1)S(1)}, u32[]{:S(2)}, u32[]{:S(2)}) collective-permute-start(bf16[12,12,256]{2,1,0:T(8,128)(2,1)} %slice.96), channel_id=1, source_target_pairs={{64,0},{96,32},{128,64},{160,96},{192,128},{224,160},{65,1},{97,33... | collective-permute-start | bytes 221192 | tf_op jit(solution)/shard_map/ppermute | solution.py:12
  159.6 8.9 %collective-permute-start.11 = (bf16[4,12,256]{2,1,0:T(8,128)(2,1)}, bf16[4,12,256]{2,1,0:T(8,128)(2,1)}, u32[]{:S(2)}, u32[]{:S(2)}) collective-permute-start(bf16[4,12,256]{2,1,0:T(8,128)(2,1)} %slice.98), channel_id=1, source_target_pairs={{96,0},{128,32},{160,64},{192,96},{224,128},{97,1},{129,33},{161,6... | collective-permute-start | bytes 73736 | tf_op jit(solution)/shard_map/ppermute | solution.py:12
  162.9 9.1 %collective-permute-start.17 = (bf16[12,12,256]{2,1,0:T(8,128)(2,1)}, bf16[12,12,256]{2,1,0:T(8,128)(2,1)S(1)}, u32[]{:S(2)}, u32[]{:S(2)}) collective-permute-start(bf16[12,12,256]{2,1,0:T(8,128)(2,1)} %slice.102), channel_id=1, source_target_pairs={{0,64},{32,96},{64,128},{96,160},{128,192},{160,224},{1,65},{33,97... | collective-permute-start | bytes 221192 | tf_op jit(solution)/shard_map/ppermute | solution.py:12
  169.3 13.6 %collective-permute-start.12 = (bf16[16,12,256]{2,1,0:T(8,128)(2,1)S(1)}, bf16[16,12,256]{2,1,0:T(8,128)(2,1)}, u32[]{:S(2)}, u32[]{:S(2)}) collective-permute-start(bf16[16,12,256]{2,1,0:T(8,128)(2,1)S(1)} %constant_dynamic-update-slice_fusion), channel_id=1, source_target_pairs={{3,0},{4,1},{5,2},{6,3},{7,4},{8,5},{9,6},{10,7},{11,8},{12,9},{13... | collective-permute-start | bytes 294920 | tf_op jit(solution)/shard_map/ppermute | solution.py:18
  171.9 11.9 %collective-permute-start.13 = (bf16[16,12,256]{2,1,0:T(8,128)(2,1)S(1)}, bf16[16,12,256]{2,1,0:T(8,128)(2,1)}, u32[]{:S(2)}, u32[]{:S(2)}) collective-permute-start(bf16[16,12,256]{2,1,0:T(8,128)(2,1)S(1)} %constant_dynamic-update-slice_fusion), channel_id=1, source_target_pairs={{29,0},{30,1},{31,2},{0,3},{1,4},{2,5},{3,6},{4,7},{5,8},{6,9},{7,... | collective-permute-start | bytes 294920 | tf_op jit(solution)/shard_map/ppermute | solution.py:18
  172.0 12.8 %collective-permute-start.19 = (bf16[16,12,256]{2,1,0:T(8,128)(2,1)S(1)}, bf16[16,12,256]{2,1,0:T(8,128)(2,1)}, u32[]{:S(2)}, u32[]{:S(2)}) collective-permute-start(bf16[16,12,256]{2,1,0:T(8,128)(2,1)S(1)} %constant_dynamic-update-slice_fusion.2), channel_id=1, source_target_pairs={{29,0},{30,1},{31,2},{0,3},{1,4},{2,5},{3,6},{4,7},{5,8},{6,9},{7,... | collective-permute-start | bytes 294920 | tf_op jit(solution)/shard_map/ppermute | solution.py:18
  178.1 7.6 %collective-permute-start.18 = (bf16[16,12,256]{2,1,0:T(8,128)(2,1)S(1)}, bf16[16,12,256]{2,1,0:T(8,128)(2,1)}, u32[]{:S(2)}, u32[]{:S(2)}) collective-permute-start(bf16[16,12,256]{2,1,0:T(8,128)(2,1)S(1)} %constant_dynamic-update-slice_fusion.2), channel_id=1, source_target_pairs={{3,0},{4,1},{5,2},{6,3},{7,4},{8,5},{9,6},{10,7},{11,8},{12,9},{13... | collective-permute-start | bytes 294920 | tf_op jit(solution)/shard_map/ppermute | solution.py:18
  193.2 113.4 %copy-start.3 = (f32[192,2048]{1,0:T(8,128)S(1)}, f32[192,2048]{1,0:T(8,128)}, u32[]{:S(2)}) copy-start(f32[192,2048]{1,0:T(8,128)} %fusion.18) | copy-start | bytes 4718596
  (10 other events, 70.2 us)
Sparse Core Ops, SparseCore 0:
  144.0 160.8 reduce-scatter.1
  307.7 93.3 all-reduce.1
where the time goes:
time: 412 us; the launch traced here: 410 us
  waiting for transfers between devices  222 us (54%)
  matrix products  69.3 us (17%)
  local copies, waits for them, and re-layouts  51.1 us (12%)
  starting transfers between devices  48.2 us (12%)
  between operations  14.5 us (4%)
  other arithmetic  4.65 us (1%)
    reduce_scatter x1, waiting for transfers between devices, shards(): lax.psum_scatter(local_terms, 'lon', scatter_dimension=0, tiled=True)  109 us
    psum x1, waiting for transfers between devices, shards(): weight_grads = lax.psum(longitude_sum, 'lat')  90.2 us
    ppermute x8, starting transfers between devices, shifted(): return lax.ppermute(value, axis, pairs)  26.3 us
    dot_general x12, matrix products, multiply_transposed(): lax.dot_general(left, right, (((1,), (1,)), ((), ())), preferred_element_...  23.9 us
    ppermute x12, starting transfers between devices, shifted_2(): return lax.ppermute(block, axis, route)  21.8 us
    dot_general x12, matrix products, contract_row_axes(): lax.dot_general(left, right, (((0,), (0,)), ((), ())), preferred_element_...  20.6 us
    dot_general x9, matrix products, shards(): jnp.dot(feature_tap_list[kernel_tap_index], atrous_kernel_weight[kernel_t...  20.6 us
    reshape x16, local copies, waits for them, and re-layouts, neighbour_window(): shifted_taps[upward_direction, across_axis].reshape(-1, last_width)  16.2 us
  transfers between devices with their start and end apart: 22, of which 7 were waited for; matrix products, arithmetic and copies ran while one was open for 22% of the time, Pallas kernels for 0%

commit v1 on v0

v1 whole, which is shorter than its diff:
```python
import functools

import jax
import jax.numpy as jnp
from jax import lax
from jax.experimental import pallas as pl
from jax.experimental.pallas import tpu as pltpu
from jax.sharding import Mesh, PartitionSpec as P

ATROUS_DILATION = 36
LAT = ("y", "xh")
LON = ("xl", "z", "c")
AXIS_SIZES = {"y": 4, "xh": 2, "xl": 2, "z": 8, "c": 2}
LAT_COUNT = 8
LON_COUNT = 32
VMEM = pl.BlockSpec(memory_space=pltpu.VMEM)
SMEM = pl.BlockSpec(memory_space=pltpu.SMEM)
ANY = pl.BlockSpec(memory_space=pl.ANY)


def shift_rows(value, by):
    pairs = [(i, i + by) for i in range(LAT_COUNT) if 0 <= i + by < LAT_COUNT]
    return lax.ppermute(value, LAT, pairs)


def shift_columns(value, by):
    return lax.ppermute(value, LON, [(i, (i + by) % LON_COUNT) for i in range(LON_COUNT)])


def contract_row_axes(left, right):
    return lax.dot_general(
        left, right, (((0,), (0,)), ((), ())), preferred_element_type=jnp.float32
    )


def multiply_transposed(left, right):
    return lax.dot_general(
        left, right, (((1,), (1,)), ((), ())), preferred_element_type=jnp.float32
    )


def multiply(left, right):
    return jnp.dot(left, right, preferred_element_type=jnp.float32)


def sigmoid(value):
    return 1.0 / (1.0 + jnp.exp(-value))


def params(megabytes=24):
    return pltpu.CompilerParams(vmem_limit_bytes=megabytes * 2**20)


def cost(flops, moved):
    return pl.CostEstimate(flops=int(flops), bytes_accessed=int(moved), transcendentals=0)


def like(shape, dtype):
    return jax.ShapeDtypeStruct(shape, dtype)


def stream(sources, buffer_ref, semaphores):
    depth = buffer_ref.shape[0]

    def copy(at):
        return pltpu.make_async_copy(
            sources[at], buffer_ref.at[at % depth], semaphores.at[at % depth]
        )

    for at in range(min(depth - 1, len(sources))):
        copy(at).start()
    for at in range(len(sources)):
        if at + depth - 1 < len(sources):
            copy(at + depth - 1).start()
        copy(at).wait()
        yield buffer_ref.at[at % depth]


STREAM_DEPTH = 3


def stream_scratch(in_width, width):
    return [
        pltpu.VMEM((STREAM_DEPTH, in_width, width), jnp.bfloat16),
        pltpu.SemaphoreType.DMA((STREAM_DEPTH,)),
    ]


def outer_taps_kernel(
    flat_ref,
    kernel_ref,
    below_near_ref,
    below_far_ref,
    above_near_ref,
    above_far_ref,
    buffer_ref,
    semaphores,
):
    width = buffer_ref.shape[2]
    pixels = flat_ref.shape[0]
    far = below_far_ref.shape[0]
    sources = [kernel_ref.at[tap] for tap in (6, 7, 8, 0, 1, 2)]
    for at, tap_ref in enumerate(stream(sources, buffer_ref, semaphores)):
        product = multiply(flat_ref[...], tap_ref[...]).astype(jnp.bfloat16)
        lanes = slice((at % 3) * width, (at % 3 + 1) * width)
        if at < 3:
            below_far_ref[:, lanes] = product[:far]
            below_near_ref[:, lanes] = product[far:]
        else:
            above_near_ref[:, lanes] = product[: pixels - far]
            above_far_ref[:, lanes] = product[pixels - far :]


def outer_taps(flat, kernel, far):
    pixels, in_width = flat.shape
    width = kernel.shape[2]
    near_shape = like((pixels - far, 3 * width), jnp.bfloat16)
    far_shape = like((far, 3 * width), jnp.bfloat16)
    return pl.pallas_call(
        outer_taps_kernel,
        out_shape=(near_shape, far_shape, near_shape, far_shape),
        in_specs=[VMEM, ANY],
        out_specs=(VMEM,) * 4,
        scratch_shapes=stream_scratch(in_width, width),
        compiler_params=params(60),
        cost_estimate=cost(12 * pixels * in_width * width, 12 * in_width * width),
    )(flat, kernel)


def inner_taps_kernel(
    flat_ref, kernel_ref, point_weight_ref, level_ref, point_ref, buffer_ref, semaphores
):
    width = point_ref.shape[1]
    sources = [kernel_ref.at[tap] for tap in (3, 4, 5)] + [point_weight_ref]
    for at, tap_ref in enumerate(stream(sources, buffer_ref, semaphores)):
        product = multiply(flat_ref[...], tap_ref[...])
        if at < 3:
            level_ref[:, at * width : (at + 1) * width] = product
        else:
            point_ref[...] = product


def inner_taps(flat, kernel, point_weight):
    pixels, in_width = flat.shape
    width = kernel.shape[2]
    return pl.pallas_call(
        inner_taps_kernel,
        out_shape=(
            like((pixels, 3 * width), jnp.float32),
            like((pixels, width), jnp.float32),
        ),
        in_specs=[VMEM, ANY, ANY],
        out_specs=(VMEM,) * 2,
        scratch_shapes=stream_scratch(in_width, width),
        compiler_params=params(60),
        cost_estimate=cost(8 * pixels * in_width * width, 8 * in_width * width),
    )(flat, kernel, point_weight)


def slices_kernel(flat_ref, after_ref, slices_ref):
    count, _, size = slices_ref.shape
    part = size // count
    source = lax.broadcasted_iota(jnp.int32, (size, size), 0)
    target = lax.broadcasted_iota(jnp.int32, (size, size), 1)
    wanted = (source % count) * part + source // count
    picker = jnp.where(target == wanted, 1.0, 0.0).astype(jnp.bfloat16)
    sorted_blocks = [
        multiply(flat_ref[:, size * b : size * (b + 1)], picker).astype(jnp.bfloat16)
        for b in range(count)
    ]
    for a in range(count):
        slices_ref[a] = jnp.concatenate(
            [block[:, part * a : part * (a + 1)] for block in sorted_blocks], axis=1
        )


def channel_slices(flat, after):
    pixels, in_width = flat.shape
    return pl.pallas_call(
        slices_kernel,
        out_shape=like((LAT_COUNT, pixels, in_width // LAT_COUNT), jnp.bfloat16),
        in_specs=[VMEM, ANY],
        out_specs=VMEM,
        compiler_params=params(),
        cost_estimate=cost(2 * pixels * in_width * in_width // LAT_COUNT, 4 * pixels * in_width),
    )(flat, after)


def row_sum_kernel(
    level_ref,
    below_near_ref,
    below_far_ref,
    above_near_ref,
    above_far_ref,
    west_ref,
    east_ref,
    center_ref,
):
    width = center_ref.shape[1]
    near, far = below_near_ref.shape[0], below_far_ref.shape[0]
    f32 = jnp.float32
    below = jnp.concatenate([below_near_ref[...].astype(f32), below_far_ref[...].astype(f32)])
    above = jnp.concatenate([above_far_ref[...].astype(f32), above_near_ref[...].astype(f32)])
    total = level_ref[...] + below + above
    west_ref[...] = total[:, :width].astype(jnp.bfloat16)
    center_ref[...] = total[:, width : 2 * width]
    east_ref[...] = total[:, 2 * width :].astype(jnp.bfloat16)


def row_sum(level, received):
    pixels, wide = level.shape
    side = like((pixels, wide // 3), jnp.bfloat16)
    return pl.pallas_call(
        row_sum_kernel,
        out_shape=(side, side, like((pixels, wide // 3), jnp.float32)),
        in_specs=[VMEM] * 5,
        out_specs=(VMEM,) * 3,
        compiler_params=params(),
        cost_estimate=cost(3 * pixels * wide, 8 * pixels * wide),
    )(level, *received)


def head_kernel(
    point_ref,
    center_ref,
    from_east_ref,
    from_west_ref,
    project_ref,
    upstream_ref,
    pixel_weight_ref,
    after_ref,
    head_ref,
    point_grad_ref,
    atrous_grad_ref,
    message_ref,
    *terms_refs,
):
    bf16, f32 = jnp.bfloat16, jnp.float32
    count = message_ref.shape[0]
    pixels, width = point_ref.shape
    pre_list = [
        point_ref[...],
        center_ref[...] + from_east_ref[...].astype(f32) + from_west_ref[...].astype(f32),
    ]
    gates = [sigmoid(pre) for pre in pre_list]
    acts = [(pre * gate).astype(bf16) for pre, gate in zip(pre_list, gates)]
    mixed = multiply(acts[0], project_ref[0]) + multiply(acts[1], project_ref[1])
    gate = sigmoid(mixed)
    head_ref[...] = (mixed * gate).astype(bf16)
    slope = gate * (1.0 + mixed * (1.0 - gate))
    out_grad = (upstream_ref[...].astype(f32) * pixel_weight_ref[...] * slope).astype(bf16)
    grads = [
        (
            multiply_transposed(out_grad, project_ref[k])
            * (gates[k] * (1.0 + pre_list[k] * (1.0 - gates[k])))
        ).astype(bf16)
        for k in range(2)
    ]
    point_grad_ref[...] = grads[0]
    atrous_grad_ref[...] = grads[1]
    for k in range(2):
        terms = contract_row_axes(acts[k], out_grad)
        for half, terms_ref in enumerate(terms_refs):
            terms_ref[width * k : width * (k + 1), :] = terms[:, 128 * half : 128 * half + 128]
    part = 2 * width // count
    for a in range(count):
        message_ref[a, :pixels, :] = grads[1]
        message_ref[a, pixels : 2 * pixels, :] = grads[0]
        for half, terms_ref in enumerate(terms_refs):
            message_ref[a, 2 * pixels :, 128 * half : 128 * half + 128] = terms_ref[
                pl.ds(a, part, stride=count), :
            ].astype(bf16)


def head(point_pre, center, from_east, from_west, project_weight, upstream, pixel_weight, after):
    pixels, width = point_pre.shape
    field = like((pixels, width), jnp.bfloat16)
    part = 2 * width // LAT_COUNT
    return pl.pallas_call(
        head_kernel,
        out_shape=(
            field,
            field,
            field,
            like((LAT_COUNT, 2 * pixels + part, width), jnp.bfloat16),
        ),
        in_specs=[VMEM] * 7 + [ANY],
        out_specs=(VMEM,) * 4,
        scratch_shapes=[pltpu.VMEM((2 * width, 128), jnp.float32)] * (width // 128),
        compiler_params=params(),
        cost_estimate=cost(12 * pixels * width * width, 24 * pixels * width),
    )(point_pre, center, from_east, from_west, project_weight, upstream, pixel_weight, after)


def weight_terms_kernel(
    span,
    chunk,
    core_ref,
    center_ref,
    east_ref,
    west_ref,
    message_ref,
    after_east_ref,
    after_west_ref,
    kept_ref,
    sent_ref,
):
    total, width = center_ref.shape
    bands = message_ref.shape[0]
    pixels = total // bands
    room = padded(chunk)
    core = core_ref[0]
    columns = {0: center_ref, 1: east_ref, -1: west_ref}
    atrous_grad = message_ref[:, :pixels, :].reshape(total, width)
    point_grad = message_ref[:, pixels : 2 * pixels, :].reshape(total, width)

    def store(first, value):
        count = value.shape[0]
        pieces = []
        at = 0
        while at < count:
            index, offset = divmod(first + at, chunk)
            size = min(chunk - offset, count - at)
            pieces.append((index, offset, at, size))
            at += size
        for owner in (0, 1):

            @pl.when(core == owner)
            def _():
                for index, offset, at, size in pieces:
                    target = kept_ref if index % 2 == owner else sent_ref
                    first_row = index // 2 * room + offset
                    target[first_row : first_row + size, :] = value[at : at + size]

    edge = jnp.zeros((span, width), atrous_grad.dtype)
    framed = jnp.concatenate([edge, atrous_grad, edge])
    for j in (0, 1, -1):
        right = [framed[span - span * i : span - span * i + total] for i in (-1, 0, 1)]
        if j == 0:
            right.append(point_grad)
        product = contract_row_axes(columns[j][...], jnp.concatenate(right, axis=1))
        for i in (-1, 0, 1):
            store((3 * (i + 1) + j + 1) * width, product[:, (i + 1) * width : (i + 2) * width])
        if j == 0:
            project_rows = jnp.sum(message_ref[:, 2 * pixels :, :].astype(jnp.float32), axis=0)
            store(9 * width, project_rows)
            store(9 * width + project_rows.shape[0], product[:, 3 * width :])


def padded(chunk):
    return (chunk + 7) // 8 * 8


def weight_terms(span, core, center, east, west, message, after):
    total, width = center.shape
    project_rows = message.shape[1] - 2 * total // LAT_COUNT
    chunk = (10 * width + project_rows) // LON_COUNT
    out = like((LON_COUNT // 2 * padded(chunk), width), jnp.float32)
    return pl.pallas_call(
        functools.partial(weight_terms_kernel, span, chunk),
        out_shape=(out, out),
        in_specs=[SMEM] + [VMEM] * 4 + [ANY] * 2,
        out_specs=(VMEM,) * 2,
        compiler_params=params(),
        cost_estimate=cost(20 * total * width * width, 8 * 2**20),
    )(core.reshape(1), center, east, west, message, *after)


def pair_sum_kernel(kept_ref, received_ref, out_ref):
    count, chunk, _ = out_ref.shape
    room = kept_ref.shape[0] // count
    for at in range(count):
        rows = slice(room * at, room * at + chunk)
        out_ref[at] = (kept_ref[rows, :] + received_ref[rows, :]).astype(jnp.bfloat16)


def pair_sum(kept, received, chunk):
    return pl.pallas_call(
        pair_sum_kernel,
        out_shape=like((LON_COUNT // 2, chunk, kept.shape[1]), jnp.bfloat16),
        in_specs=[VMEM] * 2,
        out_specs=VMEM,
        compiler_params=params(),
        cost_estimate=cost(kept.size, 10 * kept.size),
    )(kept, received)


def piece_sum_kernel(pieces_ref, *refs):
    out_ref = refs[-1]
    total = pieces_ref[0].astype(jnp.float32)
    for at in range(1, pieces_ref.shape[0]):
        total = total + pieces_ref[at].astype(jnp.float32)
    for at in range(out_ref.shape[0]):
        out_ref[at] = total


def piece_sum(pieces, after):
    return pl.pallas_call(
        piece_sum_kernel,
        out_shape=like((LAT_COUNT,) + pieces.shape[1:], jnp.float32),
        in_specs=[VMEM] + [ANY] * len(after),
        out_specs=VMEM,
        compiler_params=params(),
        cost_estimate=cost(pieces.size, 4 * pieces.size),
    )(pieces, *after)


def interleave_kernel(parts_ref, out_ref, *sorted_refs):
    count, size, _ = parts_ref.shape
    for half, sorted_ref in enumerate(sorted_refs):
        lanes = slice(128 * half, 128 * half + 128)
        for a in range(count):
            sorted_ref[pl.ds(a, size, stride=count), :] = parts_ref[a, :, lanes]
        out_ref[:, lanes] = sorted_ref[...]


def interleave(parts):
    count, size, width = parts.shape
    return pl.pallas_call(
        interleave_kernel,
        out_shape=like((count * size, width), jnp.float32),
        in_specs=[VMEM],
        out_specs=VMEM,
        scratch_shapes=[pltpu.VMEM((count * size, 128), jnp.float32)] * (width // 128),
        compiler_params=params(),
        cost_estimate=cost(parts.size, 8 * parts.size),
    )(parts)


def center_taps_kernel(
    span,
    lat_ref,
    message_ref,
    point_grad_ref,
    east_ref,
    west_ref,
    kernel_ref,
    point_weight_ref,
    after_ref,
    total_ref,
    up_near_ref,
    up_far_ref,
    down_near_ref,
    down_far_ref,
    sides_ref,
    buffer_ref,
    semaphores,
):
    bands = message_ref.shape[0]
    pixels, width = point_grad_ref.shape
    lat = lat_ref[0]
    near = span // pixels
    far = span - near * pixels

    def part(by, low, high):
        band = lat + by
        inside = jnp.logical_and(band >= 0, band < bands)
        value = message_ref[jnp.clip(band, 0, bands - 1), low:high, :]
        return jnp.where(inside, value, jnp.zeros_like(value))

    arriving = stream(
        [point_weight_ref] + [kernel_ref.at[tap] for tap in (1, 4, 7)], buffer_ref, semaphores
    )
    for at, side_ref in enumerate((east_ref, west_ref)):
        lanes = slice(at * width, (at + 1) * width)
        side = side_ref[...]
        sides_ref[:, lanes] = side
        up_near_ref[:, lanes] = side[far:]
        up_far_ref[:, lanes] = side[:far]
        down_near_ref[:, lanes] = side[: pixels - far]
        down_far_ref[:, lanes] = side[pixels - far :]
    windows = [
        point_grad_ref[...],
        jnp.concatenate([part(near, far, pixels), part(near + 1, 0, far)]),
        message_ref[lat, :pixels, :],
        jnp.concatenate([part(-(near + 1), pixels - far, pixels), part(-near, 0, pixels - far)]),
    ]
    for at, tap_ref in enumerate(arriving):
        add_product(total_ref, windows[at], tap_ref, at == 0)


def add_product(total_ref, window, tap_ref, first):
    size = 512
    for low in range(0, total_ref.shape[1], size):
        lanes = slice(low, low + size)
        product = multiply_transposed(window, tap_ref[low : low + size, :])
        total_ref[:, lanes] = product if first else total_ref[:, lanes] + product


def center_taps(span, lat, message, point_grad, east, west, kernel, point_weight, after):
    pixels, width = point_grad.shape
    in_width = point_weight.shape[0]
    far = span % pixels
    bf16 = jnp.bfloat16
    out_shape = (
        like((pixels, in_width), jnp.float32),
        like((pixels - far, 2 * width), bf16),
        like((far, 2 * width), bf16),
        like((pixels - far, 2 * width), bf16),
        like((far, 2 * width), bf16),
        like((pixels, 2 * width), bf16),
    )
    return pl.pallas_call(
        functools.partial(center_taps_kernel, span),
        out_shape=out_shape,
        in_specs=[SMEM] + [VMEM] * 4 + [ANY] * 3,
        out_specs=(VMEM,) * 6,
        scratch_shapes=stream_scratch(in_width, width),
        compiler_params=params(60),
        cost_estimate=cost(8 * pixels * in_width * width, 12 * in_width * width),
    )(lat.reshape(1), message, point_grad, east, west, kernel, point_weight, after)


def side_taps_kernel(
    total_ref,
    sides_ref,
    up_near_ref,
    up_far_ref,
    down_near_ref,
    down_far_ref,
    kernel_ref,
    out_ref,
    sum_ref,
    buffer_ref,
    semaphores,
):
    width = buffer_ref.shape[2]
    sources = [kernel_ref.at[tap] for tap in (2, 5, 8, 0, 3, 6)]
    sum_ref[...] = total_ref[...]
    for at, tap_ref in enumerate(stream(sources, buffer_ref, semaphores)):
        side, i = divmod(at, 3)
        lanes = slice(side * width, (side + 1) * width)
        if i == 0:
            window = jnp.concatenate([up_near_ref[:, lanes], up_far_ref[:, lanes]])
        elif i == 1:
            window = sides_ref[:, lanes]
        else:
            window = jnp.concatenate([down_far_ref[:, lanes], down_near_ref[:, lanes]])
        add_product(sum_ref, window, tap_ref, False)
    out_ref[...] = sum_ref[...].astype(out_ref.dtype)


def side_taps(total, sides, received, kernel):
    pixels, in_width = total.shape
    return pl.pallas_call(
        side_taps_kernel,
        out_shape=like((pixels, in_width), jnp.bfloat16),
        in_specs=[VMEM] * 6 + [ANY],
        out_specs=VMEM,
        scratch_shapes=[pltpu.VMEM((pixels, in_width), jnp.float32)]
        + stream_scratch(in_width, kernel.shape[2]),
        compiler_params=params(60),
        cost_estimate=cost(12 * pixels * in_width * kernel.shape[2], 16 * in_width * in_width),
    )(total, sides, *received, kernel)


def shards(features, kernel, point_weight, project_weight, upstream, labels, class_weights):
    rows, cols, in_width = features.shape
    width = point_weight.shape[1]
    pixels = rows * cols
    lat_index = lax.axis_index(LAT)
    core = lax.axis_index("c")
    near = ATROUS_DILATION // rows
    far_pixels = (ATROUS_DILATION - near * rows) * cols
    tiles_over = ATROUS_DILATION // cols
    span = ATROUS_DILATION * cols

    flat = features.reshape(pixels, in_width)
    below_near, below_far, above_near, above_far = outer_taps(flat, kernel, far_pixels)
    received = (
        shift_rows(below_near, -near),
        shift_rows(below_far, -(near + 1)),
        shift_rows(above_near, near),
        shift_rows(above_far, near + 1),
    )
    level, point_pre = inner_taps(flat, kernel, point_weight)
    slices = channel_slices(flat, received[1])
    column_features = lax.all_to_all(slices, LAT, 0, 0).reshape(LAT_COUNT * pixels, -1)
    to_east, to_west, center = row_sum(level, received)
    first_east = shift_columns(column_features, -1)
    first_west = shift_columns(column_features, 1)
    from_east = shift_columns(to_west, -tiles_over)
    from_west = shift_columns(to_east, tiles_over)
    class_index = jnp.arange(3, dtype=jnp.int32)
    pixel_weight = jnp.sum(
        jnp.where(labels[..., None] == class_index, class_weights, 0.0), axis=-1
    ).reshape(-1, 1)
    head_out, point_grad, atrous_grad, message = head(
        point_pre,
        center,
        from_east,
        from_west,
        project_weight,
        upstream.reshape(pixels, width),
        pixel_weight,
        column_features,
    )

    gathered = lax.all_to_all(message, LAT, 0, 0)
    east_features = shift_columns(first_east, 1 - tiles_over)
    west_features = shift_columns(first_west, tiles_over - 1)
    east_grad = shift_columns(atrous_grad, tiles_over)
    west_grad = shift_columns(atrous_grad, -tiles_over)

    kept, sent = weight_terms(
        span, core, column_features, east_features, west_features, gathered, (east_grad, west_grad)
    )
    chunk = (10 * in_width + 2 * width) // (LAT_COUNT * LON_COUNT)
    chip_sum = pair_sum(kept, lax.ppermute(sent, "c", [(0, 1), (1, 0)]), chunk)
    pieces = lax.all_to_all(chip_sum, ("xl", "z"), 0, 0)

    total, up_near, up_far, down_near, down_far, sides = center_taps(
        span, lat_index, gathered, point_grad, east_grad, west_grad, kernel, point_weight, chip_sum
    )
    side_rows = (
        shift_rows(up_near, -near),
        shift_rows(up_far, -(near + 1)),
        shift_rows(down_near, near),
        shift_rows(down_far, near + 1),
    )
    weight_grads = interleave(lax.all_to_all(piece_sum(pieces, side_rows), LAT, 0, 0))
    summed_input = side_taps(total, sides, side_rows, kernel)

    head_tile = head_out.reshape(rows, cols, width)
    grad_tile = summed_input.reshape(rows, cols, in_width)
    return (head_tile, grad_tile, weight_grads)


def solution(mesh):
    split = Mesh(mesh.devices.reshape(tuple(AXIS_SIZES.values())), tuple(AXIS_SIZES))
    tile = P(LAT, LON, None)
    return jax.shard_map(
        shards,
        mesh=split,
        in_specs=(tile, P(), P(), P(), tile, P(LAT, LON), P()),
        out_specs=(tile, tile, P(LON, None)),
        check_vma=False,
    )
```

time: 412 us -> 177 us (0.43)
  waiting for transfers between devices: 222 us -> 48.4 us
  matrix products: 69.3 us -> 0 us
  local copies, waits for them, and re-layouts: 51.1 us -> 9.09 us
  Pallas kernels: 0 us -> 35.4 us
  starting transfers between devices: 48.2 us -> 81.6 us
  between operations: 14.5 us -> 1.03 us
  other arithmetic: 4.65 us -> 0.08 us
    reduce_scatter x1 -> x0, waiting for transfers between devices: 109 us -> none  [shards(): lax.psum_scatter(local_terms, 'lon', scatter_dimension=0, tiled=True)]
    psum x1 -> x0, waiting for transfers between devices: 90.2 us -> none  [shards(): weight_grads = lax.psum(longitude_sum, 'lat')]
    dot_general x36 -> x0, matrix products: 69.3 us -> none  [the longest x12 23.9 us: multiply_transposed(): lax.dot_general(left, right, (((1,), (1,)), ((), ())), preferred_element_...]
    all_to_all x0 -> x4, starting transfers between devices: none -> 43.6 us  [the longest x1 23.2 us: shards(): pieces = lax.all_to_all(chip_sum, ('xl', 'z'), 0, 0)]
    pallas_call x0 -> x11, Pallas kernels: none -> 35.4 us  [the longest x1 6.58 us: side_taps(): pl.pallas_call(side_taps_kernel, out_shape=like((pixels, in_width), jnp.b...]
    ppermute x20 -> x17, waiting for transfers between devices: 23.5 us -> 46.4 us  [the longest x8 33.6 us: shift_columns(): lax.ppermute(value, LON, [(i, (i + by) % LON_COUNT) for i in range(LON_CO...]
    ppermute x6 -> x0, local copies, waits for them, and re-layouts: 14.5 us -> none  [shifted_2(): return lax.ppermute(block, axis, route)]
    reshape x20 -> x5, local copies, waits for them, and re-layouts: 16.6 us -> 2.46 us  [the longest x1 1.26 us: shards(): grad_tile = summed_input.reshape(rows, cols, in_width)]
  transfers between devices with their start and end apart: 22 -> 21, of which waited for: 7 -> 9; matrix products, arithmetic and copies ran while one was open for 22% -> 2% of each run, Pallas kernels for 0% -> 10%
where the time goes in v1:
time: 177 us; the launch traced here: 176 us
  starting transfers between devices  81.6 us (46%)
  waiting for transfers between devices  48.4 us (27%)
  Pallas kernels  35.4 us (20%)
  local copies, waits for them, and re-layouts  9.09 us (5%)
    ppermute x8, waiting for transfers between devices, shift_columns(): lax.ppermute(value, LON, [(i, (i + by) % LON_COUNT) for i in range(LON_CO...  33.6 us
    ppermute x8, starting transfers between devices, shift_rows(): return lax.ppermute(value, LAT, pairs)  27.8 us
    all_to_all x1, starting transfers between devices, shards(): pieces = lax.all_to_all(chip_sum, ('xl', 'z'), 0, 0)  23.2 us
    ppermute x8, starting transfers between devices, shift_columns(): lax.ppermute(value, LON, [(i, (i + by) % LON_COUNT) for i in range(LON_CO...  10.2 us
    ppermute x8, waiting for transfers between devices, shift_rows(): return lax.ppermute(value, LAT, pairs)  9.62 us
    all_to_all x1, starting transfers between devices, shards(): gathered = lax.all_to_all(message, LAT, 0, 0)  7.37 us
    all_to_all x1, starting transfers between devices, shards(): lax.all_to_all(slices, LAT, 0, 0).reshape(LAT_COUNT * pixels, -1)  6.82 us
    unnamed x42, local copies, waits for them, and re-layouts  6.64 us
  transfers between devices with their start and end apart: 21, of which 9 were waited for; matrix products, arithmetic and copies ran while one was open for 2% of the time, Pallas kernels for 10%

profile of v1, /device:TPU:32, one launch (start us, length us, event | category | flops | bytes accessed | tf_op | source)
XLA Modules:
  0.0 175.6 jit_solution(1152708506858956686)
XLA Ops:
  0.6 1.6 copy.19
  3.3 6.5 %shard_map.95 = (bf16[144,768]{1,0:T(8,128)(2,1)}, bf16[48,768]{1,0:T(8,128)(2,1)}, bf16[144,768]{1,0:T(8,128)(2,1)}, bf16[48,768]{1,0:T(8,128)(2,1)}) custom-call(bf16[192,2048]{1,0:T(8,128)(2,1)} %reshape.31.flat_ref, bf16[9,2048,256]{2,1,0:T(8,128)(2,1)} %kernel_ref.7), custom_call_target="tpu_custom_call" | custom-call | flops 1207959552 | bytes 6291456 | tf_op jit(solution)/shard_map/pallas_call | solution.py:119
  9.8 1.4 collective-permute-start.1
  11.2 7.6 %collective-permute-done.1.below_far_ref.after_ref = bf16[48,768]{1,0:T(8,128)(2,1)S(1)} collective-permute-done((bf16[48,768]{1,0:T(8,128)(2,1)}, bf16[48,768]{1,0:T(8,128)(2,1)S(1)}, u32[]{:S(2)}, u32[]{:S(2)}) %collective-permute-start.1) | collective-permute-done | bytes 73760 | tf_op jit(solution)/shard_map/ppermute | solution.py:23
  18.8 1.8 %shard_map.97 = bf16[8,192,256]{2,1,0:T(8,128)(2,1)} custom-call(bf16[192,2048]{1,0:T(8,128)(2,1)S(1)} %copy-done, bf16[48,768]{1,0:T(8,128)(2,1)S(1)} %collective-permute-done.1.below_far_ref.after_ref), custom_call_target="tpu_custom_call" | custom-call | flops 201326592 | bytes 1572864 | tf_op jit(solution)/shard_map/pallas_call | solution.py:179
  20.6 6.8 %all-to-all-start = ((bf16[8,192,256]{2,1,0:T(8,128)(2,1)}), bf16[8,192,256]{2,1,0:T(8,128)(2,1)S(1)}, u32[]{:S(2)}, u32[]{:S(2)}) async-start(bf16[8,192,256]{2,1,0:T(8,128)(2,1)} %shard_map.97), calls=%async_computation | async-start | bytes 1572864 | tf_op jit(solution)/shard_map/all_to_all | solution.py:578
  27.4 1.3 collective-permute-start
  28.7 4.6 %collective-permute-start.2 = (bf16[144,768]{1,0:T(8,128)(2,1)S(1)}, bf16[144,768]{1,0:T(8,128)(2,1)S(1)}, u32[]{:S(2)}, u32[]{:S(2)}) collective-permute-start(bf16[144,768]{1,0:T(8,128)(2,1)S(1)} %copy-done.16), channel_id=1, source_target_pairs={{0,64},{32,96},{64,128},{96,160},{128,192},{160,224},{1,65},{33,97... | collective-permute-start | bytes 663560 | tf_op jit(solution)/shard_map/ppermute | solution.py:23
  33.3 6.4 %collective-permute-start.3 = (bf16[48,768]{1,0:T(8,128)(2,1)S(1)}, bf16[48,768]{1,0:T(8,128)(2,1)S(1)}, u32[]{:S(2)}, u32[]{:S(2)}) collective-permute-start(bf16[48,768]{1,0:T(8,128)(2,1)S(1)} %copy-done.18), channel_id=1, source_target_pairs={{0,96},{32,128},{64,160},{96,192},{128,224},{1,97},{33,129},{65,16... | collective-permute-start | bytes 221192 | tf_op jit(solution)/shard_map/ppermute | solution.py:23
  39.8 5.3 %shard_map.94 = (f32[192,768]{1,0:T(8,128)}, f32[192,256]{1,0:T(8,128)}) custom-call(bf16[192,2048]{1,0:T(8,128)(2,1)} %reshape.31.flat_ref, bf16[9,2048,256]{2,1,0:T(8,128)(2,1)} %kernel_ref.7, bf16[2048,256]{1,0:T(8,128)(2,1)} %point_weight_ref.3), custom_call_target="tpu_custom_call" | custom-call | flops 805306368 | bytes 4194304 | tf_op jit(solution)/shard_map/pallas_call | solution.py:146
  46.3 2.4 %collective-permute-start.4 = (bf16[192,256]{1,0:T(8,128)(2,1)S(1)}, bf16[192,256]{1,0:T(8,128)(2,1)S(1)}, u32[]{:S(2)}, u32[]{:S(2)}) collective-permute-start(bf16[192,256]{1,0:T(8,128)(2,1)S(1)} %get-tuple-element.31), channel_id=1, source_target_pairs={{0,29},{1,30},{2,31},{3,0},{4,1},{5,2},{6,3},{7,4},{8,5},{9,6},{10... | collective-permute-start | bytes 294920 | tf_op jit(solution)/shard_map/ppermute | solution.py:27
  49.0 2.4 %collective-permute-done.4.from_east_ref = bf16[192,256]{1,0:T(8,128)(2,1)S(1)} collective-permute-done((bf16[192,256]{1,0:T(8,128)(2,1)S(1)}, bf16[192,256]{1,0:T(8,128)(2,1)S(1)}, u32[]{:S(2)}, u32[]{:S(2)}) %collective-permute-start.4) | collective-permute-done | bytes 98336 | tf_op jit(solution)/shard_map/ppermute | solution.py:27
  51.4 4.6 %collective-permute-done.5.from_west_ref = bf16[192,256]{1,0:T(8,128)(2,1)S(1)} collective-permute-done((bf16[192,256]{1,0:T(8,128)(2,1)S(1)}, bf16[192,256]{1,0:T(8,128)(2,1)S(1)}, u32[]{:S(2)}, u32[]{:S(2)}) %collective-permute-start.5) | collective-permute-done | bytes 98336 | tf_op jit(solution)/shard_map/ppermute | solution.py:27
  58.5 7.4 %all-to-all-start.1 = ((bf16[8,448,256]{2,1,0:T(8,128)(2,1)}), bf16[8,448,256]{2,1,0:T(8,128)(2,1)S(1)}, u32[]{:S(2)}, u32[]{:S(2)}) async-start(bf16[8,448,256]{2,1,0:T(8,128)(2,1)} %copy-done.2), calls=%async_computation.1 | async-start | bytes 3670016 | tf_op jit(solution)/shard_map/all_to_all | solution.py:599
  65.9 1.7 collective-permute-start.8
  67.7 9.8 %collective-permute-done.10 = bf16[1536,256]{1,0:T(8,128)(2,1)} collective-permute-done((bf16[1536,256]{1,0:T(8,128)(2,1)S(1)}, bf16[1536,256]{1,0:T(8,128)(2,1)}, u32[]{:S(2)}, u32[]{:S(2)}) %collective-permute-start.10) | collective-permute-done | bytes 786464 | tf_op jit(solution)/shard_map/ppermute | solution.py:27
  77.4 2.6 %collective-permute-start.9 = (bf16[1536,256]{1,0:T(8,128)(2,1)}, bf16[1536,256]{1,0:T(8,128)(2,1)}, u32[]{:S(2)}, u32[]{:S(2)}) collective-permute-start(bf16[1536,256]{1,0:T(8,128)(2,1)} %collective-permute-done.8), channel_id=1, source_target_pairs={{0,30},{1,31},{2,0},{3,1},{4,2},{5,3},{6,4},{7,5},{8,6},{9,7},{10,... | collective-permute-start | bytes 2359304 | tf_op jit(solution)/shard_map/ppermute | solution.py:27
  80.0 3.4 %collective-permute-start.7 = (bf16[192,256]{1,0:T(8,128)(2,1)S(1)}, bf16[192,256]{1,0:T(8,128)(2,1)S(1)}, u32[]{:S(2)}, u32[]{:S(2)}) collective-permute-start(bf16[192,256]{1,0:T(8,128)(2,1)S(1)} %get-tuple-element.36), channel_id=1, source_target_pairs={{0,29},{1,30},{2,31},{3,0},{4,1},{5,2},{6,3},{7,4},{8,5},{9,6},{10... | collective-permute-start | bytes 294920 | tf_op jit(solution)/shard_map/ppermute | solution.py:27
  83.5 16.8 %collective-permute-done.7.after_west_ref.west_ref = bf16[192,256]{1,0:T(8,128)(2,1)S(1)} collective-permute-done((bf16[192,256]{1,0:T(8,128)(2,1)S(1)}, bf16[192,256]{1,0:T(8,128)(2,1)S(1)}, u32[]{:S(2)}, u32[]{:S(2)}) %collective-permute-start.7) | collective-permute-done | bytes 98336 | tf_op jit(solution)/shard_map/ppermute | solution.py:27
  100.3 5.4 %shard_map.99 = (f32[1408,256]{1,0:T(8,128)S(1)}, f32[1408,256]{1,0:T(8,128)S(1)}) custom-call(s32[1]{0:T(128)} %bitcast.2.core_ref, bf16[1536,256]{1,0:T(8,128)(2,1)S(1)} %bitcast.6, bf16[1536,256]{1,0:T(8,128)(2,1)} %collective-permute-done.9.east_ref, bf16[1536,256]{1,0:T(8,128)(2,1)} %collective-permute-done.11.west_ref, ...), custom_call_target="tpu_custom_call" | custom-call | flops 2013265920 | bytes 8388608 | tf_op jit(solution)/shard_map/pallas_call | solution.py:359
  105.8 3.2 %collective-permute-done.12.received_ref = f32[1408,256]{1,0:T(8,128)S(1)} collective-permute-done((f32[1408,256]{1,0:T(8,128)S(1)}, f32[1408,256]{1,0:T(8,128)S(1)}, u32[]{:S(2)}, u32[]{:S(2)}) %collective-permute-start.12) | collective-permute-done | bytes 1441824 | tf_op jit(solution)/shard_map/ppermute | solution.py:609
  110.0 23.2 %all-to-all-start.2 = ((bf16[16,82,256]{2,1,0:T(8,128)(2,1)}), bf16[16,82,256]{2,1,0:T(8,128)(2,1)S(1)}, u32[]{:S(2)}, u32[]{:S(2)}) async-start(bf16[16,82,256]{2,1,0:T(8,128)(2,1)} %shard_map.100.after_ref), calls=%async_computation.2 | async-start | bytes 1441792 | tf_op jit(solution)/shard_map/all_to_all | solution.py:610
  133.2 6.1 %shard_map.101 = (f32[192,2048]{1,0:T(8,128)}, bf16[144,512]{1,0:T(8,128)(2,1)}, bf16[48,512]{1,0:T(8,128)(2,1)}, bf16[144,512]{1,0:T(8,128)(2,1)}, bf16[48,512]{1,0:T(8,128)(2,1)}, /*index=5*/bf16[192,512]{1,0:T(8,128)(2,1)}) custom-call(s32[1]{0:T(128)} %bitcast.1.lat_ref, bf16[8,448,256]{2,1,0:T(8,128)(2,1)} %copy-done.1, bf16[192,256]{1,0:T(8,128)(2,1)} %copy-done.10, ...), custom_call_target="tpu_custom_call" | custom-call | flops 805306368 | bytes 6291456 | tf_op jit(solution)/shard_map/pallas_call | solution.py:503
  139.3 1.3 collective-permute-start.13
  140.6 4.6 %collective-permute-start.15 = (bf16[144,512]{1,0:T(8,128)(2,1)}, bf16[144,512]{1,0:T(8,128)(2,1)S(1)}, u32[]{:S(2)}, u32[]{:S(2)}) collective-permute-start(bf16[144,512]{1,0:T(8,128)(2,1)} %get-tuple-element.43), channel_id=1, source_target_pairs={{0,64},{32,96},{64,128},{96,160},{128,192},{160,224},{1,65},{33,97... | collective-permute-start | bytes 442376 | tf_op jit(solution)/shard_map/ppermute | solution.py:23
  145.2 1.3 collective-permute-start.14
  146.5 7.0 %collective-permute-start.16 = (bf16[48,512]{1,0:T(8,128)(2,1)}, bf16[48,512]{1,0:T(8,128)(2,1)S(1)}, u32[]{:S(2)}, u32[]{:S(2)}) collective-permute-start(bf16[48,512]{1,0:T(8,128)(2,1)} %get-tuple-element.44), channel_id=1, source_target_pairs={{0,96},{32,128},{64,160},{96,192},{128,224},{1,97},{33,129},{65,16... | collective-permute-start | bytes 147464 | tf_op jit(solution)/shard_map/ppermute | solution.py:23
  153.8 1.7 collective-permute-done.16.down_far_ref.refs_3_
  156.5 6.2 %all-to-all-start.3 = ((f32[8,82,256]{2,1,0:T(8,128)}), f32[8,82,256]{2,1,0:T(8,128)S(1)}, u32[]{:S(2)}, u32[]{:S(2)}) async-start(f32[8,82,256]{2,1,0:T(8,128)} %shard_map.103), calls=%async_computation.3 | async-start | bytes 1441792 | tf_op jit(solution)/shard_map/all_to_all | solution.py:621
  163.4 6.6 %shard_map.102 = bf16[192,2048]{1,0:T(8,128)(2,1)} custom-call(f32[192,2048]{1,0:T(8,128)} %get-tuple-element.39.total_ref, bf16[192,512]{1,0:T(8,128)(2,1)} %get-tuple-element.40.sides_ref, bf16[144,512]{1,0:T(8,128)(2,1)} %copy-done.4, bf16[48,512]{1,0:T(8,128)(2,1)} %copy-done.7, bf16[144,512]{1,0:T(8,128)(2,1)} %copy-done.5, bf16[48,512]{1,0:T(8,128)(2,1)} %copy-done.8, ...), custom_call_target="tpu_custom_call" | custom-call | flops 1207959552 | bytes 67108864 | tf_op jit(solution)/shard_map/pallas_call | solution.py:545
  171.3 1.3 copy.23
  172.6 1.9 %all-to-all-done.3.parts_ref = f32[8,82,256]{2,1,0:T(8,128)S(1)} async-done(((f32[8,82,256]{2,1,0:T(8,128)}), f32[8,82,256]{2,1,0:T(8,128)S(1)}, u32[]{:S(2)}, u32[]{:S(2)}) %all-to-all-start.3) | async-done | bytes 671776 | tf_op jit(solution)/shard_map/all_to_all | solution.py:621
  (69 shorter events, 10.5 us)
Async XLA Ops:
  3.3 15.5 %copy-start = (bf16[192,2048]{1,0:T(8,128)(2,1)S(1)}, bf16[192,2048]{1,0:T(8,128)(2,1)}, u32[]{:S(2)}) copy-start(bf16[192,2048]{1,0:T(8,128)(2,1)} %reshape.31.flat_ref) | copy-start | bytes 2359300
  9.8 17.6 %copy-start.17 = (bf16[144,768]{1,0:T(8,128)(2,1)S(1)}, bf16[144,768]{1,0:T(8,128)(2,1)}, u32[]{:S(2)}) copy-start(bf16[144,768]{1,0:T(8,128)(2,1)} %get-tuple-element.26) | copy-start | bytes 663556
  9.8 18.9 %copy-start.16 = (bf16[144,768]{1,0:T(8,128)(2,1)S(1)}, bf16[144,768]{1,0:T(8,128)(2,1)}, u32[]{:S(2)}) copy-start(bf16[144,768]{1,0:T(8,128)(2,1)} %get-tuple-element.28) | copy-start | bytes 663556
  9.8 23.5 %copy-start.18 = (bf16[48,768]{1,0:T(8,128)(2,1)S(1)}, bf16[48,768]{1,0:T(8,128)(2,1)}, u32[]{:S(2)}) copy-start(bf16[48,768]{1,0:T(8,128)(2,1)} %get-tuple-element.29) | copy-start | bytes 221188
  9.8 9.0 %collective-permute-start.1 = (bf16[48,768]{1,0:T(8,128)(2,1)}, bf16[48,768]{1,0:T(8,128)(2,1)S(1)}, u32[]{:S(2)}, u32[]{:S(2)}) collective-permute-start(bf16[48,768]{1,0:T(8,128)(2,1)} %get-tuple-element.27), channel_id=1, source_target_pairs={{96,0},{128,32},{160,64},{192,96},{224,128},{97,1},{129,33},{161,6... | collective-permute-start | bytes 221192 | tf_op jit(solution)/shard_map/ppermute | solution.py:23
  20.6 35.4 %all-to-all-start = ((bf16[8,192,256]{2,1,0:T(8,128)(2,1)}), bf16[8,192,256]{2,1,0:T(8,128)(2,1)S(1)}, u32[]{:S(2)}, u32[]{:S(2)}) async-start(bf16[8,192,256]{2,1,0:T(8,128)(2,1)} %shard_map.97), calls=%async_computation | async-start | bytes 1572864 | tf_op jit(solution)/shard_map/all_to_all | solution.py:578
  27.4 17.7 %collective-permute-start = (bf16[144,768]{1,0:T(8,128)(2,1)S(1)}, bf16[144,768]{1,0:T(8,128)(2,1)S(1)}, u32[]{:S(2)}, u32[]{:S(2)}) collective-permute-start(bf16[144,768]{1,0:T(8,128)(2,1)S(1)} %copy-done.17), channel_id=1, source_target_pairs={{64,0},{96,32},{128,64},{160,96},{192,128},{224,160},{65,1},{97,33... | collective-permute-start | bytes 663560 | tf_op jit(solution)/shard_map/ppermute | solution.py:23
  28.7 16.4 %collective-permute-start.2 = (bf16[144,768]{1,0:T(8,128)(2,1)S(1)}, bf16[144,768]{1,0:T(8,128)(2,1)S(1)}, u32[]{:S(2)}, u32[]{:S(2)}) collective-permute-start(bf16[144,768]{1,0:T(8,128)(2,1)S(1)} %copy-done.16), channel_id=1, source_target_pairs={{0,64},{32,96},{64,128},{96,160},{128,192},{160,224},{1,65},{33,97... | collective-permute-start | bytes 663560 | tf_op jit(solution)/shard_map/ppermute | solution.py:23
  33.3 15.4 %copy-start.14 = (s32[16,12]{1,0:T(8,128)S(1)}, s32[16,12]{1,0:T(8,128)}, u32[]{:S(2)}) copy-start(s32[16,12]{1,0:T(8,128)} %param.12) | copy-start | bytes 2308
  33.3 15.4 %copy-start.15 = (f32[3]{0:T(128)S(1)}, f32[3]{0:T(128)}, u32[]{:S(2)}) copy-start(f32[3]{0:T(128)} %param.13) | copy-start | bytes 40
  33.3 15.6 %copy-start.13 = (bf16[16,12,256]{2,0,1:T(8,128)(2,1)S(1)}, bf16[16,12,256]{2,0,1:T(8,128)(2,1)}, u32[]{:S(2)}) copy-start(bf16[16,12,256]{2,0,1:T(8,128)(2,1)} %param.11) | copy-start | bytes 294916
  33.3 11.8 %collective-permute-start.3 = (bf16[48,768]{1,0:T(8,128)(2,1)S(1)}, bf16[48,768]{1,0:T(8,128)(2,1)S(1)}, u32[]{:S(2)}, u32[]{:S(2)}) collective-permute-start(bf16[48,768]{1,0:T(8,128)(2,1)S(1)} %copy-done.18), channel_id=1, source_target_pairs={{0,96},{32,128},{64,160},{96,192},{128,224},{1,97},{33,129},{65,16... | collective-permute-start | bytes 221192 | tf_op jit(solution)/shard_map/ppermute | solution.py:23
  39.8 16.2 %copy-start.6 = (bf16[2,256,256]{2,1,0:T(8,128)(2,1)S(1)}, bf16[2,256,256]{2,1,0:T(8,128)(2,1)}, u32[]{:S(2)}) copy-start(bf16[2,256,256]{2,1,0:T(8,128)(2,1)} %project_ref.1) | copy-start | bytes 786436
  46.2 9.8 %copy-start.9 = (f32[192,256]{1,0:T(8,128)S(1)}, f32[192,256]{1,0:T(8,128)}, u32[]{:S(2)}) copy-start(f32[192,256]{1,0:T(8,128)} %get-tuple-element.24.point_ref) | copy-start | bytes 589828
  46.3 5.1 %collective-permute-start.4 = (bf16[192,256]{1,0:T(8,128)(2,1)S(1)}, bf16[192,256]{1,0:T(8,128)(2,1)S(1)}, u32[]{:S(2)}, u32[]{:S(2)}) collective-permute-start(bf16[192,256]{1,0:T(8,128)(2,1)S(1)} %get-tuple-element.31), channel_id=1, source_target_pairs={{0,29},{1,30},{2,31},{3,0},{4,1},{5,2},{6,3},{7,4},{8,5},{9,6},{10... | collective-permute-start | bytes 294920 | tf_op jit(solution)/shard_map/ppermute | solution.py:27
  48.7 7.3 %collective-permute-start.5 = (bf16[192,256]{1,0:T(8,128)(2,1)S(1)}, bf16[192,256]{1,0:T(8,128)(2,1)S(1)}, u32[]{:S(2)}, u32[]{:S(2)}) collective-permute-start(bf16[192,256]{1,0:T(8,128)(2,1)S(1)} %get-tuple-element.32), channel_id=1, source_target_pairs={{0,3},{1,4},{2,5},{3,6},{4,7},{5,8},{6,9},{7,10},{8,11},{9,12},{10... | collective-permute-start | bytes 294920 | tf_op jit(solution)/shard_map/ppermute | solution.py:27
  58.5 41.7 %all-to-all-start.1 = ((bf16[8,448,256]{2,1,0:T(8,128)(2,1)}), bf16[8,448,256]{2,1,0:T(8,128)(2,1)S(1)}, u32[]{:S(2)}, u32[]{:S(2)}) async-start(bf16[8,448,256]{2,1,0:T(8,128)(2,1)} %copy-done.2), calls=%async_computation.1 | async-start | bytes 3670016 | tf_op jit(solution)/shard_map/all_to_all | solution.py:599
  65.9 11.5 %collective-permute-start.10 = (bf16[1536,256]{1,0:T(8,128)(2,1)S(1)}, bf16[1536,256]{1,0:T(8,128)(2,1)}, u32[]{:S(2)}, u32[]{:S(2)}) collective-permute-start(bf16[1536,256]{1,0:T(8,128)(2,1)S(1)} %bitcast.4), channel_id=1, source_target_pairs={{0,1},{1,2},{2,3},{3,4},{4,5},{5,6},{6,7},{7,8},{8,9},{9,10},{10,1... | collective-permute-start | bytes 2359304 | tf_op jit(solution)/shard_map/ppermute | solution.py:27
  65.9 11.5 %collective-permute-start.8 = (bf16[1536,256]{1,0:T(8,128)(2,1)S(1)}, bf16[1536,256]{1,0:T(8,128)(2,1)}, u32[]{:S(2)}, u32[]{:S(2)}) collective-permute-start(bf16[1536,256]{1,0:T(8,128)(2,1)S(1)} %bitcast.5), channel_id=1, source_target_pairs={{0,31},{1,0},{2,1},{3,2},{4,3},{5,4},{6,5},{7,6},{8,7},{9,8},{10,9... | collective-permute-start | bytes 2359304 | tf_op jit(solution)/shard_map/ppermute | solution.py:27
  77.4 22.8 %collective-permute-start.11 = (bf16[1536,256]{1,0:T(8,128)(2,1)}, bf16[1536,256]{1,0:T(8,128)(2,1)}, u32[]{:S(2)}, u32[]{:S(2)}) collective-permute-start(bf16[1536,256]{1,0:T(8,128)(2,1)} %collective-permute-done.10), channel_id=1, source_target_pairs={{0,2},{1,3},{2,4},{3,5},{4,6},{5,7},{6,8},{7,9},{8,10},{9,11},{10,... | collective-permute-start | bytes 2359304 | tf_op jit(solution)/shard_map/ppermute | solution.py:27
  77.4 22.8 %collective-permute-start.9 = (bf16[1536,256]{1,0:T(8,128)(2,1)}, bf16[1536,256]{1,0:T(8,128)(2,1)}, u32[]{:S(2)}, u32[]{:S(2)}) collective-permute-start(bf16[1536,256]{1,0:T(8,128)(2,1)} %collective-permute-done.8), channel_id=1, source_target_pairs={{0,30},{1,31},{2,0},{3,1},{4,2},{5,3},{6,4},{7,5},{8,6},{9,7},{10,... | collective-permute-start | bytes 2359304 | tf_op jit(solution)/shard_map/ppermute | solution.py:27
  80.0 20.2 %collective-permute-start.7 = (bf16[192,256]{1,0:T(8,128)(2,1)S(1)}, bf16[192,256]{1,0:T(8,128)(2,1)S(1)}, u32[]{:S(2)}, u32[]{:S(2)}) collective-permute-start(bf16[192,256]{1,0:T(8,128)(2,1)S(1)} %get-tuple-element.36), channel_id=1, source_target_pairs={{0,29},{1,30},{2,31},{3,0},{4,1},{5,2},{6,3},{7,4},{8,5},{9,6},{10... | collective-permute-start | bytes 294920 | tf_op jit(solution)/shard_map/ppermute | solution.py:27
  83.4 16.8 %collective-permute-start.6 = (bf16[192,256]{1,0:T(8,128)(2,1)S(1)}, bf16[192,256]{1,0:T(8,128)(2,1)S(1)}, u32[]{:S(2)}, u32[]{:S(2)}) collective-permute-start(bf16[192,256]{1,0:T(8,128)(2,1)S(1)} %get-tuple-element.36), channel_id=1, source_target_pairs={{0,3},{1,4},{2,5},{3,6},{4,7},{5,8},{6,9},{7,10},{8,11},{9,12},{10... | collective-permute-start | bytes 294920 | tf_op jit(solution)/shard_map/ppermute | solution.py:27
  100.2 5.4 %copy-start.11 = (bf16[192,256]{1,0:T(8,128)(2,1)}, bf16[192,256]{1,0:T(8,128)(2,1)S(1)}, u32[]{:S(2)}) copy-start(bf16[192,256]{1,0:T(8,128)(2,1)S(1)} %collective-permute-done.7.after_west_ref.west_ref) | copy-start | bytes 294916
  100.3 5.4 %copy-start.12 = (bf16[192,256]{1,0:T(8,128)(2,1)}, bf16[192,256]{1,0:T(8,128)(2,1)S(1)}, u32[]{:S(2)}) copy-start(bf16[192,256]{1,0:T(8,128)(2,1)S(1)} %collective-permute-done.6.after_east_ref.east_ref) | copy-start | bytes 294916
  105.7 3.3 %collective-permute-start.12 = (f32[1408,256]{1,0:T(8,128)S(1)}, f32[1408,256]{1,0:T(8,128)S(1)}, u32[]{:S(2)}, u32[]{:S(2)}) collective-permute-start(f32[1408,256]{1,0:T(8,128)S(1)} %get-tuple-element.38), channel_id=1, source_target_pairs={{0,1},{1,0},{2,3},{3,2},{4,5},{5,4},{6,7},{7,6},{8,9},{9,8},{10,11... | collective-permute-start | bytes 4325384 | tf_op jit(solution)/shard_map/ppermute | solution.py:609
  110.0 45.5 %all-to-all-start.2 = ((bf16[16,82,256]{2,1,0:T(8,128)(2,1)}), bf16[16,82,256]{2,1,0:T(8,128)(2,1)S(1)}, u32[]{:S(2)}, u32[]{:S(2)}) async-start(bf16[16,82,256]{2,1,0:T(8,128)(2,1)} %shard_map.100.after_ref), calls=%async_computation.2 | async-start | bytes 1441792 | tf_op jit(solution)/shard_map/all_to_all | solution.py:610
  139.3 16.2 %collective-permute-start.13 = (bf16[144,512]{1,0:T(8,128)(2,1)}, bf16[144,512]{1,0:T(8,128)(2,1)S(1)}, u32[]{:S(2)}, u32[]{:S(2)}) collective-permute-start(bf16[144,512]{1,0:T(8,128)(2,1)} %get-tuple-element.41), channel_id=1, source_target_pairs={{64,0},{96,32},{128,64},{160,96},{192,128},{224,160},{65,1},{97,33... | collective-permute-start | bytes 442376 | tf_op jit(solution)/shard_map/ppermute | solution.py:23
  140.6 14.9 %collective-permute-start.15 = (bf16[144,512]{1,0:T(8,128)(2,1)}, bf16[144,512]{1,0:T(8,128)(2,1)S(1)}, u32[]{:S(2)}, u32[]{:S(2)}) collective-permute-start(bf16[144,512]{1,0:T(8,128)(2,1)} %get-tuple-element.43), channel_id=1, source_target_pairs={{0,64},{32,96},{64,128},{96,160},{128,192},{160,224},{1,65},{33,97... | collective-permute-start | bytes 442376 | tf_op jit(solution)/shard_map/ppermute | solution.py:23
  145.2 8.6 %collective-permute-start.14 = (bf16[48,512]{1,0:T(8,128)(2,1)}, bf16[48,512]{1,0:T(8,128)(2,1)S(1)}, u32[]{:S(2)}, u32[]{:S(2)}) collective-permute-start(bf16[48,512]{1,0:T(8,128)(2,1)} %get-tuple-element.42), channel_id=1, source_target_pairs={{96,0},{128,32},{160,64},{192,96},{224,128},{97,1},{129,33},{161,6... | collective-permute-start | bytes 147464 | tf_op jit(solution)/shard_map/ppermute | solution.py:23
  146.5 9.0 %collective-permute-start.16 = (bf16[48,512]{1,0:T(8,128)(2,1)}, bf16[48,512]{1,0:T(8,128)(2,1)S(1)}, u32[]{:S(2)}, u32[]{:S(2)}) collective-permute-start(bf16[48,512]{1,0:T(8,128)(2,1)} %get-tuple-element.44), channel_id=1, source_target_pairs={{0,96},{32,128},{64,160},{96,192},{128,224},{1,97},{33,129},{65,16... | collective-permute-start | bytes 147464 | tf_op jit(solution)/shard_map/ppermute | solution.py:23
  156.5 18.0 %all-to-all-start.3 = ((f32[8,82,256]{2,1,0:T(8,128)}), f32[8,82,256]{2,1,0:T(8,128)S(1)}, u32[]{:S(2)}, u32[]{:S(2)}) async-start(f32[8,82,256]{2,1,0:T(8,128)} %shard_map.103), calls=%async_computation.3 | async-start | bytes 1441792 | tf_op jit(solution)/shard_map/all_to_all | solution.py:621
  (8 other events, 14.2 us)

commit v2 on v1

v2 whole, which is shorter than its diff:
```python
import functools

import jax
import jax.numpy as jnp
from jax import lax
from jax.experimental import pallas as pl
from jax.experimental.pallas import tpu as pltpu
from jax.sharding import Mesh, PartitionSpec as P

ATROUS_DILATION = 36
LAT = ("y", "xh")
LON = ("xl", "z", "c")
AXIS_SIZES = {"y": 4, "xh": 2, "xl": 2, "z": 8, "c": 2}
LAT_COUNT = 8
LON_COUNT = 32
VMEM = pl.BlockSpec(memory_space=pltpu.VMEM)
SMEM = pl.BlockSpec(memory_space=pltpu.SMEM)
ANY = pl.BlockSpec(memory_space=pl.ANY)


def shift_rows(value, by):
    pairs = [(i, i + by) for i in range(LAT_COUNT) if 0 <= i + by < LAT_COUNT]
    return lax.ppermute(value, LAT, pairs)


def shift_columns(value, by):
    return lax.ppermute(value, LON, [(i, (i + by) % LON_COUNT) for i in range(LON_COUNT)])


def contract_row_axes(left, right):
    return lax.dot_general(
        left, right, (((0,), (0,)), ((), ())), preferred_element_type=jnp.float32
    )


def multiply_transposed(left, right):
    return lax.dot_general(
        left, right, (((1,), (1,)), ((), ())), preferred_element_type=jnp.float32
    )


def multiply(left, right):
    return jnp.dot(left, right, preferred_element_type=jnp.float32)


def sigmoid(value):
    return 1.0 / (1.0 + jnp.exp(-value))


def params(megabytes=24):
    return pltpu.CompilerParams(vmem_limit_bytes=megabytes * 2**20)


def cost(flops, moved):
    return pl.CostEstimate(flops=int(flops), bytes_accessed=int(moved), transcendentals=0)


def like(shape, dtype):
    return jax.ShapeDtypeStruct(shape, dtype)


def stream(sources, buffer_ref, semaphores):
    depth = buffer_ref.shape[0]

    def copy(at):
        return pltpu.make_async_copy(
            sources[at], buffer_ref.at[at % depth], semaphores.at[at % depth]
        )

    for at in range(min(depth - 1, len(sources))):
        copy(at).start()
    for at in range(len(sources)):
        if at + depth - 1 < len(sources):
            copy(at + depth - 1).start()
        copy(at).wait()
        yield buffer_ref.at[at % depth]


STREAM_DEPTH = 3


def stream_scratch(in_width, width):
    return [
        pltpu.VMEM((STREAM_DEPTH, in_width, width), jnp.bfloat16),
        pltpu.SemaphoreType.DMA((STREAM_DEPTH,)),
    ]


def products_kernel(
    flat_ref,
    kernel_ref,
    point_weight_ref,
    after_ref,
    below_near_ref,
    below_far_ref,
    above_near_ref,
    above_far_ref,
    level_ref,
    point_ref,
):
    width = kernel_ref.shape[2]
    pixels = flat_ref.shape[0]
    far = below_far_ref.shape[0]
    for at, tap in enumerate((6, 7, 8, 0, 1, 2, 3, 4, 5)):
        product = multiply(flat_ref[...], kernel_ref[tap])
        rounded = product.astype(jnp.bfloat16)
        lanes = slice((at % 3) * width, (at % 3 + 1) * width)
        if at < 3:
            below_far_ref[:, lanes] = rounded[:far]
            below_near_ref[:, lanes] = rounded[far:]
        elif at < 6:
            above_near_ref[:, lanes] = rounded[: pixels - far]
            above_far_ref[:, lanes] = rounded[pixels - far :]
        else:
            level_ref[:, lanes] = product
    point_ref[...] = multiply(flat_ref[...], point_weight_ref[...])


def tap_products(flat, kernel, point_weight, far, after):
    pixels, in_width = flat.shape
    width = kernel.shape[2]
    near_shape = like((pixels - far, 3 * width), jnp.bfloat16)
    far_shape = like((far, 3 * width), jnp.bfloat16)
    return pl.pallas_call(
        products_kernel,
        out_shape=(near_shape, far_shape, near_shape, far_shape)
        + (like((pixels, 3 * width), jnp.float32), like((pixels, width), jnp.float32)),
        in_specs=[VMEM] * 3 + [ANY],
        out_specs=(VMEM,) * 6,
        compiler_params=params(),
        cost_estimate=cost(20 * pixels * in_width * width, 20 * in_width * width),
    )(flat, kernel, point_weight, after)


def slices_kernel(flat_ref, slices_ref):
    count, _, size = slices_ref.shape
    part = size // count
    source = lax.broadcasted_iota(jnp.int32, (size, size), 0)
    target = lax.broadcasted_iota(jnp.int32, (size, size), 1)
    wanted = (source % count) * part + source // count
    picker = jnp.where(target == wanted, 1.0, 0.0).astype(jnp.bfloat16)
    sorted_blocks = [
        multiply(flat_ref[:, size * b : size * (b + 1)], picker).astype(jnp.bfloat16)
        for b in range(count)
    ]
    for a in range(count):
        slices_ref[a] = jnp.concatenate(
            [block[:, part * a : part * (a + 1)] for block in sorted_blocks], axis=1
        )


def channel_slices(flat):
    pixels, in_width = flat.shape
    return pl.pallas_call(
        slices_kernel,
        out_shape=like((LAT_COUNT, pixels, in_width // LAT_COUNT), jnp.bfloat16),
        in_specs=[VMEM],
        out_specs=VMEM,
        compiler_params=params(),
        cost_estimate=cost(10**10, 4 * pixels * in_width),
    )(flat)


def row_sum_kernel(
    level_ref,
    below_near_ref,
    below_far_ref,
    above_near_ref,
    above_far_ref,
    features_in_ref,
    west_ref,
    east_ref,
    center_ref,
    features_out_ref,
):
    width = center_ref.shape[1]
    near, far = below_near_ref.shape[0], below_far_ref.shape[0]
    f32 = jnp.float32
    below = jnp.concatenate([below_near_ref[...].astype(f32), below_far_ref[...].astype(f32)])
    above = jnp.concatenate([above_far_ref[...].astype(f32), above_near_ref[...].astype(f32)])
    total = level_ref[...] + below + above
    west_ref[...] = total[:, :width].astype(jnp.bfloat16)
    center_ref[...] = total[:, width : 2 * width]
    east_ref[...] = total[:, 2 * width :].astype(jnp.bfloat16)


def row_sum(level, received, features):
    pixels, wide = level.shape
    side = like((pixels, wide // 3), jnp.bfloat16)
    return pl.pallas_call(
        row_sum_kernel,
        out_shape=(
            side,
            side,
            like((pixels, wide // 3), jnp.float32),
            like(features.shape, features.dtype),
        ),
        in_specs=[VMEM] * 5 + [ANY],
        out_specs=(VMEM,) * 3 + (ANY,),
        input_output_aliases={5: 3},
        compiler_params=params(),
        cost_estimate=cost(3 * pixels * wide, 8 * pixels * wide),
    )(level, *received, features)


def head_kernel(
    point_ref,
    center_ref,
    from_east_ref,
    from_west_ref,
    project_ref,
    upstream_ref,
    pixel_weight_ref,
    after_east_ref,
    after_west_ref,
    head_ref,
    grads_ref,
    message_ref,
    *terms_refs,
):
    bf16, f32 = jnp.bfloat16, jnp.float32
    width = point_ref.shape[1]
    pre_list = [
        point_ref[...],
        center_ref[...] + from_east_ref[...].astype(f32) + from_west_ref[...].astype(f32),
    ]
    gates = [sigmoid(pre) for pre in pre_list]
    acts = [(pre * gate).astype(bf16) for pre, gate in zip(pre_list, gates)]
    mixed = multiply(acts[0], project_ref[0]) + multiply(acts[1], project_ref[1])
    gate = sigmoid(mixed)
    head_ref[...] = (mixed * gate).astype(bf16)
    slope = gate * (1.0 + mixed * (1.0 - gate))
    out_grad = (upstream_ref[...].astype(f32) * pixel_weight_ref[...] * slope).astype(bf16)
    grads = [
        (
            multiply_transposed(out_grad, project_ref[k])
            * (gates[k] * (1.0 + pre_list[k] * (1.0 - gates[k])))
        ).astype(bf16)
        for k in range(2)
    ]
    pixels = grads_ref.shape[0]
    grads_ref[:, :width] = grads[1]
    grads_ref[:, width:] = grads[0]
    for k in range(2):
        terms = contract_row_axes(acts[k], out_grad)
        for half, terms_ref in enumerate(terms_refs):
            terms_ref[width * k : width * (k + 1), :] = terms[:, 128 * half : 128 * half + 128]
    count = message_ref.shape[0]
    part = 2 * width // count
    for a in range(count):
        message_ref[a, :pixels, :] = grads[1]
        message_ref[a, pixels : 2 * pixels, :] = grads[0]
        for half, terms_ref in enumerate(terms_refs):
            message_ref[a, 2 * pixels :, 128 * half : 128 * half + 128] = terms_ref[
                pl.ds(a, part, stride=count), :
            ].astype(bf16)


def head(point_pre, center, from_east, from_west, project, upstream, pixel_weight, after):
    pixels, width = point_pre.shape
    part = 2 * width // LAT_COUNT
    bf16, f32 = jnp.bfloat16, jnp.float32
    return pl.pallas_call(
        head_kernel,
        out_shape=(
            like((pixels, width), bf16),
            like((pixels, 2 * width), bf16),
            like((LAT_COUNT, 2 * pixels + part, width), bf16),
        ),
        in_specs=[VMEM] * 7 + [ANY] * 2,
        out_specs=(VMEM,) * 3,
        scratch_shapes=[pltpu.VMEM((2 * width, 128), f32)] * (width // 128),
        compiler_params=params(),
        cost_estimate=cost(12 * pixels * width * width, 24 * pixels * width),
    )(point_pre, center, from_east, from_west, project, upstream, pixel_weight, *after)


def weight_terms_kernel(
    span,
    chunk,
    place_ref,
    center_ref,
    east_first_ref,
    west_first_ref,
    east_second_ref,
    west_second_ref,
    message_ref,
    east_grad_ref,
    west_grad_ref,
    kept_ref,
    sent_ref,
    windows_ref,
    up_near_ref,
    up_far_ref,
    down_near_ref,
    down_far_ref,
    framed_ref,
):
    total, width = center_ref.shape
    pixels = total // LAT_COUNT
    room = padded(chunk)
    core, lat = place_ref[0], place_ref[1]
    far = up_far_ref.shape[0]
    columns = {
        0: (center_ref,),
        1: (east_first_ref, east_second_ref),
        -1: (west_first_ref, west_second_ref),
    }

    edge = jnp.zeros((span, width), framed_ref.dtype)
    framed_ref[total : total + span, :width] = edge
    framed_ref[span : 2 * span, 2 * width : 3 * width] = edge
    for band in range(LAT_COUNT):
        piece = message_ref[band, :pixels, :]
        for i in (-1, 0, 1):
            first = span + span * i + band * pixels
            framed_ref[first : first + pixels, (i + 1) * width : (i + 2) * width] = piece
        first = span + band * pixels
        framed_ref[first : first + pixels, 3 * width :] = message_ref[band, pixels : 2 * pixels, :]
    for at, side_ref in enumerate((east_grad_ref, west_grad_ref)):
        lanes = slice(at * width, (at + 1) * width)
        side = side_ref[...]
        up_near_ref[:, lanes] = side[far:]
        up_far_ref[:, lanes] = side[:far]
        down_near_ref[:, lanes] = side[: pixels - far]
        down_far_ref[:, lanes] = side[pixels - far :]
    own_rows = pl.ds(pl.multiple_of(span + lat * pixels, 16), pixels)
    windows_ref[...] = framed_ref[own_rows, : 3 * width]

    def store(first, value):
        count = value.shape[0]
        pieces = []
        at = 0
        while at < count:
            index, offset = divmod(first + at, chunk)
            size = min(chunk - offset, count - at)
            pieces.append((index, offset, at, size))
            at += size
        for owner in (0, 1):

            @pl.when(core == owner)
            def _():
                for index, offset, at, size in pieces:
                    target = kept_ref if index % 2 == owner else sent_ref
                    first_row = index // 2 * room + offset
                    target[first_row : first_row + size, :] = value[at : at + size]

    for j in (0, 1, -1):
        wide = 4 * width if j == 0 else 3 * width
        product, low = 0.0, span
        for part_ref in columns[j]:
            high = low + part_ref.shape[0]
            product += contract_row_axes(part_ref[...], framed_ref[low:high, :wide])
            low = high
        for i in (-1, 0, 1):
            store((3 * (i + 1) + j + 1) * width, product[:, (i + 1) * width : (i + 2) * width])
        if j == 0:
            project_rows = jnp.sum(message_ref[:, 2 * pixels :, :].astype(jnp.float32), axis=0)
            store(9 * width, project_rows)
            store(9 * width + project_rows.shape[0], product[:, 3 * width :])


def padded(chunk):
    return (chunk + 7) // 8 * 8


def weight_terms(span, place, features, message, sides):
    total, width = features[0].shape
    pixels = total // LAT_COUNT
    far = span % pixels
    chunk = (10 * width + message.shape[1] - 2 * pixels) // LON_COUNT
    out = like((LON_COUNT // 2 * padded(chunk), width), jnp.float32)
    near_shape = like((pixels - far, 2 * width), jnp.bfloat16)
    far_shape = like((far, 2 * width), jnp.bfloat16)
    return pl.pallas_call(
        functools.partial(weight_terms_kernel, span, chunk),
        out_shape=(out, out, like((pixels, 3 * width), jnp.bfloat16))
        + (near_shape, far_shape, near_shape, far_shape),
        in_specs=[SMEM] + [VMEM] * 8,
        out_specs=(VMEM,) * 7,
        scratch_shapes=[pltpu.VMEM((2 * span + total, 4 * width), jnp.bfloat16)],
        compiler_params=params(),
        cost_estimate=cost(20 * total * width * width, 8 * 2**20),
    )(place, *features, message, *sides)


def pair_sum_kernel(kept_ref, received_ref, out_ref):
    count, chunk, _ = out_ref.shape
    room = kept_ref.shape[0] // count
    for at in range(count):
        rows = slice(room * at, room * at + chunk)
        out_ref[at] = (kept_ref[rows, :] + received_ref[rows, :]).astype(jnp.bfloat16)


def pair_sum(kept, received, chunk):
    return pl.pallas_call(
        pair_sum_kernel,
        out_shape=like((LON_COUNT // 2, chunk, kept.shape[1]), jnp.bfloat16),
        in_specs=[VMEM] * 2,
        out_specs=VMEM,
        compiler_params=params(),
        cost_estimate=cost(kept.size, 10 * kept.size),
    )(kept, received)


def piece_sum_kernel(pieces_ref, *refs):
    out_ref = refs[-1]
    total = pieces_ref[0].astype(jnp.float32)
    for at in range(1, pieces_ref.shape[0]):
        total = total + pieces_ref[at].astype(jnp.float32)
    for at in range(out_ref.shape[0]):
        out_ref[at] = total


def piece_sum(pieces, after):
    return pl.pallas_call(
        piece_sum_kernel,
        out_shape=like((LAT_COUNT,) + pieces.shape[1:], jnp.float32),
        in_specs=[VMEM] + [ANY] * len(after),
        out_specs=VMEM,
        compiler_params=params(),
        cost_estimate=cost(pieces.size, 4 * pieces.size),
    )(pieces, *after)


def interleave_kernel(parts_ref, out_ref, *sorted_refs):
    count, size, _ = parts_ref.shape
    for half, sorted_ref in enumerate(sorted_refs):
        lanes = slice(128 * half, 128 * half + 128)
        for a in range(count):
            sorted_ref[pl.ds(a, size, stride=count), :] = parts_ref[a, :, lanes]
        out_ref[:, lanes] = sorted_ref[...]


def interleave(parts):
    count, size, width = parts.shape
    return pl.pallas_call(
        interleave_kernel,
        out_shape=like((count * size, width), jnp.float32),
        in_specs=[VMEM],
        out_specs=VMEM,
        scratch_shapes=[pltpu.VMEM((count * size, 128), jnp.float32)] * (width // 128),
        compiler_params=params(),
        cost_estimate=cost(parts.size, 8 * parts.size),
    )(parts)


def add_product(total_ref, window, tap_ref, first):
    size = 512
    for low in range(0, total_ref.shape[1], size):
        lanes = slice(low, low + size)
        product = multiply_transposed(window, tap_ref[low : low + size, :])
        total_ref[:, lanes] = product if first else total_ref[:, lanes] + product


def input_gradient_kernel(
    windows_ref,
    grads_ref,
    east_ref,
    west_ref,
    up_near_ref,
    up_far_ref,
    down_near_ref,
    down_far_ref,
    kernel_ref,
    point_weight_ref,
    out_ref,
    total_ref,
    buffer_ref,
    semaphores,
):
    width = buffer_ref.shape[2]
    sources = [point_weight_ref] + [kernel_ref.at[tap] for tap in (1, 4, 7, 2, 5, 8, 0, 3, 6)]
    for at, tap_ref in enumerate(stream(sources, buffer_ref, semaphores)):
        side, i = divmod(at - 4, 3)
        lanes = slice(side * width, (side + 1) * width)
        if at == 0:
            window = grads_ref[:, width:]
        elif at < 4:
            window = windows_ref[:, (at - 1) * width : at * width]
        elif i == 0:
            window = jnp.concatenate([up_near_ref[:, lanes], up_far_ref[:, lanes]])
        elif i == 1:
            window = (east_ref, west_ref)[side][...]
        else:
            window = jnp.concatenate([down_far_ref[:, lanes], down_near_ref[:, lanes]])
        add_product(total_ref, window, tap_ref, at == 0)
    out_ref[...] = total_ref[...].astype(out_ref.dtype)


def input_gradient(windows, grads, east, west, side_rows, kernel, point_weight):
    pixels = grads.shape[0]
    in_width, width = point_weight.shape
    return pl.pallas_call(
        input_gradient_kernel,
        out_shape=like((pixels, in_width), jnp.bfloat16),
        in_specs=[VMEM] * 8 + [ANY] * 2,
        out_specs=VMEM,
        scratch_shapes=[pltpu.VMEM((pixels, in_width), jnp.float32)]
        + stream_scratch(in_width, width),
        compiler_params=params(60),
        cost_estimate=cost(20 * pixels * in_width * width, 40 * in_width * width),
    )(windows, grads, east, west, *side_rows, kernel, point_weight)


def shards(features, kernel, point_weight, project_weight, upstream, labels, class_weights):
    rows, cols, in_width = features.shape
    width = point_weight.shape[1]
    pixels = rows * cols
    place = jnp.stack([lax.axis_index("c"), lax.axis_index(LAT)])
    near = ATROUS_DILATION // rows
    far_pixels = (ATROUS_DILATION - near * rows) * cols
    tiles_over = ATROUS_DILATION // cols
    span = ATROUS_DILATION * cols

    flat = features.reshape(pixels, in_width)
    slices = channel_slices(flat)
    below_near, below_far, above_near, above_far, level, point_pre = tap_products(
        flat, kernel, point_weight, far_pixels, slices
    )
    received = (
        shift_rows(below_near, -near),
        shift_rows(below_far, -(near + 1)),
        shift_rows(above_near, near),
        shift_rows(above_far, near + 1),
    )
    column_features = lax.all_to_all(slices, LAT, 0, 0).reshape(LAT_COUNT * pixels, -1)
    half = LAT_COUNT // 2 * pixels
    first_half, second_half = column_features[:half], column_features[half:]
    to_east, to_west, center, first_half = row_sum(level, received, first_half)
    first_east = shift_columns(first_half, -tiles_over)
    first_west = shift_columns(first_half, tiles_over)
    from_east = shift_columns(to_west, -tiles_over)
    from_west = shift_columns(to_east, tiles_over)
    class_index = jnp.arange(3, dtype=jnp.int32)
    pixel_weight = jnp.sum(
        jnp.where(labels[..., None] == class_index, class_weights, 0.0), axis=-1
    ).reshape(-1, 1)
    head_out, grads, message = head(
        point_pre,
        center,
        from_east,
        from_west,
        project_weight,
        upstream.reshape(pixels, width),
        pixel_weight,
        (first_east, first_west),
    )

    gathered = lax.all_to_all(message, LAT, 0, 0)
    second_east = shift_columns(second_half, -tiles_over)
    second_west = shift_columns(second_half, tiles_over)
    east_grad = shift_columns(grads[:, :width], tiles_over)
    west_grad = shift_columns(grads[:, :width], -tiles_over)

    kept, sent, windows, up_near, up_far, down_near, down_far = weight_terms(
        span,
        place,
        (column_features, first_east, first_west, second_east, second_west),
        gathered,
        (east_grad, west_grad),
    )
    side_rows = (
        shift_rows(up_near, -near),
        shift_rows(up_far, -(near + 1)),
        shift_rows(down_near, near),
        shift_rows(down_far, near + 1),
    )
    chunk = (10 * in_width + 2 * width) // (LAT_COUNT * LON_COUNT)
    chip_sum = pair_sum(kept, lax.ppermute(sent, "c", [(0, 1), (1, 0)]), chunk)
    pieces = lax.all_to_all(chip_sum, ("xl", "z"), 0, 0)

    weight_grads = interleave(lax.all_to_all(piece_sum(pieces, side_rows), LAT, 0, 0))
    summed_input = input_gradient(
        windows, grads, east_grad, west_grad, side_rows, kernel, point_weight
    )

    head_tile = head_out.reshape(rows, cols, width)
    grad_tile = summed_input.reshape(rows, cols, in_width)
    return (head_tile, grad_tile, weight_grads)


def solution(mesh):
    split = Mesh(mesh.devices.reshape(tuple(AXIS_SIZES.values())), tuple(AXIS_SIZES))
    tile = P(LAT, LON, None)
    return jax.shard_map(
        shards,
        mesh=split,
        in_specs=(tile, P(), P(), P(), tile, P(LAT, LON), P()),
        out_specs=(tile, tile, P(LON, None)),
        check_vma=False,
    )
```

time: 177 us -> 161 us (0.910)
  Pallas kernels: 35.4 us -> 21.5 us
  starting transfers between devices: 81.6 us -> 69.9 us
  local copies, waits for them, and re-layouts: 9.09 us -> 14.9 us
  waiting for transfers between devices: 48.4 us -> 50.6 us
    all_to_all x1, starting transfers between devices: 23.2 us -> 9.07 us  [shards(): pieces = lax.all_to_all(chip_sum, ('xl', 'z'), 0, 0)]
    pallas_call x5 -> x3, Pallas kernels: 25.1 us -> 11.9 us  [the longest x1 8.62 us: input_gradient(): pl.pallas_call(input_gradient_kernel, out_shape=like((pixels, in_width),...]
    all_to_all x1, waiting for transfers between devices: 0.01 us -> 12.1 us  [shards(): gathered = lax.all_to_all(message, LAT, 0, 0)]
    ppermute x8, waiting for transfers between devices: 33.6 us -> 26.1 us  [shift_columns(): lax.ppermute(value, LON, [(i, (i + by) % LON_COUNT) for i in range(LON_CO...]
    unnamed x42 -> x38, local copies, waits for them, and re-layouts: 6.64 us -> 12.5 us
    ppermute x8, waiting for transfers between devices: 9.62 us -> 5.57 us  [shift_rows(): return lax.ppermute(value, LAT, pairs)]
    all_to_all x1, waiting for transfers between devices: 0.01 us -> 3.7 us  [shards(): pieces = lax.all_to_all(chip_sum, ('xl', 'z'), 0, 0)]
    ppermute x8, starting transfers between devices: 10.2 us -> 13.1 us  [shift_columns(): lax.ppermute(value, LON, [(i, (i + by) % LON_COUNT) for i in range(LON_CO...]
  transfers between devices with their start and end apart: 21 -> 21, of which waited for: 9 -> 11; matrix products, arithmetic and copies ran while one was open for 2% -> 4% of each run, Pallas kernels for 10% -> 7%
where the time goes in v2:
time: 161 us; the launch traced here: 159 us
  starting transfers between devices  69.9 us (43%)
  waiting for transfers between devices  50.6 us (31%)
  Pallas kernels  21.5 us (13%)
  local copies, waits for them, and re-layouts  14.9 us (9%)
    ppermute x8, starting transfers between devices, shift_rows(): return lax.ppermute(value, LAT, pairs)  28.3 us
    ppermute x8, waiting for transfers between devices, shift_columns(): lax.ppermute(value, LON, [(i, (i + by) % LON_COUNT) for i in range(LON_CO...  26.1 us
    ppermute x8, starting transfers between devices, shift_columns(): lax.ppermute(value, LON, [(i, (i + by) % LON_COUNT) for i in range(LON_CO...  13.1 us
    unnamed x38, local copies, waits for them, and re-layouts  12.5 us
    all_to_all x1, waiting for transfers between devices, shards(): gathered = lax.all_to_all(message, LAT, 0, 0)  12.1 us
    all_to_all x1, starting transfers between devices, shards(): pieces = lax.all_to_all(chip_sum, ('xl', 'z'), 0, 0)  9.07 us
    all_to_all x1, starting transfers between devices, shards(): gathered = lax.all_to_all(message, LAT, 0, 0)  8.64 us
    pallas_call x1, Pallas kernels, input_gradient(): pl.pallas_call(input_gradient_kernel, out_shape=like((pixels, in_width),...  8.62 us
  transfers between devices with their start and end apart: 21, of which 11 were waited for; matrix products, arithmetic and copies ran while one was open for 4% of the time, Pallas kernels for 7%

profile of v2, /device:TPU:32, one launch (start us, length us, event | category | flops | bytes accessed | tf_op | source)
XLA Modules:
  0.0 159.3 jit_solution(13012162862442041847)
XLA Ops:
  0.6 1.6 copy.20
  2.4 1.8 %shard_map.94.after_ref = bf16[8,192,256]{2,1,0:T(8,128)(2,1)} custom-call(bf16[192,2048]{1,0:T(8,128)(2,1)S(1)} %reshape.27.flat_ref), custom_call_target="tpu_custom_call" | custom-call | flops 10000000000 | bytes 1572864 | tf_op jit(solution)/shard_map/pallas_call | solution.py:154
  4.2 7.1 %all-to-all-start = ((bf16[8,192,256]{2,1,0:T(8,128)(2,1)}), bf16[8,192,256]{2,1,0:T(8,128)(2,1)S(1)}, u32[]{:S(2)}, u32[]{:S(2)}) async-start(bf16[8,192,256]{2,1,0:T(8,128)(2,1)} %shard_map.94.after_ref), calls=%async_computation | async-start | bytes 1572864 | tf_op jit(solution)/shard_map/all_to_all | solution.py:527
  11.2 3.7 %copy-done = bf16[9,2048,256]{2,1,0:T(8,128)(2,1)S(1)} copy-done((bf16[9,2048,256]{2,1,0:T(8,128)(2,1)S(1)}, bf16[9,2048,256]{2,1,0:T(8,128)(2,1)}, u32[]{:S(2)}) %copy-start) | copy-done | bytes 9437208
  14.9 2.7 %shard_map.95 = (bf16[144,768]{1,0:T(8,128)(2,1)}, bf16[48,768]{1,0:T(8,128)(2,1)S(1)}, bf16[144,768]{1,0:T(8,128)(2,1)}, bf16[48,768]{1,0:T(8,128)(2,1)S(1)}, f...) custom-call(bf16[192,2048]{1,0:T(8,128)(2,1)S(1)} %reshape.27.flat_ref, bf16[9,2048,256]{2,1,0:T(8,128)(2,1)S(1)} %copy-done, ...), custom_call_target="tpu_custom_call" | custom-call | flops 2013265920 | bytes 10485760 | tf_op jit(solution)/shard_map/pallas_call | solution.py:124
  17.6 1.3 collective-permute-start.1
  18.9 7.0 %collective-permute-start.3 = (bf16[48,768]{1,0:T(8,128)(2,1)S(1)}, bf16[48,768]{1,0:T(8,128)(2,1)S(1)}, u32[]{:S(2)}, u32[]{:S(2)}) collective-permute-start(bf16[48,768]{1,0:T(8,128)(2,1)S(1)} %get-tuple-element.28), channel_id=1, source_target_pairs={{0,96},{32,128},{64,160},{96,192},{128,224},{1,97},{33,129},{65,16... | collective-permute-start | bytes 221192 | tf_op jit(solution)/shard_map/ppermute | solution.py:23
  25.8 1.3 collective-permute-start
  27.2 4.7 %collective-permute-start.2 = (bf16[144,768]{1,0:T(8,128)(2,1)}, bf16[144,768]{1,0:T(8,128)(2,1)S(1)}, u32[]{:S(2)}, u32[]{:S(2)}) collective-permute-start(bf16[144,768]{1,0:T(8,128)(2,1)} %get-tuple-element.27), channel_id=1, source_target_pairs={{0,64},{32,96},{64,128},{96,160},{128,192},{160,224},{1,65},{33,97... | collective-permute-start | bytes 663560 | tf_op jit(solution)/shard_map/ppermute | solution.py:23
  32.7 3.2 %collective-permute-done.below_near_ref = bf16[144,768]{1,0:T(8,128)(2,1)S(1)} collective-permute-done((bf16[144,768]{1,0:T(8,128)(2,1)}, bf16[144,768]{1,0:T(8,128)(2,1)S(1)}, u32[]{:S(2)}, u32[]{:S(2)}) %collective-permute-start) | collective-permute-done | bytes 221216 | tf_op jit(solution)/shard_map/ppermute | solution.py:23
  36.8 4.6 %collective-permute-start.6 = (bf16[768,256]{1,0:T(8,128)(2,1)S(1)}, bf16[768,256]{1,0:T(8,128)(2,1)S(1)}, u32[]{:S(2)}, u32[]{:S(2)}) collective-permute-start(bf16[768,256]{1,0:T(8,128)(2,1)S(1)} %get-tuple-element.32), channel_id=1, source_target_pairs={{0,29},{1,30},{2,31},{3,0},{4,1},{5,2},{6,3},{7,4},{8,5},{9,6},{10... | collective-permute-start | bytes 1179656 | tf_op jit(solution)/shard_map/ppermute | solution.py:27
  41.4 1.5 collective-permute-start.4
  45.0 13.2 %collective-permute-done.4.from_east_ref = bf16[192,256]{1,0:T(8,128)(2,1)S(1)} collective-permute-done((bf16[192,256]{1,0:T(8,128)(2,1)S(1)}, bf16[192,256]{1,0:T(8,128)(2,1)S(1)}, u32[]{:S(2)}, u32[]{:S(2)}) %collective-permute-start.4) | collective-permute-done | bytes 98336 | tf_op jit(solution)/shard_map/ppermute | solution.py:27
  58.9 1.3 copy-done.2
  60.2 8.6 %all-to-all-start.1 = ((bf16[8,448,256]{2,1,0:T(8,128)(2,1)}), bf16[8,448,256]{2,1,0:T(8,128)(2,1)S(1)}, u32[]{:S(2)}, u32[]{:S(2)}) async-start(bf16[8,448,256]{2,1,0:T(8,128)(2,1)} %copy-done.2), calls=%async_computation.1 | async-start | bytes 3670016 | tf_op jit(solution)/shard_map/all_to_all | solution.py:550
  69.4 4.2 %collective-permute-start.8 = (bf16[768,256]{1,0:T(8,128)(2,1)}, bf16[768,256]{1,0:T(8,128)(2,1)}, u32[]{:S(2)}, u32[]{:S(2)}) collective-permute-start(bf16[768,256]{1,0:T(8,128)(2,1)} %bitcast.8), channel_id=1, source_target_pairs={{0,29},{1,30},{2,31},{3,0},{4,1},{5,2},{6,3},{7,4},{8,5},{9,6},{10... | collective-permute-start | bytes 1179656 | tf_op jit(solution)/shard_map/ppermute | solution.py:27
  73.7 1.7 %collective-permute-start.10 = (bf16[192,256]{1,0:T(8,128)(2,1)S(1)}, bf16[192,256]{1,0:T(8,128)(2,1)S(1)}, u32[]{:S(2)}, u32[]{:S(2)}) collective-permute-start(bf16[192,256]{1,0:T(8,128)(2,1)S(1)} %slice.20), channel_id=1, source_target_pairs={{0,3},{1,4},{2,5},{3,6},{4,7},{5,8},{6,9},{7,10},{8,11},{9,12},{10... | collective-permute-start | bytes 294920 | tf_op jit(solution)/shard_map/ppermute | solution.py:27
  76.1 11.1 %collective-permute-done.9.west_second_ref = bf16[768,256]{1,0:T(8,128)(2,1)} collective-permute-done((bf16[768,256]{1,0:T(8,128)(2,1)}, bf16[768,256]{1,0:T(8,128)(2,1)}, u32[]{:S(2)}, u32[]{:S(2)}) %collective-permute-start.9) | collective-permute-done | bytes 393248 | tf_op jit(solution)/shard_map/ppermute | solution.py:27
  88.9 12.1 %all-to-all-done.1.message_ref = bf16[8,448,256]{2,1,0:T(8,128)(2,1)S(1)} async-done(((bf16[8,448,256]{2,1,0:T(8,128)(2,1)}), bf16[8,448,256]{2,1,0:T(8,128)(2,1)S(1)}, u32[]{:S(2)}, u32[]{:S(2)}) %all-to-all-start.1) | async-done | bytes 1835040 | tf_op jit(solution)/shard_map/all_to_all | solution.py:550
  102.8 4.7 %shard_map.98 = (f32[1408,256]{1,0:T(8,128)S(1)}, f32[1408,256]{1,0:T(8,128)S(1)}, bf16[192,768]{1,0:T(8,128)(2,1)S(1)}, bf16[144,512]{1,0:T(8,128)(2,1)S(1)}, b...) custom-call(s32[2]{0:T(128)S(1)} %copy-done.16, ...), custom_call_target="tpu_custom_call" | custom-call | flops 2013265920 | bytes 8388608 | tf_op jit(solution)/shard_map/pallas_call | solution.py:375
  109.0 3.1 %collective-permute-done.16.received_ref = f32[1408,256]{1,0:T(8,128)S(1)} collective-permute-done((f32[1408,256]{1,0:T(8,128)S(1)}, f32[1408,256]{1,0:T(8,128)S(1)}, u32[]{:S(2)}, u32[]{:S(2)}) %collective-permute-start.16) | collective-permute-done | bytes 1441824 | tf_op jit(solution)/shard_map/ppermute | solution.py:570
  113.1 9.1 %all-to-all-start.2 = ((bf16[16,82,256]{2,1,0:T(8,128)(2,1)}), bf16[16,82,256]{2,1,0:T(8,128)(2,1)S(1)}, u32[]{:S(2)}, u32[]{:S(2)}) async-start(bf16[16,82,256]{2,1,0:T(8,128)(2,1)} %shard_map.100), calls=%async_computation.2 | async-start | bytes 1441792 | tf_op jit(solution)/shard_map/all_to_all | solution.py:571
  122.2 1.3 collective-permute-start.12
  123.5 4.6 %collective-permute-start.14 = (bf16[144,512]{1,0:T(8,128)(2,1)S(1)}, bf16[144,512]{1,0:T(8,128)(2,1)S(1)}, u32[]{:S(2)}, u32[]{:S(2)}) collective-permute-start(bf16[144,512]{1,0:T(8,128)(2,1)S(1)} %get-tuple-element.39), channel_id=1, source_target_pairs={{0,64},{32,96},{64,128},{96,160},{128,192},{160,224},{1,65},{33,97... | collective-permute-start | bytes 442376 | tf_op jit(solution)/shard_map/ppermute | solution.py:23
  128.0 1.3 collective-permute-start.13
  129.3 7.0 %collective-permute-start.15 = (bf16[48,512]{1,0:T(8,128)(2,1)S(1)}, bf16[48,512]{1,0:T(8,128)(2,1)S(1)}, u32[]{:S(2)}, u32[]{:S(2)}) collective-permute-start(bf16[48,512]{1,0:T(8,128)(2,1)S(1)} %get-tuple-element.40), channel_id=1, source_target_pairs={{0,96},{32,128},{64,160},{96,192},{128,224},{1,97},{33,129},{65,16... | collective-permute-start | bytes 147464 | tf_op jit(solution)/shard_map/ppermute | solution.py:23
  136.6 1.4 collective-permute-done.15.down_far_ref.refs_3_
  138.0 3.7 %all-to-all-done.2.pieces_ref = bf16[16,82,256]{2,1,0:T(8,128)(2,1)S(1)} async-done(((bf16[16,82,256]{2,1,0:T(8,128)(2,1)}), bf16[16,82,256]{2,1,0:T(8,128)(2,1)S(1)}, u32[]{:S(2)}, u32[]{:S(2)}) %all-to-all-start.2) | async-done | bytes 671776 | tf_op jit(solution)/shard_map/all_to_all | solution.py:571
  142.7 3.5 %all-to-all-start.3 = ((f32[8,82,256]{2,1,0:T(8,128)}), f32[8,82,256]{2,1,0:T(8,128)S(1)}, u32[]{:S(2)}, u32[]{:S(2)}) async-start(f32[8,82,256]{2,1,0:T(8,128)} %shard_map.101), calls=%async_computation.3 | async-start | bytes 1441792 | tf_op jit(solution)/shard_map/all_to_all | solution.py:573
  147.0 8.6 %shard_map.99 = bf16[192,2048]{1,0:T(8,128)(2,1)} custom-call(bf16[192,768]{1,0:T(8,128)(2,1)} %copy-done.8, bf16[192,512]{1,0:T(8,128)(2,1)} %copy-done.5, bf16[192,256]{1,0:T(8,128)(2,1)} %copy-done.13, bf16[192,256]{1,0:T(8,128)(2,1)} %copy-done.12, bf16[144,512]{1,0:T(8,128)(2,1)} %copy-done.3, bf16[48,512]{1,0:T(8,128)(2,1)} %copy-done.10, ...), custom_call_target="tpu_custom_call" | custom-call | flops 2013265920 | bytes 20971520 | tf_op jit(solution)/shard_map/pallas_call | solution.py:494
  155.6 1.3 reshape.32
  156.9 1.3 copy.24
  (66 shorter events, 15.0 us)
Async XLA Ops:
  4.2 7.1 %copy-start.1 = (bf16[2048,256]{1,0:T(8,128)(2,1)S(1)}, bf16[2048,256]{1,0:T(8,128)(2,1)}, u32[]{:S(2)}) copy-start(bf16[2048,256]{1,0:T(8,128)(2,1)} %point_weight_ref.3) | copy-start | bytes 3145732
  4.2 27.7 %all-to-all-start = ((bf16[8,192,256]{2,1,0:T(8,128)(2,1)}), bf16[8,192,256]{2,1,0:T(8,128)(2,1)S(1)}, u32[]{:S(2)}, u32[]{:S(2)}) async-start(bf16[8,192,256]{2,1,0:T(8,128)(2,1)} %shard_map.94.after_ref), calls=%async_computation | async-start | bytes 1572864 | tf_op jit(solution)/shard_map/all_to_all | solution.py:527
  11.2 3.7 %copy-start = (bf16[9,2048,256]{2,1,0:T(8,128)(2,1)S(1)}, bf16[9,2048,256]{2,1,0:T(8,128)(2,1)}, u32[]{:S(2)}) copy-start(bf16[9,2048,256]{2,1,0:T(8,128)(2,1)} %kernel_ref.3) | copy-start | bytes 28311556
  17.6 15.1 %collective-permute-start.1 = (bf16[48,768]{1,0:T(8,128)(2,1)S(1)}, bf16[48,768]{1,0:T(8,128)(2,1)S(1)}, u32[]{:S(2)}, u32[]{:S(2)}) collective-permute-start(bf16[48,768]{1,0:T(8,128)(2,1)S(1)} %get-tuple-element.26), channel_id=1, source_target_pairs={{96,0},{128,32},{160,64},{192,96},{224,128},{97,1},{129,33},{161,6... | collective-permute-start | bytes 221192 | tf_op jit(solution)/shard_map/ppermute | solution.py:23
  18.9 13.8 %collective-permute-start.3 = (bf16[48,768]{1,0:T(8,128)(2,1)S(1)}, bf16[48,768]{1,0:T(8,128)(2,1)S(1)}, u32[]{:S(2)}, u32[]{:S(2)}) collective-permute-start(bf16[48,768]{1,0:T(8,128)(2,1)S(1)} %get-tuple-element.28), channel_id=1, source_target_pairs={{0,96},{32,128},{64,160},{96,192},{128,224},{1,97},{33,129},{65,16... | collective-permute-start | bytes 221192 | tf_op jit(solution)/shard_map/ppermute | solution.py:23
  25.8 10.0 %collective-permute-start = (bf16[144,768]{1,0:T(8,128)(2,1)}, bf16[144,768]{1,0:T(8,128)(2,1)S(1)}, u32[]{:S(2)}, u32[]{:S(2)}) collective-permute-start(bf16[144,768]{1,0:T(8,128)(2,1)} %get-tuple-element.25), channel_id=1, source_target_pairs={{64,0},{96,32},{128,64},{160,96},{192,128},{224,160},{65,1},{97,33... | collective-permute-start | bytes 663560 | tf_op jit(solution)/shard_map/ppermute | solution.py:23
  27.1 31.1 %copy-start.9 = (bf16[2,256,256]{2,1,0:T(8,128)(2,1)S(1)}, bf16[2,256,256]{2,1,0:T(8,128)(2,1)}, u32[]{:S(2)}) copy-start(bf16[2,256,256]{2,1,0:T(8,128)(2,1)} %project_ref.1) | copy-start | bytes 786436
  27.2 9.3 %collective-permute-start.2 = (bf16[144,768]{1,0:T(8,128)(2,1)}, bf16[144,768]{1,0:T(8,128)(2,1)S(1)}, u32[]{:S(2)}, u32[]{:S(2)}) collective-permute-start(bf16[144,768]{1,0:T(8,128)(2,1)} %get-tuple-element.27), channel_id=1, source_target_pairs={{0,64},{32,96},{64,128},{96,160},{128,192},{160,224},{1,65},{33,97... | collective-permute-start | bytes 663560 | tf_op jit(solution)/shard_map/ppermute | solution.py:23
  36.6 21.6 %collective-permute-start.7 = (bf16[768,256]{1,0:T(8,128)(2,1)S(1)}, bf16[768,256]{1,0:T(8,128)(2,1)S(1)}, u32[]{:S(2)}, u32[]{:S(2)}) collective-permute-start(bf16[768,256]{1,0:T(8,128)(2,1)S(1)} %get-tuple-element.32), channel_id=1, source_target_pairs={{0,3},{1,4},{2,5},{3,6},{4,7},{5,8},{6,9},{7,10},{8,11},{9,12},{10... | collective-permute-start | bytes 1179656 | tf_op jit(solution)/shard_map/ppermute | solution.py:27
  36.8 21.5 %collective-permute-start.6 = (bf16[768,256]{1,0:T(8,128)(2,1)S(1)}, bf16[768,256]{1,0:T(8,128)(2,1)S(1)}, u32[]{:S(2)}, u32[]{:S(2)}) collective-permute-start(bf16[768,256]{1,0:T(8,128)(2,1)S(1)} %get-tuple-element.32), channel_id=1, source_target_pairs={{0,29},{1,30},{2,31},{3,0},{4,1},{5,2},{6,3},{7,4},{8,5},{9,6},{10... | collective-permute-start | bytes 1179656 | tf_op jit(solution)/shard_map/ppermute | solution.py:27
  41.4 16.8 %collective-permute-start.4 = (bf16[192,256]{1,0:T(8,128)(2,1)S(1)}, bf16[192,256]{1,0:T(8,128)(2,1)S(1)}, u32[]{:S(2)}, u32[]{:S(2)}) collective-permute-start(bf16[192,256]{1,0:T(8,128)(2,1)S(1)} %get-tuple-element.30), channel_id=1, source_target_pairs={{0,29},{1,30},{2,31},{3,0},{4,1},{5,2},{6,3},{7,4},{8,5},{9,6},{10... | collective-permute-start | bytes 294920 | tf_op jit(solution)/shard_map/ppermute | solution.py:27
  42.9 15.3 %collective-permute-start.5 = (bf16[192,256]{1,0:T(8,128)(2,1)S(1)}, bf16[192,256]{1,0:T(8,128)(2,1)S(1)}, u32[]{:S(2)}, u32[]{:S(2)}) collective-permute-start(bf16[192,256]{1,0:T(8,128)(2,1)S(1)} %get-tuple-element.31), channel_id=1, source_target_pairs={{0,3},{1,4},{2,5},{3,6},{4,7},{5,8},{6,9},{7,10},{8,11},{9,12},{10... | collective-permute-start | bytes 294920 | tf_op jit(solution)/shard_map/ppermute | solution.py:27
  60.2 13.4 %copy-start.5 = (bf16[192,512]{1,0:T(8,128)(2,1)}, bf16[192,512]{1,0:T(8,128)(2,1)S(1)}, u32[]{:S(2)}) copy-start(bf16[192,512]{1,0:T(8,128)(2,1)S(1)} %get-tuple-element.35.grads_ref) | copy-start | bytes 589828
  60.2 40.9 %all-to-all-start.1 = ((bf16[8,448,256]{2,1,0:T(8,128)(2,1)}), bf16[8,448,256]{2,1,0:T(8,128)(2,1)S(1)}, u32[]{:S(2)}, u32[]{:S(2)}) async-start(bf16[8,448,256]{2,1,0:T(8,128)(2,1)} %copy-done.2), calls=%async_computation.1 | async-start | bytes 3670016 | tf_op jit(solution)/shard_map/all_to_all | solution.py:550
  68.8 18.4 %collective-permute-start.9 = (bf16[768,256]{1,0:T(8,128)(2,1)}, bf16[768,256]{1,0:T(8,128)(2,1)}, u32[]{:S(2)}, u32[]{:S(2)}) collective-permute-start(bf16[768,256]{1,0:T(8,128)(2,1)} %bitcast.7), channel_id=1, source_target_pairs={{0,3},{1,4},{2,5},{3,6},{4,7},{5,8},{6,9},{7,10},{8,11},{9,12},{10... | collective-permute-start | bytes 1179656 | tf_op jit(solution)/shard_map/ppermute | solution.py:27
  69.4 17.8 %collective-permute-start.8 = (bf16[768,256]{1,0:T(8,128)(2,1)}, bf16[768,256]{1,0:T(8,128)(2,1)}, u32[]{:S(2)}, u32[]{:S(2)}) collective-permute-start(bf16[768,256]{1,0:T(8,128)(2,1)} %bitcast.8), channel_id=1, source_target_pairs={{0,29},{1,30},{2,31},{3,0},{4,1},{5,2},{6,3},{7,4},{8,5},{9,6},{10... | collective-permute-start | bytes 1179656 | tf_op jit(solution)/shard_map/ppermute | solution.py:27
  73.6 14.4 %collective-permute-start.11 = (bf16[192,256]{1,0:T(8,128)(2,1)S(1)}, bf16[192,256]{1,0:T(8,128)(2,1)S(1)}, u32[]{:S(2)}, u32[]{:S(2)}) collective-permute-start(bf16[192,256]{1,0:T(8,128)(2,1)S(1)} %slice.20), channel_id=1, source_target_pairs={{0,29},{1,30},{2,31},{3,0},{4,1},{5,2},{6,3},{7,4},{8,5},{9,6},{10... | collective-permute-start | bytes 294920 | tf_op jit(solution)/shard_map/ppermute | solution.py:27
  73.7 15.2 %collective-permute-start.10 = (bf16[192,256]{1,0:T(8,128)(2,1)S(1)}, bf16[192,256]{1,0:T(8,128)(2,1)S(1)}, u32[]{:S(2)}, u32[]{:S(2)}) collective-permute-start(bf16[192,256]{1,0:T(8,128)(2,1)S(1)} %slice.20), channel_id=1, source_target_pairs={{0,3},{1,4},{2,5},{3,6},{4,7},{5,8},{6,9},{7,10},{8,11},{9,12},{10... | collective-permute-start | bytes 294920 | tf_op jit(solution)/shard_map/ppermute | solution.py:27
  88.0 19.5 %copy-start.12 = (bf16[192,256]{1,0:T(8,128)(2,1)}, bf16[192,256]{1,0:T(8,128)(2,1)S(1)}, u32[]{:S(2)}) copy-start(bf16[192,256]{1,0:T(8,128)(2,1)S(1)} %collective-permute-done.11.west_grad_ref.west_ref) | copy-start | bytes 294916
  88.9 18.5 %copy-start.13 = (bf16[192,256]{1,0:T(8,128)(2,1)}, bf16[192,256]{1,0:T(8,128)(2,1)S(1)}, u32[]{:S(2)}) copy-start(bf16[192,256]{1,0:T(8,128)(2,1)S(1)} %collective-permute-done.10.east_grad_ref.east_ref) | copy-start | bytes 294916
  108.9 3.2 %collective-permute-start.16 = (f32[1408,256]{1,0:T(8,128)S(1)}, f32[1408,256]{1,0:T(8,128)S(1)}, u32[]{:S(2)}, u32[]{:S(2)}) collective-permute-start(f32[1408,256]{1,0:T(8,128)S(1)} %get-tuple-element.42), channel_id=1, source_target_pairs={{0,1},{1,0},{2,3},{3,2},{4,5},{5,4},{6,7},{7,6},{8,9},{9,8},{10,11... | collective-permute-start | bytes 4325384 | tf_op jit(solution)/shard_map/ppermute | solution.py:570
  112.1 10.1 %copy-start.15 = (bf16[144,512]{1,0:T(8,128)(2,1)S(1)}, bf16[144,512]{1,0:T(8,128)(2,1)}, u32[]{:S(2)}) copy-start(bf16[144,512]{1,0:T(8,128)(2,1)} %copy-done.14) | copy-start | bytes 442372
  113.1 28.7 %all-to-all-start.2 = ((bf16[16,82,256]{2,1,0:T(8,128)(2,1)}), bf16[16,82,256]{2,1,0:T(8,128)(2,1)S(1)}, u32[]{:S(2)}, u32[]{:S(2)}) async-start(bf16[16,82,256]{2,1,0:T(8,128)(2,1)} %shard_map.100), calls=%async_computation.2 | async-start | bytes 1441792 | tf_op jit(solution)/shard_map/all_to_all | solution.py:571
  122.2 15.9 %collective-permute-start.12 = (bf16[144,512]{1,0:T(8,128)(2,1)S(1)}, bf16[144,512]{1,0:T(8,128)(2,1)S(1)}, u32[]{:S(2)}, u32[]{:S(2)}) collective-permute-start(bf16[144,512]{1,0:T(8,128)(2,1)S(1)} %copy-done.15), channel_id=1, source_target_pairs={{64,0},{96,32},{128,64},{160,96},{192,128},{224,160},{65,1},{97,33... | collective-permute-start | bytes 442376 | tf_op jit(solution)/shard_map/ppermute | solution.py:23
  123.5 14.6 %collective-permute-start.14 = (bf16[144,512]{1,0:T(8,128)(2,1)S(1)}, bf16[144,512]{1,0:T(8,128)(2,1)S(1)}, u32[]{:S(2)}, u32[]{:S(2)}) collective-permute-start(bf16[144,512]{1,0:T(8,128)(2,1)S(1)} %get-tuple-element.39), channel_id=1, source_target_pairs={{0,64},{32,96},{64,128},{96,160},{128,192},{160,224},{1,65},{33,97... | collective-permute-start | bytes 442376 | tf_op jit(solution)/shard_map/ppermute | solution.py:23
  128.0 8.6 %collective-permute-start.13 = (bf16[48,512]{1,0:T(8,128)(2,1)S(1)}, bf16[48,512]{1,0:T(8,128)(2,1)S(1)}, u32[]{:S(2)}, u32[]{:S(2)}) collective-permute-start(bf16[48,512]{1,0:T(8,128)(2,1)S(1)} %get-tuple-element.38), channel_id=1, source_target_pairs={{96,0},{128,32},{160,64},{192,96},{224,128},{97,1},{129,33},{161,6... | collective-permute-start | bytes 147464 | tf_op jit(solution)/shard_map/ppermute | solution.py:23
  129.3 8.7 %collective-permute-start.15 = (bf16[48,512]{1,0:T(8,128)(2,1)S(1)}, bf16[48,512]{1,0:T(8,128)(2,1)S(1)}, u32[]{:S(2)}, u32[]{:S(2)}) collective-permute-start(bf16[48,512]{1,0:T(8,128)(2,1)S(1)} %get-tuple-element.40), channel_id=1, source_target_pairs={{0,96},{32,128},{64,160},{96,192},{128,224},{1,97},{33,129},{65,16... | collective-permute-start | bytes 147464 | tf_op jit(solution)/shard_map/ppermute | solution.py:23
  136.6 10.4 %copy-start.10 = (bf16[48,512]{1,0:T(8,128)(2,1)}, bf16[48,512]{1,0:T(8,128)(2,1)S(1)}, u32[]{:S(2)}) copy-start(bf16[48,512]{1,0:T(8,128)(2,1)S(1)} %collective-permute-done.13.up_far_ref.refs_1_) | copy-start | bytes 147460
  138.0 9.0 %copy-start.11 = (bf16[48,512]{1,0:T(8,128)(2,1)}, bf16[48,512]{1,0:T(8,128)(2,1)S(1)}, u32[]{:S(2)}) copy-start(bf16[48,512]{1,0:T(8,128)(2,1)S(1)} %collective-permute-done.15.down_far_ref.refs_3_) | copy-start | bytes 147460
  138.0 9.0 %copy-start.3 = (bf16[144,512]{1,0:T(8,128)(2,1)}, bf16[144,512]{1,0:T(8,128)(2,1)S(1)}, u32[]{:S(2)}) copy-start(bf16[144,512]{1,0:T(8,128)(2,1)S(1)} %collective-permute-done.12.up_near_ref.refs_0_) | copy-start | bytes 442372
  138.0 8.9 %copy-start.4 = (bf16[144,512]{1,0:T(8,128)(2,1)}, bf16[144,512]{1,0:T(8,128)(2,1)S(1)}, u32[]{:S(2)}) copy-start(bf16[144,512]{1,0:T(8,128)(2,1)S(1)} %collective-permute-done.14.down_near_ref.refs_2_) | copy-start | bytes 442372
  142.7 15.5 %all-to-all-start.3 = ((f32[8,82,256]{2,1,0:T(8,128)}), f32[8,82,256]{2,1,0:T(8,128)S(1)}, u32[]{:S(2)}, u32[]{:S(2)}) async-start(f32[8,82,256]{2,1,0:T(8,128)} %shard_map.101), calls=%async_computation.3 | async-start | bytes 1441792 | tf_op jit(solution)/shard_map/all_to_all | solution.py:573
  (6 other events, 6.3 us)

commit v3 on v2

--- a/solution.py
+++ b/solution.py
@@ -13,6 +13,7 @@
 AXIS_SIZES = {"y": 4, "xh": 2, "xl": 2, "z": 8, "c": 2}
 LAT_COUNT = 8
 LON_COUNT = 32
+FIRST_BANDS = 4
 VMEM = pl.BlockSpec(memory_space=pltpu.VMEM)
 SMEM = pl.BlockSpec(memory_space=pltpu.SMEM)
 ANY = pl.BlockSpec(memory_space=pl.ANY)
@@ -132,7 +133,15 @@
     )(flat, kernel, point_weight, after)
 
 
-def slices_kernel(flat_ref, slices_ref):
+def slices_kernel(columns_ref, flat_ref, slices_ref, *row_refs):
+    cols, rows, _ = columns_ref.shape
+    for block, row_ref in enumerate(row_refs):
+        lanes = slice(128 * block, 128 * block + 128)
+        for col in range(cols):
+            row_ref[pl.ds(col, rows, stride=cols), :] = columns_ref[col, :, lanes].astype(
+                jnp.float32
+            )
+        flat_ref[:, lanes] = row_ref[...].astype(jnp.bfloat16)
     count, _, size = slices_ref.shape
     part = size // count
     source = lax.broadcasted_iota(jnp.int32, (size, size), 0)
@@ -149,16 +158,21 @@
         )
 
 
-def channel_slices(flat):
-    pixels, in_width = flat.shape
+def channel_slices(features):
+    rows, cols, in_width = features.shape
+    pixels = rows * cols
     return pl.pallas_call(
         slices_kernel,
-        out_shape=like((LAT_COUNT, pixels, in_width // LAT_COUNT), jnp.bfloat16),
+        out_shape=(
+            like((pixels, in_width), jnp.bfloat16),
+            like((LAT_COUNT, pixels, in_width // LAT_COUNT), jnp.bfloat16),
+        ),
         in_specs=[VMEM],
-        out_specs=VMEM,
+        out_specs=(VMEM,) * 2,
+        scratch_shapes=[pltpu.VMEM((pixels, 128), jnp.float32)] * (in_width // 128),
         compiler_params=params(),
-        cost_estimate=cost(10**10, 4 * pixels * in_width),
-    )(flat)
+        cost_estimate=cost(2 * pixels * in_width * in_width // LAT_COUNT, 6 * pixels * in_width),
+    )(jnp.swapaxes(features, 0, 1))
 
 
 def row_sum_kernel(
@@ -167,11 +181,9 @@
     below_far_ref,
     above_near_ref,
     above_far_ref,
-    features_in_ref,
     west_ref,
     east_ref,
     center_ref,
-    features_out_ref,
 ):
     width = center_ref.shape[1]
     near, far = below_near_ref.shape[0], below_far_ref.shape[0]
@@ -184,7 +196,7 @@
     east_ref[...] = total[:, 2 * width :].astype(jnp.bfloat16)
 
 
-def row_sum(level, received, features):
+def row_sum(level, received):
     pixels, wide = level.shape
     side = like((pixels, wide // 3), jnp.bfloat16)
     return pl.pallas_call(
@@ -193,17 +205,16 @@
             side,
             side,
             like((pixels, wide // 3), jnp.float32),
-            like(features.shape, features.dtype),
         ),
-        in_specs=[VMEM] * 5 + [ANY],
-        out_specs=(VMEM,) * 3 + (ANY,),
-        input_output_aliases={5: 3},
+        in_specs=[VMEM] * 5,
+        out_specs=(VMEM,) * 3,
         compiler_params=params(),
         cost_estimate=cost(3 * pixels * wide, 8 * pixels * wide),
-    )(level, *received, features)
+    )(level, *received)
 
 
 def head_kernel(
+    place_ref,
     point_ref,
     center_ref,
     from_east_ref,
@@ -211,15 +222,15 @@
     project_ref,
     upstream_ref,
     pixel_weight_ref,
-    after_east_ref,
-    after_west_ref,
     head_ref,
     grads_ref,
     message_ref,
+    mine_ref,
     *terms_refs,
 ):
     bf16, f32 = jnp.bfloat16, jnp.float32
     width = point_ref.shape[1]
+    xh = place_ref[2]
     pre_list = [
         point_ref[...],
         center_ref[...] + from_east_ref[...].astype(f32) + from_west_ref[...].astype(f32),
@@ -241,50 +252,97 @@
     pixels = grads_ref.shape[0]
     grads_ref[:, :width] = grads[1]
     grads_ref[:, width:] = grads[0]
+    message_ref[:pixels, :width] = grads[1]
+    message_ref[:pixels, width:] = grads[0]
     for k in range(2):
         terms = contract_row_axes(acts[k], out_grad)
         for half, terms_ref in enumerate(terms_refs):
             terms_ref[width * k : width * (k + 1), :] = terms[:, 128 * half : 128 * half + 128]
-    count = message_ref.shape[0]
-    part = 2 * width // count
-    for a in range(count):
-        message_ref[a, :pixels, :] = grads[1]
-        message_ref[a, pixels : 2 * pixels, :] = grads[0]
+    count, part, _ = mine_ref.shape
+    for y in range(count):
+        rows = slice(pixels + y % 2 * part, pixels + y % 2 * part + part)
         for half, terms_ref in enumerate(terms_refs):
-            message_ref[a, 2 * pixels :, 128 * half : 128 * half + 128] = terms_ref[
-                pl.ds(a, part, stride=count), :
-            ].astype(bf16)
-
-
-def head(point_pre, center, from_east, from_west, project, upstream, pixel_weight, after):
+            even = terms_ref[pl.ds(2 * y, part, stride=2 * count), :]
+            odd = terms_ref[pl.ds(2 * y + 1, part, stride=2 * count), :]
+            lanes = slice(128 * half, 128 * half + 128)
+            mine_ref[y, :, lanes] = jnp.where(xh == 0, even, odd)
+            low = y // 2 * width + 128 * half
+            message_ref[rows, low : low + 128] = jnp.where(xh == 0, odd, even).astype(bf16)
+
+
+def head(place, point_pre, center, from_east, from_west, project, upstream, pixel_weight):
     pixels, width = point_pre.shape
-    part = 2 * width // LAT_COUNT
+    count = AXIS_SIZES["y"]
+    part = width // count
     bf16, f32 = jnp.bfloat16, jnp.float32
     return pl.pallas_call(
         head_kernel,
         out_shape=(
             like((pixels, width), bf16),
             like((pixels, 2 * width), bf16),
-            like((LAT_COUNT, 2 * pixels + part, width), bf16),
+            like((pixels + 2 * part, 2 * width), bf16),
+            like((count, part, width), f32),
         ),
-        in_specs=[VMEM] * 7 + [ANY] * 2,
-        out_specs=(VMEM,) * 3,
+        in_specs=[SMEM] + [VMEM] * 7,
+        out_specs=(VMEM,) * 4,
         scratch_shapes=[pltpu.VMEM((2 * width, 128), f32)] * (width // 128),
         compiler_params=params(),
         cost_estimate=cost(12 * pixels * width * width, 24 * pixels * width),
-    )(point_pre, center, from_east, from_west, project, upstream, pixel_weight, *after)
+    )(place, point_pre, center, from_east, from_west, project, upstream, pixel_weight)
+
+
+def forward_kernel(
+    grads_ref,
+    received_ref,
+    mine_ref,
+    after_east_ref,
+    after_west_ref,
+    features_in_ref,
+    message_ref,
+    features_out_ref,
+):
+    count, part, width = mine_ref.shape
+    pixels = grads_ref.shape[0]
+    for at in range(count):
+        for slot, piece_ref in enumerate((grads_ref, received_ref)):
+            for k in (0, 1):
+                first = (2 * slot + k) * pixels
+                message_ref[at, first : first + pixels, :] = piece_ref[
+                    :pixels, k * width : (k + 1) * width
+                ]
+        rows = slice(pixels + at % 2 * part, pixels + at % 2 * part + part)
+        low = at // 2 * width
+        terms = mine_ref[at] + received_ref[rows, low : low + width].astype(jnp.float32)
+        message_ref[at, 4 * pixels :, :] = terms.astype(jnp.bfloat16)
+
+
+def forward(grads, received, mine, after, features):
+    count, part, width = mine.shape
+    pixels = grads.shape[0]
+    return pl.pallas_call(
+        forward_kernel,
+        out_shape=(
+            like((count, 4 * pixels + part, width), jnp.bfloat16),
+            like(features.shape, features.dtype),
+        ),
+        in_specs=[VMEM] * 3 + [ANY] * 3,
+        out_specs=(VMEM, ANY),
+        input_output_aliases={5: 1},
+        compiler_params=params(),
+        cost_estimate=cost(mine.size, 8 * received.size),
+    )(grads, received, mine, *after, features)
 
 
 def weight_terms_kernel(
     span,
     chunk,
     place_ref,
-    center_ref,
+    center_in_ref,
     east_first_ref,
+    east_second_ref,
     west_first_ref,
-    east_second_ref,
     west_second_ref,
-    message_ref,
+    message_in_ref,
     east_grad_ref,
     west_grad_ref,
     kept_ref,
@@ -295,28 +353,61 @@
     down_near_ref,
     down_far_ref,
     framed_ref,
+    features_ref,
+    message_ref,
+    semaphores,
 ):
-    total, width = center_ref.shape
+    _, total, width = features_ref.shape
+    first_rows = east_first_ref.shape[0]
+    message_copy = pltpu.make_async_copy(message_in_ref, message_ref, semaphores.at[0])
+    copies = {
+        0: [pltpu.make_async_copy(center_in_ref, features_ref.at[0], semaphores.at[1])],
+        1: [
+            pltpu.make_async_copy(
+                east_first_ref, features_ref.at[1, pl.ds(0, first_rows)], semaphores.at[2]
+            ),
+            pltpu.make_async_copy(
+                east_second_ref,
+                features_ref.at[1, pl.ds(first_rows, total - first_rows)],
+                semaphores.at[3],
+            ),
+        ],
+        -1: [
+            pltpu.make_async_copy(
+                west_first_ref, features_ref.at[2, pl.ds(0, first_rows)], semaphores.at[4]
+            ),
+            pltpu.make_async_copy(
+                west_second_ref,
+                features_ref.at[2, pl.ds(first_rows, total - first_rows)],
+                semaphores.at[5],
+            ),
+        ],
+    }
+    message_copy.start()
+    for j in (0, 1, -1):
+        for copy in copies[j]:
+            copy.start()
     pixels = total // LAT_COUNT
     room = padded(chunk)
-    core, lat = place_ref[0], place_ref[1]
+    core, y, xh = place_ref[0], place_ref[1], place_ref[2]
     far = up_far_ref.shape[0]
-    columns = {
-        0: (center_ref,),
-        1: (east_first_ref, east_second_ref),
-        -1: (west_first_ref, west_second_ref),
-    }
 
     edge = jnp.zeros((span, width), framed_ref.dtype)
     framed_ref[total : total + span, :width] = edge
     framed_ref[span : 2 * span, 2 * width : 3 * width] = edge
-    for band in range(LAT_COUNT):
-        piece = message_ref[band, :pixels, :]
-        for i in (-1, 0, 1):
-            first = span + span * i + band * pixels
-            framed_ref[first : first + pixels, (i + 1) * width : (i + 2) * width] = piece
-        first = span + band * pixels
-        framed_ref[first : first + pixels, 3 * width :] = message_ref[band, pixels : 2 * pixels, :]
+    message_copy.wait()
+    for at in range(message_ref.shape[0]):
+        for slot in (0, 1):
+            band = 2 * at + (xh + slot) % 2
+            low = 2 * slot * pixels
+            piece = message_ref[at, low : low + pixels, :]
+            for i in (-1, 0, 1):
+                first = pl.multiple_of(span + span * i + band * pixels, 16)
+                framed_ref[pl.ds(first, pixels), (i + 1) * width : (i + 2) * width] = piece
+            first = pl.multiple_of(span + band * pixels, 16)
+            framed_ref[pl.ds(first, pixels), 3 * width :] = message_ref[
+                at, low + pixels : low + 2 * pixels, :
+            ]
     for at, side_ref in enumerate((east_grad_ref, west_grad_ref)):
         lanes = slice(at * width, (at + 1) * width)
         side = side_ref[...]
@@ -324,7 +415,7 @@
         up_far_ref[:, lanes] = side[:far]
         down_near_ref[:, lanes] = side[: pixels - far]
         down_far_ref[:, lanes] = side[pixels - far :]
-    own_rows = pl.ds(pl.multiple_of(span + lat * pixels, 16), pixels)
+    own_rows = pl.ds(pl.multiple_of(span + (2 * y + xh) * pixels, 16), pixels)
     windows_ref[...] = framed_ref[own_rows, : 3 * width]
 
     def store(first, value):
@@ -347,15 +438,13 @@
 
     for j in (0, 1, -1):
         wide = 4 * width if j == 0 else 3 * width
-        product, low = 0.0, span
-        for part_ref in columns[j]:
-            high = low + part_ref.shape[0]
-            product += contract_row_axes(part_ref[...], framed_ref[low:high, :wide])
-            low = high
+        for copy in copies[j]:
+            copy.wait()
+        product = contract_row_axes(features_ref[j % 3], framed_ref[span : span + total, :wide])
         for i in (-1, 0, 1):
             store((3 * (i + 1) + j + 1) * width, product[:, (i + 1) * width : (i + 2) * width])
         if j == 0:
-            project_rows = jnp.sum(message_ref[:, 2 * pixels :, :].astype(jnp.float32), axis=0)
+            project_rows = jnp.sum(message_ref[:, 4 * pixels :, :].astype(jnp.float32), axis=0)
             store(9 * width, project_rows)
             store(9 * width + project_rows.shape[0], product[:, 3 * width :])
 
@@ -368,7 +457,7 @@
     total, width = features[0].shape
     pixels = total // LAT_COUNT
     far = span % pixels
-    chunk = (10 * width + message.shape[1] - 2 * pixels) // LON_COUNT
+    chunk = (10 * width + message.shape[1] - 4 * pixels) // LON_COUNT
     out = like((LON_COUNT // 2 * padded(chunk), width), jnp.float32)
     near_shape = like((pixels - far, 2 * width), jnp.bfloat16)
     far_shape = like((far, 2 * width), jnp.bfloat16)
@@ -376,10 +465,15 @@
         functools.partial(weight_terms_kernel, span, chunk),
         out_shape=(out, out, like((pixels, 3 * width), jnp.bfloat16))
         + (near_shape, far_shape, near_shape, far_shape),
-        in_specs=[SMEM] + [VMEM] * 8,
+        in_specs=[SMEM] + [ANY] * 6 + [VMEM] * 2,
         out_specs=(VMEM,) * 7,
-        scratch_shapes=[pltpu.VMEM((2 * span + total, 4 * width), jnp.bfloat16)],
-        compiler_params=params(),
+        scratch_shapes=[
+            pltpu.VMEM((2 * span + total, 4 * width), jnp.bfloat16),
+            pltpu.VMEM((3, total, width), jnp.bfloat16),
+            pltpu.VMEM(message.shape, jnp.bfloat16),
+            pltpu.SemaphoreType.DMA((6,)),
+        ],
+        compiler_params=params(60),
         cost_estimate=cost(20 * total * width * width, 8 * 2**20),
     )(place, *features, message, *sides)
 
@@ -393,11 +487,15 @@
 
 
 def pair_sum(kept, received, chunk):
+    width = kept.shape[1]
+    steps, count = 4, LON_COUNT // 2
+    block = pl.BlockSpec((kept.shape[0] // steps, width), lambda s: (s, 0))
     return pl.pallas_call(
         pair_sum_kernel,
-        out_shape=like((LON_COUNT // 2, chunk, kept.shape[1]), jnp.bfloat16),
-        in_specs=[VMEM] * 2,
-        out_specs=VMEM,
+        grid=(steps,),
+        out_shape=like((count, chunk, width), jnp.bfloat16),
+        in_specs=[block, block],
+        out_specs=pl.BlockSpec((count // steps, chunk, width), lambda s: (s, 0, 0)),
         compiler_params=params(),
         cost_estimate=cost(kept.size, 10 * kept.size),
     )(kept, received)
@@ -468,8 +566,10 @@
     total_ref,
     buffer_ref,
     semaphores,
+    *row_refs,
 ):
     width = buffer_ref.shape[2]
+    cols, rows, _ = out_ref.shape
     sources = [point_weight_ref] + [kernel_ref.at[tap] for tap in (1, 4, 7, 2, 5, 8, 0, 3, 6)]
     for at, tap_ref in enumerate(stream(sources, buffer_ref, semaphores)):
         side, i = divmod(at - 4, 3)
@@ -485,19 +585,24 @@
         else:
             window = jnp.concatenate([down_far_ref[:, lanes], down_near_ref[:, lanes]])
         add_product(total_ref, window, tap_ref, at == 0)
-    out_ref[...] = total_ref[...].astype(out_ref.dtype)
-
-
-def input_gradient(windows, grads, east, west, side_rows, kernel, point_weight):
+    for block, row_ref in enumerate(row_refs):
+        lanes = slice(128 * block, 128 * block + 128)
+        row_ref[...] = total_ref[:, lanes]
+        for col in range(cols):
+            out_ref[col, :, lanes] = row_ref[pl.ds(col, rows, stride=cols), :].astype(out_ref.dtype)
+
+
+def input_gradient(rows, windows, grads, east, west, side_rows, kernel, point_weight):
     pixels = grads.shape[0]
     in_width, width = point_weight.shape
     return pl.pallas_call(
         input_gradient_kernel,
-        out_shape=like((pixels, in_width), jnp.bfloat16),
+        out_shape=like((pixels // rows, rows, in_width), jnp.bfloat16),
         in_specs=[VMEM] * 8 + [ANY] * 2,
         out_specs=VMEM,
         scratch_shapes=[pltpu.VMEM((pixels, in_width), jnp.float32)]
-        + stream_scratch(in_width, width),
+        + stream_scratch(in_width, width)
+        + [pltpu.VMEM((pixels, 128), jnp.float32)] * (in_width // 128),
         compiler_params=params(60),
         cost_estimate=cost(20 * pixels * in_width * width, 40 * in_width * width),
     )(windows, grads, east, west, *side_rows, kernel, point_weight)
@@ -507,14 +612,13 @@
     rows, cols, in_width = features.shape
     width = point_weight.shape[1]
     pixels = rows * cols
-    place = jnp.stack([lax.axis_index("c"), lax.axis_index(LAT)])
+    place = jnp.stack([lax.axis_index("c"), lax.axis_index("y"), lax.axis_index("xh")])
     near = ATROUS_DILATION // rows
     far_pixels = (ATROUS_DILATION - near * rows) * cols
     tiles_over = ATROUS_DILATION // cols
     span = ATROUS_DILATION * cols
 
-    flat = features.reshape(pixels, in_width)
-    slices = channel_slices(flat)
+    flat, slices = channel_slices(features)
     below_near, below_far, above_near, above_far, level, point_pre = tap_products(
         flat, kernel, point_weight, far_pixels, slices
     )
@@ -525,18 +629,17 @@
         shift_rows(above_far, near + 1),
     )
     column_features = lax.all_to_all(slices, LAT, 0, 0).reshape(LAT_COUNT * pixels, -1)
-    half = LAT_COUNT // 2 * pixels
-    first_half, second_half = column_features[:half], column_features[half:]
-    to_east, to_west, center, first_half = row_sum(level, received, first_half)
-    first_east = shift_columns(first_half, -tiles_over)
-    first_west = shift_columns(first_half, tiles_over)
+    first_rows = FIRST_BANDS * pixels
+    first_features, second_features = column_features[:first_rows], column_features[first_rows:]
+    to_east, to_west, center = row_sum(level, received)
     from_east = shift_columns(to_west, -tiles_over)
     from_west = shift_columns(to_east, tiles_over)
     class_index = jnp.arange(3, dtype=jnp.int32)
     pixel_weight = jnp.sum(
         jnp.where(labels[..., None] == class_index, class_weights, 0.0), axis=-1
     ).reshape(-1, 1)
-    head_out, grads, message = head(
+    head_out, grads, message, mine = head(
+        place,
         point_pre,
         center,
         from_east,
@@ -544,19 +647,24 @@
         project_weight,
         upstream.reshape(pixels, width),
         pixel_weight,
-        (first_east, first_west),
-    )
-
-    gathered = lax.all_to_all(message, LAT, 0, 0)
-    second_east = shift_columns(second_half, -tiles_over)
-    second_west = shift_columns(second_half, tiles_over)
+    )
+
+    other = lax.ppermute(message, "xh", [(0, 1), (1, 0)])
+    first_east = shift_columns(first_features, -tiles_over)
+    first_west = shift_columns(first_features, tiles_over)
+    message, second_features = forward(
+        grads, other, mine, (first_east, first_west), second_features
+    )
+    gathered = lax.all_to_all(message, "y", 0, 0)
+    second_east = shift_columns(second_features, -tiles_over)
+    second_west = shift_columns(second_features, tiles_over)
     east_grad = shift_columns(grads[:, :width], tiles_over)
     west_grad = shift_columns(grads[:, :width], -tiles_over)
 
     kept, sent, windows, up_near, up_far, down_near, down_far = weight_terms(
         span,
         place,
-        (column_features, first_east, first_west, second_east, second_west),
+        (column_features, first_east, second_east, first_west, second_west),
         gathered,
         (east_grad, west_grad),
     )
@@ -571,12 +679,12 @@
     pieces = lax.all_to_all(chip_sum, ("xl", "z"), 0, 0)
 
     weight_grads = interleave(lax.all_to_all(piece_sum(pieces, side_rows), LAT, 0, 0))
-    summed_input = input_gradient(
-        windows, grads, east_grad, west_grad, side_rows, kernel, point_weight
+    input_grad = input_gradient(
+        rows, windows, grads, east_grad, west_grad, side_rows, kernel, point_weight
     )
 
     head_tile = head_out.reshape(rows, cols, width)
-    grad_tile = summed_input.reshape(rows, cols, in_width)
+    grad_tile = jnp.swapaxes(input_grad, 0, 1)
     return (head_tile, grad_tile, weight_grads)
 
 

time: 161 us -> 158 us (0.981)
  waiting for transfers between devices: 50.6 us -> 36.4 us
  starting transfers between devices: 69.9 us -> 80.7 us
  Pallas kernels: 21.5 us -> 27.1 us
  local copies, waits for them, and re-layouts: 14.9 us -> 11.2 us
    all_to_all x1, waiting for transfers between devices: 12.1 us -> 0.01 us  [shards(): gathered = lax.all_to_all(message, 'y', 0, 0)]
    ppermute x8, waiting for transfers between devices: 26.1 us -> 14.9 us  [shift_columns(): lax.ppermute(value, LON, [(i, (i + by) % LON_COUNT) for i in range(LON_CO...]
    ppermute x0 -> x1, waiting for transfers between devices: none -> 9.31 us  [shards(): other = lax.ppermute(message, 'xh', [(0, 1), (1, 0)])]
    ppermute x0 -> x1, starting transfers between devices: none -> 5.21 us  [shards(): other = lax.ppermute(message, 'xh', [(0, 1), (1, 0)])]
    all_to_all x1, starting transfers between devices: 3.54 us -> 7.75 us  [shards(): lax.all_to_all(piece_sum(pieces, side_rows), LAT, 0, 0)]
    pallas_call x1, Pallas kernels: 4.7 us -> 8.03 us  [weight_terms(): pl.pallas_call(functools.partial(weight_terms_kernel, span, chunk), out_s...]
    unnamed x38 -> x48, local copies, waits for them, and re-layouts: 12.5 us -> 9.89 us
    pallas_call x3 -> x4, Pallas kernels: 11.4 us -> 13.6 us  [the longest x1 8.65 us: input_gradient(): pl.pallas_call(input_gradient_kernel, out_shape=like((pixels // rows, row...]
  transfers between devices with their start and end apart: 21 -> 22, of which waited for: 11 -> 10; matrix products, arithmetic and copies ran while one was open for 4% -> 2% of each run, Pallas kernels for 7% -> 8%
where the time goes in v3:
time: 158 us; the launch traced here: 156 us
  starting transfers between devices  80.7 us (51%)
  waiting for transfers between devices  36.4 us (23%)
  Pallas kernels  27.1 us (17%)
  local copies, waits for them, and re-layouts  11.2 us (7%)
    ppermute x8, starting transfers between devices, shift_rows(): return lax.ppermute(value, LAT, pairs)  28.9 us
    ppermute x8, starting transfers between devices, shift_columns(): lax.ppermute(value, LON, [(i, (i + by) % LON_COUNT) for i in range(LON_CO...  15.1 us
    ppermute x8, waiting for transfers between devices, shift_columns(): lax.ppermute(value, LON, [(i, (i + by) % LON_COUNT) for i in range(LON_CO...  14.9 us
    unnamed x48, local copies, waits for them, and re-layouts  9.89 us
    ppermute x1, waiting for transfers between devices, shards(): other = lax.ppermute(message, 'xh', [(0, 1), (1, 0)])  9.31 us
    all_to_all x1, starting transfers between devices, shards(): pieces = lax.all_to_all(chip_sum, ('xl', 'z'), 0, 0)  9.11 us
    pallas_call x1, Pallas kernels, input_gradient(): pl.pallas_call(input_gradient_kernel, out_shape=like((pixels // rows, row...  8.65 us
    pallas_call x1, Pallas kernels, weight_terms(): pl.pallas_call(functools.partial(weight_terms_kernel, span, chunk), out_s...  8.03 us
  transfers between devices with their start and end apart: 22, of which 10 were waited for; matrix products, arithmetic and copies ran while one was open for 2% of the time, Pallas kernels for 8%

profile of v3, /device:TPU:32, one launch (start us, length us, event | category | flops | bytes accessed | tf_op | source)
XLA Modules:
  0.0 156.5 jit_solution(8535765542421045928)
XLA Ops:
  1.9 1.9 %shard_map.94 = (bf16[192,2048]{1,0:T(8,128)(2,1)S(1)}, bf16[8,192,256]{2,1,0:T(8,128)(2,1)}) custom-call(bf16[12,16,2048]{2,1,0:T(8,128)(2,1)S(1)} %bitcast.9), custom_call_target="tpu_custom_call" | custom-call | flops 201326592 | bytes 2359296 | tf_op jit(solution)/shard_map/pallas_call | solution.py:164
  3.8 6.9 %all-to-all-start = ((bf16[8,192,256]{2,1,0:T(8,128)(2,1)}), bf16[8,192,256]{2,1,0:T(8,128)(2,1)}, u32[]{:S(2)}, u32[]{:S(2)}) async-start(bf16[8,192,256]{2,1,0:T(8,128)(2,1)} %get-tuple-element.28.after_ref), calls=%async_computation | async-start | bytes 1572864 | tf_op jit(solution)/shard_map/all_to_all | solution.py:631
  10.7 3.7 %copy-done = bf16[9,2048,256]{2,1,0:T(8,128)(2,1)S(1)} copy-done((bf16[9,2048,256]{2,1,0:T(8,128)(2,1)S(1)}, bf16[9,2048,256]{2,1,0:T(8,128)(2,1)}, u32[]{:S(2)}) %copy-start) | copy-done | bytes 9437208
  14.4 2.2 %shard_map.95 = (bf16[144,768]{1,0:T(8,128)(2,1)S(1)}, bf16[48,768]{1,0:T(8,128)(2,1)S(1)}, bf16[144,768]{1,0:T(8,128)(2,1)S(1)}, bf16[48,768]{1,0:T(8,128)(2,1)...) custom-call(bf16[192,2048]{1,0:T(8,128)(2,1)S(1)} %get-tuple-element.27.flat_ref, ...), custom_call_target="tpu_custom_call" | custom-call | flops 2013265920 | bytes 10485760 | tf_op jit(solution)/shard_map/pallas_call | solution.py:125
  16.6 1.4 collective-permute-start
  18.0 4.6 %collective-permute-start.2 = (bf16[144,768]{1,0:T(8,128)(2,1)S(1)}, bf16[144,768]{1,0:T(8,128)(2,1)S(1)}, u32[]{:S(2)}, u32[]{:S(2)}) collective-permute-start(bf16[144,768]{1,0:T(8,128)(2,1)S(1)} %get-tuple-element.33), channel_id=1, source_target_pairs={{0,64},{32,96},{64,128},{96,160},{128,192},{160,224},{1,65},{33,97... | collective-permute-start | bytes 663560 | tf_op jit(solution)/shard_map/ppermute | solution.py:24
  22.6 1.3 collective-permute-start.1
  23.9 7.0 %collective-permute-start.3 = (bf16[48,768]{1,0:T(8,128)(2,1)S(1)}, bf16[48,768]{1,0:T(8,128)(2,1)S(1)}, u32[]{:S(2)}, u32[]{:S(2)}) collective-permute-start(bf16[48,768]{1,0:T(8,128)(2,1)S(1)} %get-tuple-element.34), channel_id=1, source_target_pairs={{0,96},{32,128},{64,160},{96,192},{128,224},{1,97},{33,129},{65,16... | collective-permute-start | bytes 221192 | tf_op jit(solution)/shard_map/ppermute | solution.py:24
  31.3 1.6 %collective-permute-done.3.above_far_ref = bf16[48,768]{1,0:T(8,128)(2,1)S(1)} collective-permute-done((bf16[48,768]{1,0:T(8,128)(2,1)S(1)}, bf16[48,768]{1,0:T(8,128)(2,1)S(1)}, u32[]{:S(2)}, u32[]{:S(2)}) %collective-permute-start.3) | collective-permute-done | bytes 73760 | tf_op jit(solution)/shard_map/ppermute | solution.py:24
  32.9 3.0 %collective-permute-start.4 = (bf16[192,256]{1,0:T(8,128)(2,1)S(1)}, bf16[192,256]{1,0:T(8,128)(2,1)S(1)}, u32[]{:S(2)}, u32[]{:S(2)}) collective-permute-start(bf16[192,256]{1,0:T(8,128)(2,1)S(1)} %get-tuple-element.36), channel_id=1, source_target_pairs={{0,29},{1,30},{2,31},{3,0},{4,1},{5,2},{6,3},{7,4},{8,5},{9,6},{10... | collective-permute-start | bytes 294920 | tf_op jit(solution)/shard_map/ppermute | solution.py:28
  37.1 3.4 %collective-permute-start.8 = (bf16[768,256]{1,0:T(8,128)(2,1)S(1)}, bf16[768,256]{1,0:T(8,128)(2,1)S(1)}, u32[]{:S(2)}, u32[]{:S(2)}) collective-permute-start(bf16[768,256]{1,0:T(8,128)(2,1)S(1)} %bitcast.11), channel_id=1, source_target_pairs={{0,3},{1,4},{2,5},{3,6},{4,7},{5,8},{6,9},{7,10},{8,11},{9,12},{10... | collective-permute-start | bytes 1179656 | tf_op jit(solution)/shard_map/ppermute | solution.py:28
  40.5 1.5 collective-permute-start.6
  44.6 5.2 %collective-permute-start.7 = (bf16[320,512]{1,0:T(8,128)(2,1)S(1)}, bf16[320,512]{1,0:T(8,128)(2,1)S(1)}, u32[]{:S(2)}, u32[]{:S(2)}) collective-permute-start(bf16[320,512]{1,0:T(8,128)(2,1)S(1)} %get-tuple-element.40), channel_id=1, source_target_pairs={{0,32},{32,0},{1,33},{33,1},{2,34},{34,2},{3,35},{35,3},{4,36},{36... | collective-permute-start | bytes 983048 | tf_op jit(solution)/shard_map/ppermute | solution.py:652
  49.8 9.3 %collective-permute-done.7.received_ref = bf16[320,512]{1,0:T(8,128)(2,1)S(1)} collective-permute-done((bf16[320,512]{1,0:T(8,128)(2,1)S(1)}, bf16[320,512]{1,0:T(8,128)(2,1)S(1)}, u32[]{:S(2)}, u32[]{:S(2)}) %collective-permute-start.7) | collective-permute-done | bytes 327712 | tf_op jit(solution)/shard_map/ppermute | solution.py:652
  59.1 1.5 shard_map.98
  60.7 7.1 %all-to-all-start.1 = ((bf16[4,832,256]{2,1,0:T(8,128)(2,1)}), bf16[4,832,256]{2,1,0:T(8,128)(2,1)S(1)}, u32[]{:S(2)}, u32[]{:S(2)}) async-start(bf16[4,832,256]{2,1,0:T(8,128)(2,1)} %get-tuple-element.43), calls=%async_computation.1 | async-start | bytes 3407872 | tf_op jit(solution)/shard_map/all_to_all | solution.py:658
  68.0 5.2 %collective-permute-start.9 = (bf16[768,256]{1,0:T(8,128)(2,1)S(1)}, bf16[768,256]{1,0:T(8,128)(2,1)}, u32[]{:S(2)}, u32[]{:S(2)}) collective-permute-start(bf16[768,256]{1,0:T(8,128)(2,1)S(1)} %get-tuple-element.42), channel_id=1, source_target_pairs={{0,29},{1,30},{2,31},{3,0},{4,1},{5,2},{6,3},{7,4},{8,5},{9,6},{10... | collective-permute-start | bytes 1179656 | tf_op jit(solution)/shard_map/ppermute | solution.py:28
  73.1 1.8 %collective-permute-start.12 = (bf16[192,256]{1,0:T(8,128)(2,1)S(1)}, bf16[192,256]{1,0:T(8,128)(2,1)S(1)}, u32[]{:S(2)}, u32[]{:S(2)}) collective-permute-start(bf16[192,256]{1,0:T(8,128)(2,1)S(1)} %slice.20), channel_id=1, source_target_pairs={{0,29},{1,30},{2,31},{3,0},{4,1},{5,2},{6,3},{7,4},{8,5},{9,6},{10... | collective-permute-start | bytes 294920 | tf_op jit(solution)/shard_map/ppermute | solution.py:28
  75.0 14.6 %collective-permute-done.12.west_grad_ref.west_ref = bf16[192,256]{1,0:T(8,128)(2,1)S(1)} collective-permute-done((bf16[192,256]{1,0:T(8,128)(2,1)S(1)}, bf16[192,256]{1,0:T(8,128)(2,1)S(1)}, u32[]{:S(2)}, u32[]{:S(2)}) %collective-permute-start.12) | collective-permute-done | bytes 98336 | tf_op jit(solution)/shard_map/ppermute | solution.py:28
  91.5 8.0 %shard_map.99 = (f32[1408,256]{1,0:T(8,128)}, f32[1408,256]{1,0:T(8,128)}, bf16[192,768]{1,0:T(8,128)(2,1)}, bf16[144,512]{1,0:T(8,128)(2,1)}, bf16[48,512]{1,0:...) custom-call(s32[3]{0:T(128)} %copy-done.12, bf16[1536,256]{1,0:T(8,128)(2,1)} %bitcast.4.center_in_ref, ...), custom_call_target="tpu_custom_call" | custom-call | flops 2013265920 | bytes 8388608 | tf_op jit(solution)/shard_map/pallas_call | solution.py:464
  100.2 3.1 %collective-permute-done.17.received_ref = f32[1408,256]{1,0:T(8,128)S(1)} collective-permute-done((f32[1408,256]{1,0:T(8,128)}, f32[1408,256]{1,0:T(8,128)S(1)}, u32[]{:S(2)}, u32[]{:S(2)}) %collective-permute-start.17) | collective-permute-done | bytes 1441824 | tf_op jit(solution)/shard_map/ppermute | solution.py:678
  103.3 1.4 copy-done.2
  104.6 1.5 shard_map.101
  106.1 9.1 %all-to-all-start.2 = ((bf16[16,82,256]{2,1,0:T(8,128)(2,1)}), bf16[16,82,256]{2,1,0:T(8,128)(2,1)S(1)}, u32[]{:S(2)}, u32[]{:S(2)}) async-start(bf16[16,82,256]{2,1,0:T(8,128)(2,1)} %shard_map.101), calls=%async_computation.2 | async-start | bytes 1441792 | tf_op jit(solution)/shard_map/all_to_all | solution.py:679
  115.3 1.3 collective-permute-start.13
  116.6 4.6 %collective-permute-start.15 = (bf16[144,512]{1,0:T(8,128)(2,1)S(1)}, bf16[144,512]{1,0:T(8,128)(2,1)S(1)}, u32[]{:S(2)}, u32[]{:S(2)}) collective-permute-start(bf16[144,512]{1,0:T(8,128)(2,1)S(1)} %copy-done.19), channel_id=1, source_target_pairs={{0,64},{32,96},{64,128},{96,160},{128,192},{160,224},{1,65},{33,97... | collective-permute-start | bytes 442376 | tf_op jit(solution)/shard_map/ppermute | solution.py:24
  121.1 1.3 collective-permute-start.14
  122.5 7.5 %collective-permute-start.16 = (bf16[48,512]{1,0:T(8,128)(2,1)S(1)}, bf16[48,512]{1,0:T(8,128)(2,1)S(1)}, u32[]{:S(2)}, u32[]{:S(2)}) collective-permute-start(bf16[48,512]{1,0:T(8,128)(2,1)S(1)} %copy-done.21), channel_id=1, source_target_pairs={{0,96},{32,128},{64,160},{96,192},{128,224},{1,97},{33,129},{65,16... | collective-permute-start | bytes 147464 | tf_op jit(solution)/shard_map/ppermute | solution.py:24
  131.7 3.5 %all-to-all-done.2.pieces_ref = bf16[16,82,256]{2,1,0:T(8,128)(2,1)S(1)} async-done(((bf16[16,82,256]{2,1,0:T(8,128)(2,1)}), bf16[16,82,256]{2,1,0:T(8,128)(2,1)S(1)}, u32[]{:S(2)}, u32[]{:S(2)}) %all-to-all-start.2) | async-done | bytes 671776 | tf_op jit(solution)/shard_map/all_to_all | solution.py:679
  136.2 7.8 %all-to-all-start.3 = ((f32[8,82,256]{2,1,0:T(8,128)}), f32[8,82,256]{2,1,0:T(8,128)S(1)}, u32[]{:S(2)}, u32[]{:S(2)}) async-start(f32[8,82,256]{2,1,0:T(8,128)} %shard_map.102), calls=%async_computation.3 | async-start | bytes 1441792 | tf_op jit(solution)/shard_map/all_to_all | solution.py:681
  144.7 8.7 %shard_map.100 = bf16[12,16,2048]{2,1,0:T(8,128)(2,1)} custom-call(bf16[192,768]{1,0:T(8,128)(2,1)} %get-tuple-element.44.windows_ref, bf16[192,512]{1,0:T(8,128)(2,1)} %copy-done.3, bf16[192,256]{1,0:T(8,128)(2,1)} %copy-done.15, bf16[192,256]{1,0:T(8,128)(2,1)} %copy-done.14, bf16[144,512]{1,0:T(8,128)(2,1)} %copy-done.5, bf16[48,512]{1,0:T(8,128)(2,1)} %copy-done.10, ...), custom_call_target="tpu_custom_call" | custom-call | flops 2013265920 | bytes 20971520 | tf_op jit(solution)/shard_map/pallas_call | solution.py:598
  153.3 2.1 %all-to-all-done.3.parts_ref = f32[8,82,256]{2,1,0:T(8,128)S(1)} async-done(((f32[8,82,256]{2,1,0:T(8,128)}), f32[8,82,256]{2,1,0:T(8,128)S(1)}, u32[]{:S(2)}, u32[]{:S(2)}) %all-to-all-start.3) | async-done | bytes 671776 | tf_op jit(solution)/shard_map/all_to_all | solution.py:681
  (77 shorter events, 12.8 us)
Async XLA Ops:
  3.8 32.1 %all-to-all-start = ((bf16[8,192,256]{2,1,0:T(8,128)(2,1)}), bf16[8,192,256]{2,1,0:T(8,128)(2,1)}, u32[]{:S(2)}, u32[]{:S(2)}) async-start(bf16[8,192,256]{2,1,0:T(8,128)(2,1)} %get-tuple-element.28.after_ref), calls=%async_computation | async-start | bytes 1572864 | tf_op jit(solution)/shard_map/all_to_all | solution.py:631
  14.4 16.5 %copy-start.16 = (s32[16,12]{1,0:T(8,128)S(1)}, s32[16,12]{1,0:T(8,128)}, u32[]{:S(2)}) copy-start(s32[16,12]{1,0:T(8,128)} %param.12) | copy-start | bytes 2308
  14.4 16.5 %copy-start.17 = (f32[3]{0:T(128)S(1)}, f32[3]{0:T(128)}, u32[]{:S(2)}) copy-start(f32[3]{0:T(128)} %param.13) | copy-start | bytes 40
  16.6 26.9 %copy-start.9 = (bf16[2,256,256]{2,1,0:T(8,128)(2,1)S(1)}, bf16[2,256,256]{2,1,0:T(8,128)(2,1)}, u32[]{:S(2)}) copy-start(bf16[2,256,256]{2,1,0:T(8,128)(2,1)} %project_ref.1) | copy-start | bytes 786436
  16.6 16.2 %collective-permute-start = (bf16[144,768]{1,0:T(8,128)(2,1)S(1)}, bf16[144,768]{1,0:T(8,128)(2,1)S(1)}, u32[]{:S(2)}, u32[]{:S(2)}) collective-permute-start(bf16[144,768]{1,0:T(8,128)(2,1)S(1)} %get-tuple-element.31), channel_id=1, source_target_pairs={{64,0},{96,32},{128,64},{160,96},{192,128},{224,160},{65,1},{97,33... | collective-permute-start | bytes 663560 | tf_op jit(solution)/shard_map/ppermute | solution.py:24
  18.0 14.8 %collective-permute-start.2 = (bf16[144,768]{1,0:T(8,128)(2,1)S(1)}, bf16[144,768]{1,0:T(8,128)(2,1)S(1)}, u32[]{:S(2)}, u32[]{:S(2)}) collective-permute-start(bf16[144,768]{1,0:T(8,128)(2,1)S(1)} %get-tuple-element.33), channel_id=1, source_target_pairs={{0,64},{32,96},{64,128},{96,160},{128,192},{160,224},{1,65},{33,97... | collective-permute-start | bytes 663560 | tf_op jit(solution)/shard_map/ppermute | solution.py:24
  22.6 8.7 %collective-permute-start.1 = (bf16[48,768]{1,0:T(8,128)(2,1)S(1)}, bf16[48,768]{1,0:T(8,128)(2,1)S(1)}, u32[]{:S(2)}, u32[]{:S(2)}) collective-permute-start(bf16[48,768]{1,0:T(8,128)(2,1)S(1)} %get-tuple-element.32), channel_id=1, source_target_pairs={{96,0},{128,32},{160,64},{192,96},{224,128},{97,1},{129,33},{161,6... | collective-permute-start | bytes 221192 | tf_op jit(solution)/shard_map/ppermute | solution.py:24
  23.9 8.9 %collective-permute-start.3 = (bf16[48,768]{1,0:T(8,128)(2,1)S(1)}, bf16[48,768]{1,0:T(8,128)(2,1)S(1)}, u32[]{:S(2)}, u32[]{:S(2)}) collective-permute-start(bf16[48,768]{1,0:T(8,128)(2,1)S(1)} %get-tuple-element.34), channel_id=1, source_target_pairs={{0,96},{32,128},{64,160},{96,192},{128,224},{1,97},{33,129},{65,16... | collective-permute-start | bytes 221192 | tf_op jit(solution)/shard_map/ppermute | solution.py:24
  32.9 10.2 %collective-permute-start.4 = (bf16[192,256]{1,0:T(8,128)(2,1)S(1)}, bf16[192,256]{1,0:T(8,128)(2,1)S(1)}, u32[]{:S(2)}, u32[]{:S(2)}) collective-permute-start(bf16[192,256]{1,0:T(8,128)(2,1)S(1)} %get-tuple-element.36), channel_id=1, source_target_pairs={{0,29},{1,30},{2,31},{3,0},{4,1},{5,2},{6,3},{7,4},{8,5},{9,6},{10... | collective-permute-start | bytes 294920 | tf_op jit(solution)/shard_map/ppermute | solution.py:28
  35.9 7.5 %collective-permute-start.5 = (bf16[192,256]{1,0:T(8,128)(2,1)S(1)}, bf16[192,256]{1,0:T(8,128)(2,1)S(1)}, u32[]{:S(2)}, u32[]{:S(2)}) collective-permute-start(bf16[192,256]{1,0:T(8,128)(2,1)S(1)} %get-tuple-element.37), channel_id=1, source_target_pairs={{0,3},{1,4},{2,5},{3,6},{4,7},{5,8},{6,9},{7,10},{8,11},{9,12},{10... | collective-permute-start | bytes 294920 | tf_op jit(solution)/shard_map/ppermute | solution.py:28
  37.1 22.0 %collective-permute-start.8 = (bf16[768,256]{1,0:T(8,128)(2,1)S(1)}, bf16[768,256]{1,0:T(8,128)(2,1)S(1)}, u32[]{:S(2)}, u32[]{:S(2)}) collective-permute-start(bf16[768,256]{1,0:T(8,128)(2,1)S(1)} %bitcast.11), channel_id=1, source_target_pairs={{0,3},{1,4},{2,5},{3,6},{4,7},{5,8},{6,9},{7,10},{8,11},{9,12},{10... | collective-permute-start | bytes 1179656 | tf_op jit(solution)/shard_map/ppermute | solution.py:28
  40.5 18.6 %collective-permute-start.6 = (bf16[768,256]{1,0:T(8,128)(2,1)S(1)}, bf16[768,256]{1,0:T(8,128)(2,1)S(1)}, u32[]{:S(2)}, u32[]{:S(2)}) collective-permute-start(bf16[768,256]{1,0:T(8,128)(2,1)S(1)} %bitcast.12), channel_id=1, source_target_pairs={{0,29},{1,30},{2,31},{3,0},{4,1},{5,2},{6,3},{7,4},{8,5},{9,6},{10... | collective-permute-start | bytes 1179656 | tf_op jit(solution)/shard_map/ppermute | solution.py:28
  42.1 18.6 %copy-start.12 = (s32[3]{0:T(128)}, s32[3]{0:T(128)S(1)}, u32[]{:S(2)}) copy-start(s32[3]{0:T(128)S(1)} %pad_add_fusion.place_ref) | copy-start | bytes 40
  44.6 28.5 %copy-start.3 = (bf16[192,512]{1,0:T(8,128)(2,1)}, bf16[192,512]{1,0:T(8,128)(2,1)S(1)}, u32[]{:S(2)}) copy-start(bf16[192,512]{1,0:T(8,128)(2,1)S(1)} %get-tuple-element.39.grads_ref) | copy-start | bytes 589828
  44.6 14.5 %collective-permute-start.7 = (bf16[320,512]{1,0:T(8,128)(2,1)S(1)}, bf16[320,512]{1,0:T(8,128)(2,1)S(1)}, u32[]{:S(2)}, u32[]{:S(2)}) collective-permute-start(bf16[320,512]{1,0:T(8,128)(2,1)S(1)} %get-tuple-element.40), channel_id=1, source_target_pairs={{0,32},{32,0},{1,33},{33,1},{2,34},{34,2},{3,35},{35,3},{4,36},{36... | collective-permute-start | bytes 983048 | tf_op jit(solution)/shard_map/ppermute | solution.py:652
  60.7 29.6 %all-to-all-start.1 = ((bf16[4,832,256]{2,1,0:T(8,128)(2,1)}), bf16[4,832,256]{2,1,0:T(8,128)(2,1)S(1)}, u32[]{:S(2)}, u32[]{:S(2)}) async-start(bf16[4,832,256]{2,1,0:T(8,128)(2,1)} %get-tuple-element.43), calls=%async_computation.1 | async-start | bytes 3407872 | tf_op jit(solution)/shard_map/all_to_all | solution.py:658
  67.8 21.7 %collective-permute-start.10 = (bf16[768,256]{1,0:T(8,128)(2,1)S(1)}, bf16[768,256]{1,0:T(8,128)(2,1)S(1)}, u32[]{:S(2)}, u32[]{:S(2)}) collective-permute-start(bf16[768,256]{1,0:T(8,128)(2,1)S(1)} %get-tuple-element.42), channel_id=1, source_target_pairs={{0,3},{1,4},{2,5},{3,6},{4,7},{5,8},{6,9},{7,10},{8,11},{9,12},{10... | collective-permute-start | bytes 1179656 | tf_op jit(solution)/shard_map/ppermute | solution.py:28
  68.0 22.3 %collective-permute-start.9 = (bf16[768,256]{1,0:T(8,128)(2,1)S(1)}, bf16[768,256]{1,0:T(8,128)(2,1)}, u32[]{:S(2)}, u32[]{:S(2)}) collective-permute-start(bf16[768,256]{1,0:T(8,128)(2,1)S(1)} %get-tuple-element.42), channel_id=1, source_target_pairs={{0,29},{1,30},{2,31},{3,0},{4,1},{5,2},{6,3},{7,4},{8,5},{9,6},{10... | collective-permute-start | bytes 1179656 | tf_op jit(solution)/shard_map/ppermute | solution.py:28
  73.1 16.4 %collective-permute-start.12 = (bf16[192,256]{1,0:T(8,128)(2,1)S(1)}, bf16[192,256]{1,0:T(8,128)(2,1)S(1)}, u32[]{:S(2)}, u32[]{:S(2)}) collective-permute-start(bf16[192,256]{1,0:T(8,128)(2,1)S(1)} %slice.20), channel_id=1, source_target_pairs={{0,29},{1,30},{2,31},{3,0},{4,1},{5,2},{6,3},{7,4},{8,5},{9,6},{10... | collective-permute-start | bytes 294920 | tf_op jit(solution)/shard_map/ppermute | solution.py:28
  74.9 14.6 %collective-permute-start.11 = (bf16[192,256]{1,0:T(8,128)(2,1)S(1)}, bf16[192,256]{1,0:T(8,128)(2,1)S(1)}, u32[]{:S(2)}, u32[]{:S(2)}) collective-permute-start(bf16[192,256]{1,0:T(8,128)(2,1)S(1)} %slice.20), channel_id=1, source_target_pairs={{0,3},{1,4},{2,5},{3,6},{4,7},{5,8},{6,9},{7,10},{8,11},{9,12},{10... | collective-permute-start | bytes 294920 | tf_op jit(solution)/shard_map/ppermute | solution.py:28
  99.6 3.7 %collective-permute-start.17 = (f32[1408,256]{1,0:T(8,128)}, f32[1408,256]{1,0:T(8,128)S(1)}, u32[]{:S(2)}, u32[]{:S(2)}) collective-permute-start(f32[1408,256]{1,0:T(8,128)} %get-tuple-element.50), channel_id=1, source_target_pairs={{0,1},{1,0},{2,3},{3,2},{4,5},{5,4},{6,7},{7,6},{8,9},{9,8},{10,11... | collective-permute-start | bytes 4325384 | tf_op jit(solution)/shard_map/ppermute | solution.py:678
  104.6 16.5 %copy-start.22 = (bf16[48,512]{1,0:T(8,128)(2,1)S(1)}, bf16[48,512]{1,0:T(8,128)(2,1)}, u32[]{:S(2)}) copy-start(bf16[48,512]{1,0:T(8,128)(2,1)} %get-tuple-element.46) | copy-start | bytes 147460
  104.6 17.8 %copy-start.21 = (bf16[48,512]{1,0:T(8,128)(2,1)S(1)}, bf16[48,512]{1,0:T(8,128)(2,1)}, u32[]{:S(2)}) copy-start(bf16[48,512]{1,0:T(8,128)(2,1)} %get-tuple-element.48) | copy-start | bytes 147460
  106.1 29.0 %all-to-all-start.2 = ((bf16[16,82,256]{2,1,0:T(8,128)(2,1)}), bf16[16,82,256]{2,1,0:T(8,128)(2,1)S(1)}, u32[]{:S(2)}, u32[]{:S(2)}) async-start(bf16[16,82,256]{2,1,0:T(8,128)(2,1)} %shard_map.101), calls=%async_computation.2 | async-start | bytes 1441792 | tf_op jit(solution)/shard_map/all_to_all | solution.py:679
  115.3 16.5 %collective-permute-start.13 = (bf16[144,512]{1,0:T(8,128)(2,1)S(1)}, bf16[144,512]{1,0:T(8,128)(2,1)S(1)}, u32[]{:S(2)}, u32[]{:S(2)}) collective-permute-start(bf16[144,512]{1,0:T(8,128)(2,1)S(1)} %copy-done.20), channel_id=1, source_target_pairs={{64,0},{96,32},{128,64},{160,96},{192,128},{224,160},{65,1},{97,33... | collective-permute-start | bytes 442376 | tf_op jit(solution)/shard_map/ppermute | solution.py:24
  116.6 15.1 %collective-permute-start.15 = (bf16[144,512]{1,0:T(8,128)(2,1)S(1)}, bf16[144,512]{1,0:T(8,128)(2,1)S(1)}, u32[]{:S(2)}, u32[]{:S(2)}) collective-permute-start(bf16[144,512]{1,0:T(8,128)(2,1)S(1)} %copy-done.19), channel_id=1, source_target_pairs={{0,64},{32,96},{64,128},{96,160},{128,192},{160,224},{1,65},{33,97... | collective-permute-start | bytes 442376 | tf_op jit(solution)/shard_map/ppermute | solution.py:24
  121.1 10.0 %collective-permute-start.14 = (bf16[48,512]{1,0:T(8,128)(2,1)S(1)}, bf16[48,512]{1,0:T(8,128)(2,1)S(1)}, u32[]{:S(2)}, u32[]{:S(2)}) collective-permute-start(bf16[48,512]{1,0:T(8,128)(2,1)S(1)} %copy-done.22), channel_id=1, source_target_pairs={{96,0},{128,32},{160,64},{192,96},{224,128},{97,1},{129,33},{161,6... | collective-permute-start | bytes 147464 | tf_op jit(solution)/shard_map/ppermute | solution.py:24
  122.5 9.3 %collective-permute-start.16 = (bf16[48,512]{1,0:T(8,128)(2,1)S(1)}, bf16[48,512]{1,0:T(8,128)(2,1)S(1)}, u32[]{:S(2)}, u32[]{:S(2)}) collective-permute-start(bf16[48,512]{1,0:T(8,128)(2,1)S(1)} %copy-done.21), channel_id=1, source_target_pairs={{0,96},{32,128},{64,160},{96,192},{128,224},{1,97},{33,129},{65,16... | collective-permute-start | bytes 147464 | tf_op jit(solution)/shard_map/ppermute | solution.py:24
  131.1 12.8 %copy-start.10 = (bf16[48,512]{1,0:T(8,128)(2,1)}, bf16[48,512]{1,0:T(8,128)(2,1)S(1)}, u32[]{:S(2)}) copy-start(bf16[48,512]{1,0:T(8,128)(2,1)S(1)} %collective-permute-done.14.up_far_ref.refs_1_) | copy-start | bytes 147460
  131.7 12.3 %copy-start.5 = (bf16[144,512]{1,0:T(8,128)(2,1)}, bf16[144,512]{1,0:T(8,128)(2,1)S(1)}, u32[]{:S(2)}) copy-start(bf16[144,512]{1,0:T(8,128)(2,1)S(1)} %collective-permute-done.13.up_near_ref.refs_0_) | copy-start | bytes 442372
  131.7 12.3 %copy-start.6 = (bf16[144,512]{1,0:T(8,128)(2,1)}, bf16[144,512]{1,0:T(8,128)(2,1)S(1)}, u32[]{:S(2)}) copy-start(bf16[144,512]{1,0:T(8,128)(2,1)S(1)} %collective-permute-done.15.down_near_ref.refs_2_) | copy-start | bytes 442372
  136.2 19.3 %all-to-all-start.3 = ((f32[8,82,256]{2,1,0:T(8,128)}), f32[8,82,256]{2,1,0:T(8,128)S(1)}, u32[]{:S(2)}, u32[]{:S(2)}) async-start(f32[8,82,256]{2,1,0:T(8,128)} %shard_map.102), calls=%async_computation.3 | async-start | bytes 1441792 | tf_op jit(solution)/shard_map/all_to_all | solution.py:681
  (13 other events, 57.9 us)

commit v4 on v3

--- a/solution.py
+++ b/solution.py
@@ -77,7 +77,7 @@
         yield buffer_ref.at[at % depth]
 
 
-STREAM_DEPTH = 3
+STREAM_DEPTH = 6
 
 
 def stream_scratch(in_width, width):
@@ -239,7 +239,13 @@
     acts = [(pre * gate).astype(bf16) for pre, gate in zip(pre_list, gates)]
     mixed = multiply(acts[0], project_ref[0]) + multiply(acts[1], project_ref[1])
     gate = sigmoid(mixed)
-    head_ref[...] = (mixed * gate).astype(bf16)
+    out = mixed * gate
+    cols, rows, _ = head_ref.shape
+    for half, row_ref in enumerate(terms_refs):
+        lanes = slice(128 * half, 128 * half + 128)
+        row_ref[: cols * rows, :] = out[:, lanes]
+        for col in range(cols):
+            head_ref[col, :, lanes] = row_ref[pl.ds(col, rows, stride=cols), :].astype(bf16)
     slope = gate * (1.0 + mixed * (1.0 - gate))
     out_grad = (upstream_ref[...].astype(f32) * pixel_weight_ref[...] * slope).astype(bf16)
     grads = [
@@ -270,7 +276,9 @@
             message_ref[rows, low : low + 128] = jnp.where(xh == 0, odd, even).astype(bf16)
 
 
-def head(place, point_pre, center, from_east, from_west, project, upstream, pixel_weight):
+def head(
+    rows, place, point_pre, center, from_east, from_west, project, upstream, pixel_weight
+):
     pixels, width = point_pre.shape
     count = AXIS_SIZES["y"]
     part = width // count
@@ -278,7 +286,7 @@
     return pl.pallas_call(
         head_kernel,
         out_shape=(
-            like((pixels, width), bf16),
+            like((pixels // rows, rows, width), bf16),
             like((pixels, 2 * width), bf16),
             like((pixels + 2 * part, 2 * width), bf16),
             like((count, part, width), f32),
@@ -343,18 +351,15 @@
     west_first_ref,
     west_second_ref,
     message_in_ref,
-    east_grad_ref,
-    west_grad_ref,
+    after_east_ref,
+    after_west_ref,
     kept_ref,
-    sent_ref,
+    rounded_ref,
     windows_ref,
-    up_near_ref,
-    up_far_ref,
-    down_near_ref,
-    down_far_ref,
     framed_ref,
     features_ref,
     message_ref,
+    sent_ref,
     semaphores,
 ):
     _, total, width = features_ref.shape
@@ -390,7 +395,6 @@
     pixels = total // LAT_COUNT
     room = padded(chunk)
     core, y, xh = place_ref[0], place_ref[1], place_ref[2]
-    far = up_far_ref.shape[0]
 
     edge = jnp.zeros((span, width), framed_ref.dtype)
     framed_ref[total : total + span, :width] = edge
@@ -408,13 +412,6 @@
             framed_ref[pl.ds(first, pixels), 3 * width :] = message_ref[
                 at, low + pixels : low + 2 * pixels, :
             ]
-    for at, side_ref in enumerate((east_grad_ref, west_grad_ref)):
-        lanes = slice(at * width, (at + 1) * width)
-        side = side_ref[...]
-        up_near_ref[:, lanes] = side[far:]
-        up_far_ref[:, lanes] = side[:far]
-        down_near_ref[:, lanes] = side[: pixels - far]
-        down_far_ref[:, lanes] = side[pixels - far :]
     own_rows = pl.ds(pl.multiple_of(span + (2 * y + xh) * pixels, 16), pixels)
     windows_ref[...] = framed_ref[own_rows, : 3 * width]
 
@@ -447,58 +444,85 @@
             project_rows = jnp.sum(message_ref[:, 4 * pixels :, :].astype(jnp.float32), axis=0)
             store(9 * width, project_rows)
             store(9 * width + project_rows.shape[0], product[:, 3 * width :])
+    rounded_ref[...] = sent_ref[...].astype(rounded_ref.dtype)
 
 
 def padded(chunk):
-    return (chunk + 7) // 8 * 8
-
-
-def weight_terms(span, place, features, message, sides):
+    return (chunk + 15) // 16 * 16
+
+
+def weight_terms(span, place, features, message, after):
     total, width = features[0].shape
     pixels = total // LAT_COUNT
-    far = span % pixels
     chunk = (10 * width + message.shape[1] - 4 * pixels) // LON_COUNT
-    out = like((LON_COUNT // 2 * padded(chunk), width), jnp.float32)
-    near_shape = like((pixels - far, 2 * width), jnp.bfloat16)
-    far_shape = like((far, 2 * width), jnp.bfloat16)
+    terms_shape = (LON_COUNT // 2 * padded(chunk), width)
     return pl.pallas_call(
         functools.partial(weight_terms_kernel, span, chunk),
-        out_shape=(out, out, like((pixels, 3 * width), jnp.bfloat16))
-        + (near_shape, far_shape, near_shape, far_shape),
-        in_specs=[SMEM] + [ANY] * 6 + [VMEM] * 2,
-        out_specs=(VMEM,) * 7,
+        out_shape=(
+            like(terms_shape, jnp.float32),
+            like(terms_shape, jnp.bfloat16),
+            like((pixels, 3 * width), jnp.bfloat16),
+        ),
+        in_specs=[SMEM] + [ANY] * 8,
+        out_specs=(VMEM,) * 3,
         scratch_shapes=[
             pltpu.VMEM((2 * span + total, 4 * width), jnp.bfloat16),
             pltpu.VMEM((3, total, width), jnp.bfloat16),
             pltpu.VMEM(message.shape, jnp.bfloat16),
+            pltpu.VMEM(terms_shape, jnp.float32),
             pltpu.SemaphoreType.DMA((6,)),
         ],
         compiler_params=params(60),
         cost_estimate=cost(20 * total * width * width, 8 * 2**20),
-    )(place, *features, message, *sides)
+    )(place, *features, message, *after)
 
 
 def pair_sum_kernel(kept_ref, received_ref, out_ref):
     count, chunk, _ = out_ref.shape
     room = kept_ref.shape[0] // count
     for at in range(count):
-        rows = slice(room * at, room * at + chunk)
-        out_ref[at] = (kept_ref[rows, :] + received_ref[rows, :]).astype(jnp.bfloat16)
+        rows = slice(room * at, room * (at + 1))
+        total = kept_ref[rows, :] + received_ref[rows, :].astype(jnp.float32)
+        out_ref[at] = total[:chunk].astype(jnp.bfloat16)
 
 
 def pair_sum(kept, received, chunk):
-    width = kept.shape[1]
-    steps, count = 4, LON_COUNT // 2
-    block = pl.BlockSpec((kept.shape[0] // steps, width), lambda s: (s, 0))
     return pl.pallas_call(
         pair_sum_kernel,
-        grid=(steps,),
-        out_shape=like((count, chunk, width), jnp.bfloat16),
-        in_specs=[block, block],
-        out_specs=pl.BlockSpec((count // steps, chunk, width), lambda s: (s, 0, 0)),
+        out_shape=like((LON_COUNT // 2, chunk, kept.shape[1]), jnp.bfloat16),
+        in_specs=[VMEM] * 2,
+        out_specs=VMEM,
         compiler_params=params(),
         cost_estimate=cost(kept.size, 10 * kept.size),
     )(kept, received)
+
+
+def side_slices_kernel(
+    east_grad_ref, west_grad_ref, up_near_ref, up_far_ref, down_near_ref, down_far_ref
+):
+    far = up_far_ref.shape[0]
+    for at, side_ref in enumerate((east_grad_ref, west_grad_ref)):
+        side = side_ref[...]
+        pixels, width = side.shape
+        lanes = slice(at * width, (at + 1) * width)
+        up_near_ref[:, lanes] = side[far:]
+        up_far_ref[:, lanes] = side[:far]
+        down_near_ref[:, lanes] = side[: pixels - far]
+        down_far_ref[:, lanes] = side[pixels - far :]
+
+
+def side_slices(east_grad, west_grad, far):
+    pixels, width = east_grad.shape
+    near_shape = like((pixels - far, 2 * width), jnp.bfloat16)
+    far_shape = like((far, 2 * width), jnp.bfloat16)
+    return pl.pallas_call(
+        side_slices_kernel,
+        out_shape=(near_shape, far_shape, near_shape, far_shape),
+        in_specs=[VMEM] * 2,
+        out_specs=(VMEM,) * 4,
+        compiler_params=params(),
+        cost_estimate=cost(pixels * width, 8 * pixels * width),
+    )(east_grad, west_grad)
 
 
 def piece_sum_kernel(pieces_ref, *refs):
@@ -506,14 +530,15 @@
     total = pieces_ref[0].astype(jnp.float32)
     for at in range(1, pieces_ref.shape[0]):
         total = total + pieces_ref[at].astype(jnp.float32)
+    rounded = total.astype(out_ref.dtype)
     for at in range(out_ref.shape[0]):
-        out_ref[at] = total
+        out_ref[at] = rounded
 
 
 def piece_sum(pieces, after):
     return pl.pallas_call(
         piece_sum_kernel,
-        out_shape=like((LAT_COUNT,) + pieces.shape[1:], jnp.float32),
+        out_shape=like((LAT_COUNT,) + pieces.shape[1:], jnp.bfloat16),
         in_specs=[VMEM] + [ANY] * len(after),
         out_specs=VMEM,
         compiler_params=params(),
@@ -526,7 +551,9 @@
     for half, sorted_ref in enumerate(sorted_refs):
         lanes = slice(128 * half, 128 * half + 128)
         for a in range(count):
-            sorted_ref[pl.ds(a, size, stride=count), :] = parts_ref[a, :, lanes]
+            sorted_ref[pl.ds(a, size, stride=count), :] = parts_ref[a, :, lanes].astype(
+                jnp.float32
+            )
         out_ref[:, lanes] = sorted_ref[...]
 
 
@@ -639,6 +666,7 @@
         jnp.where(labels[..., None] == class_index, class_weights, 0.0), axis=-1
     ).reshape(-1, 1)
     head_out, grads, message, mine = head(
+        rows,
         place,
         point_pre,
         center,
@@ -661,21 +689,22 @@
     east_grad = shift_columns(grads[:, :width], tiles_over)
     west_grad = shift_columns(grads[:, :width], -tiles_over)
 
-    kept, sent, windows, up_near, up_far, down_near, down_far = weight_terms(
+    kept, sent, windows = weight_terms(
         span,
         place,
         (column_features, first_east, second_east, first_west, second_west),
         gathered,
         (east_grad, west_grad),
     )
+    chunk = (10 * in_width + 2 * width) // (LAT_COUNT * LON_COUNT)
+    chip_sum = pair_sum(kept, lax.ppermute(sent, "c", [(0, 1), (1, 0)]), chunk)
+    up_near, up_far, down_near, down_far = side_slices(east_grad, west_grad, far_pixels)
     side_rows = (
         shift_rows(up_near, -near),
         shift_rows(up_far, -(near + 1)),
         shift_rows(down_near, near),
         shift_rows(down_far, near + 1),
     )
-    chunk = (10 * in_width + 2 * width) // (LAT_COUNT * LON_COUNT)
-    chip_sum = pair_sum(kept, lax.ppermute(sent, "c", [(0, 1), (1, 0)]), chunk)
     pieces = lax.all_to_all(chip_sum, ("xl", "z"), 0, 0)
 
     weight_grads = interleave(lax.all_to_all(piece_sum(pieces, side_rows), LAT, 0, 0))
@@ -683,7 +712,7 @@
         rows, windows, grads, east_grad, west_grad, side_rows, kernel, point_weight
     )
 
-    head_tile = head_out.reshape(rows, cols, width)
+    head_tile = jnp.swapaxes(head_out, 0, 1)
     grad_tile = jnp.swapaxes(input_grad, 0, 1)
     return (head_tile, grad_tile, weight_grads)
 

time: 158 us -> 153 us (0.968)
  waiting for transfers between devices: 36.4 us -> 39.5 us
  local copies, waits for them, and re-layouts: 11.2 us -> 8.63 us
  Pallas kernels: 27.1 us -> 24.8 us
  starting transfers between devices: 80.7 us -> 78.4 us
    ppermute x8, waiting for transfers between devices: 14.9 us -> 19.6 us  [shift_columns(): lax.ppermute(value, LON, [(i, (i + by) % LON_COUNT) for i in range(LON_CO...]
    all_to_all x1, starting transfers between devices: 9.11 us -> 5.23 us  [shards(): pieces = lax.all_to_all(chip_sum, ('xl', 'z'), 0, 0)]
    unnamed x48 -> x45, local copies, waits for them, and re-layouts: 9.89 us -> 7.34 us
    all_to_all x1, starting transfers between devices: 7.08 us -> 9.19 us  [shards(): gathered = lax.all_to_all(message, 'y', 0, 0)]
    ppermute x1, waiting for transfers between devices: 9.31 us -> 7.71 us  [shards(): other = lax.ppermute(message, 'xh', [(0, 1), (1, 0)])]
  transfers between devices with their start and end apart: 22 -> 22, of which waited for: 10 -> 11; matrix products, arithmetic and copies ran while one was open for 2% -> 1% of each run, Pallas kernels for 8% -> 7%
where the time goes in v4:
time: 153 us; the launch traced here: 152 us
  starting transfers between devices  78.4 us (51%)
  waiting for transfers between devices  39.5 us (26%)
  Pallas kernels  24.8 us (16%)
  local copies, waits for them, and re-layouts  8.63 us (6%)
    ppermute x8, starting transfers between devices, shift_rows(): return lax.ppermute(value, LAT, pairs)  28.3 us
    ppermute x8, waiting for transfers between devices, shift_columns(): lax.ppermute(value, LON, [(i, (i + by) % LON_COUNT) for i in range(LON_CO...  19.6 us
    ppermute x8, starting transfers between devices, shift_columns(): lax.ppermute(value, LON, [(i, (i + by) % LON_COUNT) for i in range(LON_CO...  16 us
    all_to_all x1, starting transfers between devices, shards(): gathered = lax.all_to_all(message, 'y', 0, 0)  9.19 us
    ppermute x1, waiting for transfers between devices, shards(): other = lax.ppermute(message, 'xh', [(0, 1), (1, 0)])  7.71 us
    all_to_all x1, starting transfers between devices, shards(): lax.all_to_all(piece_sum(pieces, side_rows), LAT, 0, 0)  7.44 us
    pallas_call x1, Pallas kernels, weight_terms(): pl.pallas_call(functools.partial(weight_terms_kernel, span, chunk), out_s...  7.43 us
    pallas_call x1, Pallas kernels, input_gradient(): pl.pallas_call(input_gradient_kernel, out_shape=like((pixels // rows, row...  7.37 us
  transfers between devices with their start and end apart: 22, of which 11 were waited for; matrix products, arithmetic and copies ran while one was open for 1% of the time, Pallas kernels for 7%

profile of v4, /device:TPU:32, one launch (start us, length us, event | category | flops | bytes accessed | tf_op | source)
XLA Modules:
  0.0 152.4 jit_solution(11779635405503036437)
XLA Ops:
  1.9 1.9 %shard_map.94 = (bf16[192,2048]{1,0:T(8,128)(2,1)S(1)}, bf16[8,192,256]{2,1,0:T(8,128)(2,1)}) custom-call(bf16[12,16,2048]{2,1,0:T(8,128)(2,1)S(1)} %bitcast.10), custom_call_target="tpu_custom_call" | custom-call | flops 201326592 | bytes 2359296 | tf_op jit(solution)/shard_map/pallas_call | solution.py:164
  3.8 6.9 %all-to-all-start = ((bf16[8,192,256]{2,1,0:T(8,128)(2,1)}), bf16[8,192,256]{2,1,0:T(8,128)(2,1)}, u32[]{:S(2)}, u32[]{:S(2)}) async-start(bf16[8,192,256]{2,1,0:T(8,128)(2,1)} %get-tuple-element.28.after_ref), calls=%async_computation | async-start | bytes 1572864 | tf_op jit(solution)/shard_map/all_to_all | solution.py:658
  10.7 3.7 %copy-done = bf16[9,2048,256]{2,1,0:T(8,128)(2,1)S(1)} copy-done((bf16[9,2048,256]{2,1,0:T(8,128)(2,1)S(1)}, bf16[9,2048,256]{2,1,0:T(8,128)(2,1)}, u32[]{:S(2)}) %copy-start) | copy-done | bytes 9437208
  14.4 2.2 %shard_map.95 = (bf16[144,768]{1,0:T(8,128)(2,1)S(1)}, bf16[48,768]{1,0:T(8,128)(2,1)S(1)}, bf16[144,768]{1,0:T(8,128)(2,1)S(1)}, bf16[48,768]{1,0:T(8,128)(2,1)...) custom-call(bf16[192,2048]{1,0:T(8,128)(2,1)S(1)} %get-tuple-element.27.flat_ref, ...), custom_call_target="tpu_custom_call" | custom-call | flops 2013265920 | bytes 10485760 | tf_op jit(solution)/shard_map/pallas_call | solution.py:125
  16.6 1.4 collective-permute-start
  18.0 4.6 %collective-permute-start.2 = (bf16[144,768]{1,0:T(8,128)(2,1)S(1)}, bf16[144,768]{1,0:T(8,128)(2,1)S(1)}, u32[]{:S(2)}, u32[]{:S(2)}) collective-permute-start(bf16[144,768]{1,0:T(8,128)(2,1)S(1)} %get-tuple-element.33), channel_id=1, source_target_pairs={{0,64},{32,96},{64,128},{96,160},{128,192},{160,224},{1,65},{33,97... | collective-permute-start | bytes 663560 | tf_op jit(solution)/shard_map/ppermute | solution.py:24
  22.6 1.3 collective-permute-start.1
  23.9 7.0 %collective-permute-start.3 = (bf16[48,768]{1,0:T(8,128)(2,1)S(1)}, bf16[48,768]{1,0:T(8,128)(2,1)S(1)}, u32[]{:S(2)}, u32[]{:S(2)}) collective-permute-start(bf16[48,768]{1,0:T(8,128)(2,1)S(1)} %get-tuple-element.34), channel_id=1, source_target_pairs={{0,96},{32,128},{64,160},{96,192},{128,224},{1,97},{33,129},{65,16... | collective-permute-start | bytes 221192 | tf_op jit(solution)/shard_map/ppermute | solution.py:24
  31.3 1.6 %collective-permute-done.3.above_far_ref = bf16[48,768]{1,0:T(8,128)(2,1)S(1)} collective-permute-done((bf16[48,768]{1,0:T(8,128)(2,1)S(1)}, bf16[48,768]{1,0:T(8,128)(2,1)S(1)}, u32[]{:S(2)}, u32[]{:S(2)}) %collective-permute-start.3) | collective-permute-done | bytes 73760 | tf_op jit(solution)/shard_map/ppermute | solution.py:24
  32.9 3.0 %collective-permute-start.4 = (bf16[192,256]{1,0:T(8,128)(2,1)S(1)}, bf16[192,256]{1,0:T(8,128)(2,1)S(1)}, u32[]{:S(2)}, u32[]{:S(2)}) collective-permute-start(bf16[192,256]{1,0:T(8,128)(2,1)S(1)} %get-tuple-element.36), channel_id=1, source_target_pairs={{0,29},{1,30},{2,31},{3,0},{4,1},{5,2},{6,3},{7,4},{8,5},{9,6},{10... | collective-permute-start | bytes 294920 | tf_op jit(solution)/shard_map/ppermute | solution.py:28
  37.1 4.8 %collective-permute-start.6 = (bf16[768,256]{1,0:T(8,128)(2,1)S(1)}, bf16[768,256]{1,0:T(8,128)(2,1)S(1)}, u32[]{:S(2)}, u32[]{:S(2)}) collective-permute-start(bf16[768,256]{1,0:T(8,128)(2,1)S(1)} %bitcast.12), channel_id=1, source_target_pairs={{0,29},{1,30},{2,31},{3,0},{4,1},{5,2},{6,3},{7,4},{8,5},{9,6},{10... | collective-permute-start | bytes 1179656 | tf_op jit(solution)/shard_map/ppermute | solution.py:28
  43.5 1.6 %shard_map.97 = (bf16[12,16,256]{2,1,0:T(8,128)(2,1)}, bf16[192,512]{1,0:T(8,128)(2,1)S(1)}, bf16[320,512]{1,0:T(8,128)(2,1)S(1)}, f32[4,64,256]{2,1,0:T(8,128)S(1)}) custom-call(s32[3]{0:T(128)S(1)} %pad_add_fusion.place_ref, f32[192,256]{1,0:T(8,128)S(1)} %get-tuple-element.29.point_ref, f32[192,256]{1,0:T(8,128)S(1)} %get-tuple-element.35.center_ref, ...), custom_call_target="tpu_custom_call" | custom-call | flops 150994944 | bytes 1179648 | tf_op jit(solution)/shard_map/pallas_call | solution.py:286
  45.1 5.1 %collective-permute-start.7 = (bf16[320,512]{1,0:T(8,128)(2,1)S(1)}, bf16[320,512]{1,0:T(8,128)(2,1)S(1)}, u32[]{:S(2)}, u32[]{:S(2)}) collective-permute-start(bf16[320,512]{1,0:T(8,128)(2,1)S(1)} %get-tuple-element.40), channel_id=1, source_target_pairs={{0,32},{32,0},{1,33},{33,1},{2,34},{34,2},{3,35},{35,3},{4,36},{36... | collective-permute-start | bytes 983048 | tf_op jit(solution)/shard_map/ppermute | solution.py:680
  50.2 7.7 %collective-permute-done.7.received_ref = bf16[320,512]{1,0:T(8,128)(2,1)S(1)} collective-permute-done((bf16[320,512]{1,0:T(8,128)(2,1)S(1)}, bf16[320,512]{1,0:T(8,128)(2,1)S(1)}, u32[]{:S(2)}, u32[]{:S(2)}) %collective-permute-start.7) | collective-permute-done | bytes 327712 | tf_op jit(solution)/shard_map/ppermute | solution.py:680
  57.9 1.8 %collective-permute-done.8.after_west_ref.west_first_ref = bf16[768,256]{1,0:T(8,128)(2,1)S(1)} collective-permute-done((bf16[768,256]{1,0:T(8,128)(2,1)S(1)}, bf16[768,256]{1,0:T(8,128)(2,1)S(1)}, u32[]{:S(2)}, u32[]{:S(2)}) %collective-permute-start.8) | collective-permute-done | bytes 393248 | tf_op jit(solution)/shard_map/ppermute | solution.py:28
  59.7 1.3 shard_map.98
  61.0 9.2 %all-to-all-start.1 = ((bf16[4,832,256]{2,1,0:T(8,128)(2,1)}), bf16[4,832,256]{2,1,0:T(8,128)(2,1)}, u32[]{:S(2)}, u32[]{:S(2)}) async-start(bf16[4,832,256]{2,1,0:T(8,128)(2,1)} %get-tuple-element.43), calls=%async_computation.1 | async-start | bytes 3407872 | tf_op jit(solution)/shard_map/all_to_all | solution.py:686
  70.2 3.3 %collective-permute-start.9 = (bf16[768,256]{1,0:T(8,128)(2,1)S(1)}, bf16[768,256]{1,0:T(8,128)(2,1)S(1)}, u32[]{:S(2)}, u32[]{:S(2)}) collective-permute-start(bf16[768,256]{1,0:T(8,128)(2,1)S(1)} %get-tuple-element.42), channel_id=1, source_target_pairs={{0,29},{1,30},{2,31},{3,0},{4,1},{5,2},{6,3},{7,4},{8,5},{9,6},{10... | collective-permute-start | bytes 1179656 | tf_op jit(solution)/shard_map/ppermute | solution.py:28
  73.6 4.8 %collective-permute-start.12 = (bf16[192,256]{1,0:T(8,128)(2,1)S(1)}, bf16[192,256]{1,0:T(8,128)(2,1)S(1)}, u32[]{:S(2)}, u32[]{:S(2)}) collective-permute-start(bf16[192,256]{1,0:T(8,128)(2,1)S(1)} %slice.20), channel_id=1, source_target_pairs={{0,29},{1,30},{2,31},{3,0},{4,1},{5,2},{6,3},{7,4},{8,5},{9,6},{10... | collective-permute-start | bytes 294920 | tf_op jit(solution)/shard_map/ppermute | solution.py:28
  78.4 16.6 %collective-permute-done.11.after_east_ref.east_grad_ref.east_ref = bf16[192,256]{1,0:T(8,128)(2,1)S(1)} collective-permute-done((bf16[192,256]{1,0:T(8,128)(2,1)S(1)}, bf16[192,256]{1,0:T(8,128)(2,1)S(1)}, u32[]{:S(2)}, u32[]{:S(2)}) %collective-permute-start.11) | collective-permute-done | bytes 98336 | tf_op jit(solution)/shard_map/ppermute | solution.py:28
  96.0 7.4 %shard_map.99 = (f32[1536,256]{1,0:T(8,128)}, bf16[1536,256]{1,0:T(8,128)(2,1)}, bf16[192,768]{1,0:T(8,128)(2,1)}) custom-call(s32[3]{0:T(128)} %copy-done.16, bf16[1536,256]{1,0:T(8,128)(2,1)} %bitcast.5.center_in_ref, bf16[768,256]{1,0:T(8,128)(2,1)} %copy-done.11, bf16[768,256]{1,0:T(8,128)(2,1)} %copy-done.20, bf16[768,256]{1,0:T(8,128)(2,1)} %copy-done.12, ...), custom_call_target="tpu_custom_call" | custom-call | flops 2013265920 | bytes 8388608 | tf_op jit(solution)/shard_map/pallas_call | solution.py:459
  103.6 2.5 %collective-permute-done.17.received_ref = bf16[1536,256]{1,0:T(8,128)(2,1)S(1)} collective-permute-done((bf16[1536,256]{1,0:T(8,128)(2,1)}, bf16[1536,256]{1,0:T(8,128)(2,1)S(1)}, u32[]{:S(2)}, u32[]{:S(2)}) %collective-permute-start.17) | collective-permute-done | bytes 786464 | tf_op jit(solution)/shard_map/ppermute | solution.py:700
  106.0 1.4 copy-done.2
  108.4 5.2 %all-to-all-start.2 = ((bf16[16,82,256]{2,1,0:T(8,128)(2,1)}), bf16[16,82,256]{2,1,0:T(8,128)(2,1)S(1)}, u32[]{:S(2)}, u32[]{:S(2)}) async-start(bf16[16,82,256]{2,1,0:T(8,128)(2,1)} %shard_map.102), calls=%async_computation.2 | async-start | bytes 1441792 | tf_op jit(solution)/shard_map/all_to_all | solution.py:708
  113.7 1.3 collective-permute-start.13
  115.0 4.6 %collective-permute-start.15 = (bf16[144,512]{1,0:T(8,128)(2,1)S(1)}, bf16[144,512]{1,0:T(8,128)(2,1)S(1)}, u32[]{:S(2)}, u32[]{:S(2)}) collective-permute-start(bf16[144,512]{1,0:T(8,128)(2,1)S(1)} %get-tuple-element.47), channel_id=1, source_target_pairs={{0,64},{32,96},{64,128},{96,160},{128,192},{160,224},{1,65},{33,97... | collective-permute-start | bytes 442376 | tf_op jit(solution)/shard_map/ppermute | solution.py:24
  119.6 1.3 collective-permute-start.14
  120.9 7.0 %collective-permute-start.16 = (bf16[48,512]{1,0:T(8,128)(2,1)S(1)}, bf16[48,512]{1,0:T(8,128)(2,1)S(1)}, u32[]{:S(2)}, u32[]{:S(2)}) collective-permute-start(bf16[48,512]{1,0:T(8,128)(2,1)S(1)} %get-tuple-element.48), channel_id=1, source_target_pairs={{0,96},{32,128},{64,160},{96,192},{128,224},{1,97},{33,129},{65,16... | collective-permute-start | bytes 147464 | tf_op jit(solution)/shard_map/ppermute | solution.py:24
  129.6 4.1 %all-to-all-done.2.pieces_ref = bf16[16,82,256]{2,1,0:T(8,128)(2,1)S(1)} async-done(((bf16[16,82,256]{2,1,0:T(8,128)(2,1)}), bf16[16,82,256]{2,1,0:T(8,128)(2,1)S(1)}, u32[]{:S(2)}, u32[]{:S(2)}) %all-to-all-start.2) | async-done | bytes 671776 | tf_op jit(solution)/shard_map/all_to_all | solution.py:708
  134.6 7.4 %all-to-all-start.3 = ((bf16[8,82,256]{2,1,0:T(8,128)(2,1)}), bf16[8,82,256]{2,1,0:T(8,128)(2,1)S(1)}, u32[]{:S(2)}, u32[]{:S(2)}) async-start(bf16[8,82,256]{2,1,0:T(8,128)(2,1)} %shard_map.103), calls=%async_computation.3 | async-start | bytes 720896 | tf_op jit(solution)/shard_map/all_to_all | solution.py:710
  142.0 7.4 %shard_map.101 = bf16[12,16,2048]{2,1,0:T(8,128)(2,1)} custom-call(bf16[192,768]{1,0:T(8,128)(2,1)} %get-tuple-element.44.windows_ref, bf16[192,512]{1,0:T(8,128)(2,1)} %copy-done.3, bf16[192,256]{1,0:T(8,128)(2,1)} %copy-done.7, bf16[192,256]{1,0:T(8,128)(2,1)} %copy-done.9, bf16[144,512]{1,0:T(8,128)(2,1)} %copy-done.5, bf16[48,512]{1,0:T(8,128)(2,1)} %copy-done.14, ...), custom_call_target="tpu_custom_call" | custom-call | flops 2013265920 | bytes 20971520 | tf_op jit(solution)/shard_map/pallas_call | solution.py:625
  149.4 1.9 %all-to-all-done.3.parts_ref = bf16[8,82,256]{2,1,0:T(8,128)(2,1)S(1)} async-done(((bf16[8,82,256]{2,1,0:T(8,128)(2,1)}), bf16[8,82,256]{2,1,0:T(8,128)(2,1)S(1)}, u32[]{:S(2)}, u32[]{:S(2)}) %all-to-all-start.3) | async-done | bytes 335904 | tf_op jit(solution)/shard_map/all_to_all | solution.py:710
  (74 shorter events, 10.2 us)
Async XLA Ops:
  3.8 32.2 %all-to-all-start = ((bf16[8,192,256]{2,1,0:T(8,128)(2,1)}), bf16[8,192,256]{2,1,0:T(8,128)(2,1)}, u32[]{:S(2)}, u32[]{:S(2)}) async-start(bf16[8,192,256]{2,1,0:T(8,128)(2,1)} %get-tuple-element.28.after_ref), calls=%async_computation | async-start | bytes 1572864 | tf_op jit(solution)/shard_map/all_to_all | solution.py:658
  14.4 16.5 %copy-start.18 = (s32[16,12]{1,0:T(8,128)S(1)}, s32[16,12]{1,0:T(8,128)}, u32[]{:S(2)}) copy-start(s32[16,12]{1,0:T(8,128)} %param.12) | copy-start | bytes 2308
  14.4 16.5 %copy-start.19 = (f32[3]{0:T(128)S(1)}, f32[3]{0:T(128)}, u32[]{:S(2)}) copy-start(f32[3]{0:T(128)} %param.13) | copy-start | bytes 40
  16.6 25.4 %copy-start.17 = (bf16[16,12,256]{2,0,1:T(8,128)(2,1)S(1)}, bf16[16,12,256]{2,0,1:T(8,128)(2,1)}, u32[]{:S(2)}) copy-start(bf16[16,12,256]{2,0,1:T(8,128)(2,1)} %param.11) | copy-start | bytes 294916
  16.6 26.9 %copy-start.13 = (bf16[2,256,256]{2,1,0:T(8,128)(2,1)S(1)}, bf16[2,256,256]{2,1,0:T(8,128)(2,1)}, u32[]{:S(2)}) copy-start(bf16[2,256,256]{2,1,0:T(8,128)(2,1)} %project_ref.1) | copy-start | bytes 786436
  16.6 16.2 %collective-permute-start = (bf16[144,768]{1,0:T(8,128)(2,1)S(1)}, bf16[144,768]{1,0:T(8,128)(2,1)S(1)}, u32[]{:S(2)}, u32[]{:S(2)}) collective-permute-start(bf16[144,768]{1,0:T(8,128)(2,1)S(1)} %get-tuple-element.31), channel_id=1, source_target_pairs={{64,0},{96,32},{128,64},{160,96},{192,128},{224,160},{65,1},{97,33... | collective-permute-start | bytes 663560 | tf_op jit(solution)/shard_map/ppermute | solution.py:24
  18.0 14.8 %collective-permute-start.2 = (bf16[144,768]{1,0:T(8,128)(2,1)S(1)}, bf16[144,768]{1,0:T(8,128)(2,1)S(1)}, u32[]{:S(2)}, u32[]{:S(2)}) collective-permute-start(bf16[144,768]{1,0:T(8,128)(2,1)S(1)} %get-tuple-element.33), channel_id=1, source_target_pairs={{0,64},{32,96},{64,128},{96,160},{128,192},{160,224},{1,65},{33,97... | collective-permute-start | bytes 663560 | tf_op jit(solution)/shard_map/ppermute | solution.py:24
  22.6 8.7 %collective-permute-start.1 = (bf16[48,768]{1,0:T(8,128)(2,1)S(1)}, bf16[48,768]{1,0:T(8,128)(2,1)S(1)}, u32[]{:S(2)}, u32[]{:S(2)}) collective-permute-start(bf16[48,768]{1,0:T(8,128)(2,1)S(1)} %get-tuple-element.32), channel_id=1, source_target_pairs={{96,0},{128,32},{160,64},{192,96},{224,128},{97,1},{129,33},{161,6... | collective-permute-start | bytes 221192 | tf_op jit(solution)/shard_map/ppermute | solution.py:24
  23.9 8.9 %collective-permute-start.3 = (bf16[48,768]{1,0:T(8,128)(2,1)S(1)}, bf16[48,768]{1,0:T(8,128)(2,1)S(1)}, u32[]{:S(2)}, u32[]{:S(2)}) collective-permute-start(bf16[48,768]{1,0:T(8,128)(2,1)S(1)} %get-tuple-element.34), channel_id=1, source_target_pairs={{0,96},{32,128},{64,160},{96,192},{128,224},{1,97},{33,129},{65,16... | collective-permute-start | bytes 221192 | tf_op jit(solution)/shard_map/ppermute | solution.py:24
  32.9 9.2 %collective-permute-start.4 = (bf16[192,256]{1,0:T(8,128)(2,1)S(1)}, bf16[192,256]{1,0:T(8,128)(2,1)S(1)}, u32[]{:S(2)}, u32[]{:S(2)}) collective-permute-start(bf16[192,256]{1,0:T(8,128)(2,1)S(1)} %get-tuple-element.36), channel_id=1, source_target_pairs={{0,29},{1,30},{2,31},{3,0},{4,1},{5,2},{6,3},{7,4},{8,5},{9,6},{10... | collective-permute-start | bytes 294920 | tf_op jit(solution)/shard_map/ppermute | solution.py:28
  35.9 7.5 %collective-permute-start.5 = (bf16[192,256]{1,0:T(8,128)(2,1)S(1)}, bf16[192,256]{1,0:T(8,128)(2,1)S(1)}, u32[]{:S(2)}, u32[]{:S(2)}) collective-permute-start(bf16[192,256]{1,0:T(8,128)(2,1)S(1)} %get-tuple-element.37), channel_id=1, source_target_pairs={{0,3},{1,4},{2,5},{3,6},{4,7},{5,8},{6,9},{7,10},{8,11},{9,12},{10... | collective-permute-start | bytes 294920 | tf_op jit(solution)/shard_map/ppermute | solution.py:28
  37.1 20.8 %collective-permute-start.6 = (bf16[768,256]{1,0:T(8,128)(2,1)S(1)}, bf16[768,256]{1,0:T(8,128)(2,1)S(1)}, u32[]{:S(2)}, u32[]{:S(2)}) collective-permute-start(bf16[768,256]{1,0:T(8,128)(2,1)S(1)} %bitcast.12), channel_id=1, source_target_pairs={{0,29},{1,30},{2,31},{3,0},{4,1},{5,2},{6,3},{7,4},{8,5},{9,6},{10... | collective-permute-start | bytes 1179656 | tf_op jit(solution)/shard_map/ppermute | solution.py:28
  41.9 17.8 %collective-permute-start.8 = (bf16[768,256]{1,0:T(8,128)(2,1)S(1)}, bf16[768,256]{1,0:T(8,128)(2,1)S(1)}, u32[]{:S(2)}, u32[]{:S(2)}) collective-permute-start(bf16[768,256]{1,0:T(8,128)(2,1)S(1)} %bitcast.13), channel_id=1, source_target_pairs={{0,3},{1,4},{2,5},{3,6},{4,7},{5,8},{6,9},{7,10},{8,11},{9,12},{10... | collective-permute-start | bytes 1179656 | tf_op jit(solution)/shard_map/ppermute | solution.py:28
  42.0 19.0 %copy-start.16 = (s32[3]{0:T(128)}, s32[3]{0:T(128)S(1)}, u32[]{:S(2)}) copy-start(s32[3]{0:T(128)S(1)} %pad_add_fusion.place_ref) | copy-start | bytes 40
  45.1 28.4 %copy-start.3 = (bf16[192,512]{1,0:T(8,128)(2,1)}, bf16[192,512]{1,0:T(8,128)(2,1)S(1)}, u32[]{:S(2)}) copy-start(bf16[192,512]{1,0:T(8,128)(2,1)S(1)} %get-tuple-element.39.grads_ref) | copy-start | bytes 589828
  45.1 12.8 %collective-permute-start.7 = (bf16[320,512]{1,0:T(8,128)(2,1)S(1)}, bf16[320,512]{1,0:T(8,128)(2,1)S(1)}, u32[]{:S(2)}, u32[]{:S(2)}) collective-permute-start(bf16[320,512]{1,0:T(8,128)(2,1)S(1)} %get-tuple-element.40), channel_id=1, source_target_pairs={{0,32},{32,0},{1,33},{33,1},{2,34},{34,2},{3,35},{35,3},{4,36},{36... | collective-permute-start | bytes 983048 | tf_op jit(solution)/shard_map/ppermute | solution.py:680
  61.0 34.1 %all-to-all-start.1 = ((bf16[4,832,256]{2,1,0:T(8,128)(2,1)}), bf16[4,832,256]{2,1,0:T(8,128)(2,1)}, u32[]{:S(2)}, u32[]{:S(2)}) async-start(bf16[4,832,256]{2,1,0:T(8,128)(2,1)} %get-tuple-element.43), calls=%async_computation.1 | async-start | bytes 3407872 | tf_op jit(solution)/shard_map/all_to_all | solution.py:686
  70.2 24.8 %collective-permute-start.9 = (bf16[768,256]{1,0:T(8,128)(2,1)S(1)}, bf16[768,256]{1,0:T(8,128)(2,1)S(1)}, u32[]{:S(2)}, u32[]{:S(2)}) collective-permute-start(bf16[768,256]{1,0:T(8,128)(2,1)S(1)} %get-tuple-element.42), channel_id=1, source_target_pairs={{0,29},{1,30},{2,31},{3,0},{4,1},{5,2},{6,3},{7,4},{8,5},{9,6},{10... | collective-permute-start | bytes 1179656 | tf_op jit(solution)/shard_map/ppermute | solution.py:28
  73.5 21.5 %collective-permute-start.10 = (bf16[768,256]{1,0:T(8,128)(2,1)S(1)}, bf16[768,256]{1,0:T(8,128)(2,1)S(1)}, u32[]{:S(2)}, u32[]{:S(2)}) collective-permute-start(bf16[768,256]{1,0:T(8,128)(2,1)S(1)} %get-tuple-element.42), channel_id=1, source_target_pairs={{0,3},{1,4},{2,5},{3,6},{4,7},{5,8},{6,9},{7,10},{8,11},{9,12},{10... | collective-permute-start | bytes 1179656 | tf_op jit(solution)/shard_map/ppermute | solution.py:28
  73.5 21.5 %collective-permute-start.11 = (bf16[192,256]{1,0:T(8,128)(2,1)S(1)}, bf16[192,256]{1,0:T(8,128)(2,1)S(1)}, u32[]{:S(2)}, u32[]{:S(2)}) collective-permute-start(bf16[192,256]{1,0:T(8,128)(2,1)S(1)} %slice.20), channel_id=1, source_target_pairs={{0,3},{1,4},{2,5},{3,6},{4,7},{5,8},{6,9},{7,10},{8,11},{9,12},{10... | collective-permute-start | bytes 294920 | tf_op jit(solution)/shard_map/ppermute | solution.py:28
  73.6 21.4 %collective-permute-start.12 = (bf16[192,256]{1,0:T(8,128)(2,1)S(1)}, bf16[192,256]{1,0:T(8,128)(2,1)S(1)}, u32[]{:S(2)}, u32[]{:S(2)}) collective-permute-start(bf16[192,256]{1,0:T(8,128)(2,1)S(1)} %slice.20), channel_id=1, source_target_pairs={{0,29},{1,30},{2,31},{3,0},{4,1},{5,2},{6,3},{7,4},{8,5},{9,6},{10... | collective-permute-start | bytes 294920 | tf_op jit(solution)/shard_map/ppermute | solution.py:28
  103.5 2.6 %collective-permute-start.17 = (bf16[1536,256]{1,0:T(8,128)(2,1)}, bf16[1536,256]{1,0:T(8,128)(2,1)S(1)}, u32[]{:S(2)}, u32[]{:S(2)}) collective-permute-start(bf16[1536,256]{1,0:T(8,128)(2,1)} %get-tuple-element.50), channel_id=1, source_target_pairs={{0,1},{1,0},{2,3},{3,2},{4,5},{5,4},{6,7},{7,6},{8,9},{9,8},{10,11... | collective-permute-start | bytes 2359304 | tf_op jit(solution)/shard_map/ppermute | solution.py:700
  108.4 25.3 %all-to-all-start.2 = ((bf16[16,82,256]{2,1,0:T(8,128)(2,1)}), bf16[16,82,256]{2,1,0:T(8,128)(2,1)S(1)}, u32[]{:S(2)}, u32[]{:S(2)}) async-start(bf16[16,82,256]{2,1,0:T(8,128)(2,1)} %shard_map.102), calls=%async_computation.2 | async-start | bytes 1441792 | tf_op jit(solution)/shard_map/all_to_all | solution.py:708
  113.7 15.9 %collective-permute-start.13 = (bf16[144,512]{1,0:T(8,128)(2,1)S(1)}, bf16[144,512]{1,0:T(8,128)(2,1)S(1)}, u32[]{:S(2)}, u32[]{:S(2)}) collective-permute-start(bf16[144,512]{1,0:T(8,128)(2,1)S(1)} %get-tuple-element.45), channel_id=1, source_target_pairs={{64,0},{96,32},{128,64},{160,96},{192,128},{224,160},{65,1},{97,33... | collective-permute-start | bytes 442376 | tf_op jit(solution)/shard_map/ppermute | solution.py:24
  115.0 14.6 %collective-permute-start.15 = (bf16[144,512]{1,0:T(8,128)(2,1)S(1)}, bf16[144,512]{1,0:T(8,128)(2,1)S(1)}, u32[]{:S(2)}, u32[]{:S(2)}) collective-permute-start(bf16[144,512]{1,0:T(8,128)(2,1)S(1)} %get-tuple-element.47), channel_id=1, source_target_pairs={{0,64},{32,96},{64,128},{96,160},{128,192},{160,224},{1,65},{33,97... | collective-permute-start | bytes 442376 | tf_op jit(solution)/shard_map/ppermute | solution.py:24
  119.6 9.0 %collective-permute-start.14 = (bf16[48,512]{1,0:T(8,128)(2,1)S(1)}, bf16[48,512]{1,0:T(8,128)(2,1)S(1)}, u32[]{:S(2)}, u32[]{:S(2)}) collective-permute-start(bf16[48,512]{1,0:T(8,128)(2,1)S(1)} %get-tuple-element.46), channel_id=1, source_target_pairs={{96,0},{128,32},{160,64},{192,96},{224,128},{97,1},{129,33},{161,6... | collective-permute-start | bytes 147464 | tf_op jit(solution)/shard_map/ppermute | solution.py:24
  120.9 8.7 %collective-permute-start.16 = (bf16[48,512]{1,0:T(8,128)(2,1)S(1)}, bf16[48,512]{1,0:T(8,128)(2,1)S(1)}, u32[]{:S(2)}, u32[]{:S(2)}) collective-permute-start(bf16[48,512]{1,0:T(8,128)(2,1)S(1)} %get-tuple-element.48), channel_id=1, source_target_pairs={{0,96},{32,128},{64,160},{96,192},{128,224},{1,97},{33,129},{65,16... | collective-permute-start | bytes 147464 | tf_op jit(solution)/shard_map/ppermute | solution.py:24
  128.6 13.4 %copy-start.14 = (bf16[48,512]{1,0:T(8,128)(2,1)}, bf16[48,512]{1,0:T(8,128)(2,1)S(1)}, u32[]{:S(2)}) copy-start(bf16[48,512]{1,0:T(8,128)(2,1)S(1)} %collective-permute-done.14.up_far_ref.refs_1_) | copy-start | bytes 147460
  129.6 12.4 %copy-start.15 = (bf16[48,512]{1,0:T(8,128)(2,1)}, bf16[48,512]{1,0:T(8,128)(2,1)S(1)}, u32[]{:S(2)}) copy-start(bf16[48,512]{1,0:T(8,128)(2,1)S(1)} %collective-permute-done.16.down_far_ref.refs_3_) | copy-start | bytes 147460
  129.6 12.4 %copy-start.5 = (bf16[144,512]{1,0:T(8,128)(2,1)}, bf16[144,512]{1,0:T(8,128)(2,1)S(1)}, u32[]{:S(2)}) copy-start(bf16[144,512]{1,0:T(8,128)(2,1)S(1)} %collective-permute-done.13.up_near_ref.refs_0_) | copy-start | bytes 442372
  129.6 12.4 %copy-start.6 = (bf16[144,512]{1,0:T(8,128)(2,1)}, bf16[144,512]{1,0:T(8,128)(2,1)S(1)}, u32[]{:S(2)}) copy-start(bf16[144,512]{1,0:T(8,128)(2,1)S(1)} %collective-permute-done.15.down_near_ref.refs_2_) | copy-start | bytes 442372
  134.6 16.8 %all-to-all-start.3 = ((bf16[8,82,256]{2,1,0:T(8,128)(2,1)}), bf16[8,82,256]{2,1,0:T(8,128)(2,1)S(1)}, u32[]{:S(2)}, u32[]{:S(2)}) async-start(bf16[8,82,256]{2,1,0:T(8,128)(2,1)} %shard_map.103), calls=%async_computation.3 | async-start | bytes 720896 | tf_op jit(solution)/shard_map/all_to_all | solution.py:710
  (12 other events, 36.3 us)

commit v5 on v4

--- a/solution.py
+++ b/solution.py
@@ -303,12 +303,9 @@
     grads_ref,
     received_ref,
     mine_ref,
-    after_east_ref,
-    after_west_ref,
-    features_in_ref,
-    message_ref,
-    features_out_ref,
+    *refs,
 ):
+    message_ref = refs[-2]
     count, part, width = mine_ref.shape
     pixels = grads_ref.shape[0]
     for at in range(count):
@@ -333,9 +330,9 @@
             like((count, 4 * pixels + part, width), jnp.bfloat16),
             like(features.shape, features.dtype),
         ),
-        in_specs=[VMEM] * 3 + [ANY] * 3,
+        in_specs=[VMEM] * 3 + [ANY] * 5,
         out_specs=(VMEM, ANY),
-        input_output_aliases={5: 1},
+        input_output_aliases={7: 1},
         compiler_params=params(),
         cost_estimate=cost(mine.size, 8 * received.size),
     )(grads, received, mine, *after, features)
@@ -351,8 +348,6 @@
     west_first_ref,
     west_second_ref,
     message_in_ref,
-    after_east_ref,
-    after_west_ref,
     kept_ref,
     rounded_ref,
     windows_ref,
@@ -451,7 +446,7 @@
     return (chunk + 15) // 16 * 16
 
 
-def weight_terms(span, place, features, message, after):
+def weight_terms(span, place, features, message):
     total, width = features[0].shape
     pixels = total // LAT_COUNT
     chunk = (10 * width + message.shape[1] - 4 * pixels) // LON_COUNT
@@ -463,7 +458,7 @@
             like(terms_shape, jnp.bfloat16),
             like((pixels, 3 * width), jnp.bfloat16),
         ),
-        in_specs=[SMEM] + [ANY] * 8,
+        in_specs=[SMEM] + [ANY] * 6,
         out_specs=(VMEM,) * 3,
         scratch_shapes=[
             pltpu.VMEM((2 * span + total, 4 * width), jnp.bfloat16),
@@ -474,7 +469,7 @@
         ],
         compiler_params=params(60),
         cost_estimate=cost(20 * total * width * width, 8 * 2**20),
-    )(place, *features, message, *after)
+    )(place, *features, message)
 
 
 def pair_sum_kernel(kept_ref, received_ref, out_ref):
@@ -680,21 +675,20 @@
     other = lax.ppermute(message, "xh", [(0, 1), (1, 0)])
     first_east = shift_columns(first_features, -tiles_over)
     first_west = shift_columns(first_features, tiles_over)
+    east_grad = shift_columns(grads[:, :width], tiles_over)
+    west_grad = shift_columns(grads[:, :width], -tiles_over)
     message, second_features = forward(
-        grads, other, mine, (first_east, first_west), second_features
+        grads, other, mine, (first_east, first_west, east_grad, west_grad), second_features
     )
     gathered = lax.all_to_all(message, "y", 0, 0)
     second_east = shift_columns(second_features, -tiles_over)
     second_west = shift_columns(second_features, tiles_over)
-    east_grad = shift_columns(grads[:, :width], tiles_over)
-    west_grad = shift_columns(grads[:, :width], -tiles_over)
 
     kept, sent, windows = weight_terms(
         span,
         place,
         (column_features, first_east, second_east, first_west, second_west),
         gathered,
-        (east_grad, west_grad),
     )
     chunk = (10 * in_width + 2 * width) // (LAT_COUNT * LON_COUNT)
     chip_sum = pair_sum(kept, lax.ppermute(sent, "c", [(0, 1), (1, 0)]), chunk)

time: 153 us -> 153 us (level)
    ppermute x8, waiting for transfers between devices: 19.6 us -> 27.5 us  [shift_columns(): lax.ppermute(value, LON, [(i, (i + by) % LON_COUNT) for i in range(LON_CO...]
    ppermute x1, waiting for transfers between devices: 7.71 us -> 0.01 us  [shards(): other = lax.ppermute(message, 'xh', [(0, 1), (1, 0)])]
    all_to_all x1, starting transfers between devices: 5.23 us -> 8.63 us  [shards(): pieces = lax.all_to_all(chip_sum, ('xl', 'z'), 0, 0)]
    all_to_all x1, starting transfers between devices: 7.44 us -> 5.12 us  [shards(): lax.all_to_all(piece_sum(pieces, side_rows), LAT, 0, 0)]
    unnamed x45 -> x41, local copies, waits for them, and re-layouts: 7.34 us -> 7.16 us
where the time goes in v5:
time: 153 us; the launch traced here: 152 us
  starting transfers between devices  78.1 us (51%)
  waiting for transfers between devices  39.6 us (26%)
  Pallas kernels  24.9 us (16%)
  local copies, waits for them, and re-layouts  8.45 us (6%)
    ppermute x8, starting transfers between devices, shift_rows(): return lax.ppermute(value, LAT, pairs)  28.3 us
    ppermute x8, waiting for transfers between devices, shift_columns(): lax.ppermute(value, LON, [(i, (i + by) % LON_COUNT) for i in range(LON_CO...  27.5 us
    ppermute x8, starting transfers between devices, shift_columns(): lax.ppermute(value, LON, [(i, (i + by) % LON_COUNT) for i in range(LON_CO...  14.7 us
    all_to_all x1, starting transfers between devices, shards(): gathered = lax.all_to_all(message, 'y', 0, 0)  9.19 us
    all_to_all x1, starting transfers between devices, shards(): pieces = lax.all_to_all(chip_sum, ('xl', 'z'), 0, 0)  8.63 us
    pallas_call x1, Pallas kernels, weight_terms(): pl.pallas_call(functools.partial(weight_terms_kernel, span, chunk), out_s...  7.43 us
    pallas_call x1, Pallas kernels, input_gradient(): pl.pallas_call(input_gradient_kernel, out_shape=like((pixels // rows, row...  7.37 us
    unnamed x41, local copies, waits for them, and re-layouts  7.16 us
  transfers between devices with their start and end apart: 22, of which 11 were waited for; matrix products, arithmetic and copies ran while one was open for 1% of the time, Pallas kernels for 7%

profile of v5, /device:TPU:32, one launch (start us, length us, event | category | flops | bytes accessed | tf_op | source)
XLA Modules:
  0.0 152.1 jit_solution(14433355759174187639)
XLA Ops:
  1.9 1.9 %shard_map.94 = (bf16[192,2048]{1,0:T(8,128)(2,1)S(1)}, bf16[8,192,256]{2,1,0:T(8,128)(2,1)}) custom-call(bf16[12,16,2048]{2,1,0:T(8,128)(2,1)S(1)} %bitcast.10), custom_call_target="tpu_custom_call" | custom-call | flops 201326592 | bytes 2359296 | tf_op jit(solution)/shard_map/pallas_call | solution.py:164
  3.8 6.9 %all-to-all-start = ((bf16[8,192,256]{2,1,0:T(8,128)(2,1)}), bf16[8,192,256]{2,1,0:T(8,128)(2,1)}, u32[]{:S(2)}, u32[]{:S(2)}) async-start(bf16[8,192,256]{2,1,0:T(8,128)(2,1)} %get-tuple-element.28.after_ref), calls=%async_computation | async-start | bytes 1572864 | tf_op jit(solution)/shard_map/all_to_all | solution.py:653
  10.7 3.7 %copy-done = bf16[9,2048,256]{2,1,0:T(8,128)(2,1)S(1)} copy-done((bf16[9,2048,256]{2,1,0:T(8,128)(2,1)S(1)}, bf16[9,2048,256]{2,1,0:T(8,128)(2,1)}, u32[]{:S(2)}) %copy-start) | copy-done | bytes 9437208
  14.4 2.2 %shard_map.95 = (bf16[144,768]{1,0:T(8,128)(2,1)S(1)}, bf16[48,768]{1,0:T(8,128)(2,1)S(1)}, bf16[144,768]{1,0:T(8,128)(2,1)S(1)}, bf16[48,768]{1,0:T(8,128)(2,1)...) custom-call(bf16[192,2048]{1,0:T(8,128)(2,1)S(1)} %get-tuple-element.27.flat_ref, ...), custom_call_target="tpu_custom_call" | custom-call | flops 2013265920 | bytes 10485760 | tf_op jit(solution)/shard_map/pallas_call | solution.py:125
  16.6 1.4 collective-permute-start
  18.0 4.6 %collective-permute-start.2 = (bf16[144,768]{1,0:T(8,128)(2,1)S(1)}, bf16[144,768]{1,0:T(8,128)(2,1)S(1)}, u32[]{:S(2)}, u32[]{:S(2)}) collective-permute-start(bf16[144,768]{1,0:T(8,128)(2,1)S(1)} %get-tuple-element.33), channel_id=1, source_target_pairs={{0,64},{32,96},{64,128},{96,160},{128,192},{160,224},{1,65},{33,97... | collective-permute-start | bytes 663560 | tf_op jit(solution)/shard_map/ppermute | solution.py:24
  22.6 1.3 collective-permute-start.1
  23.9 7.0 %collective-permute-start.3 = (bf16[48,768]{1,0:T(8,128)(2,1)S(1)}, bf16[48,768]{1,0:T(8,128)(2,1)S(1)}, u32[]{:S(2)}, u32[]{:S(2)}) collective-permute-start(bf16[48,768]{1,0:T(8,128)(2,1)S(1)} %get-tuple-element.34), channel_id=1, source_target_pairs={{0,96},{32,128},{64,160},{96,192},{128,224},{1,97},{33,129},{65,16... | collective-permute-start | bytes 221192 | tf_op jit(solution)/shard_map/ppermute | solution.py:24
  31.3 1.6 %collective-permute-done.3.above_far_ref = bf16[48,768]{1,0:T(8,128)(2,1)S(1)} collective-permute-done((bf16[48,768]{1,0:T(8,128)(2,1)S(1)}, bf16[48,768]{1,0:T(8,128)(2,1)S(1)}, u32[]{:S(2)}, u32[]{:S(2)}) %collective-permute-start.3) | collective-permute-done | bytes 73760 | tf_op jit(solution)/shard_map/ppermute | solution.py:24
  32.9 3.0 %collective-permute-start.4 = (bf16[192,256]{1,0:T(8,128)(2,1)S(1)}, bf16[192,256]{1,0:T(8,128)(2,1)S(1)}, u32[]{:S(2)}, u32[]{:S(2)}) collective-permute-start(bf16[192,256]{1,0:T(8,128)(2,1)S(1)} %get-tuple-element.36), channel_id=1, source_target_pairs={{0,29},{1,30},{2,31},{3,0},{4,1},{5,2},{6,3},{7,4},{8,5},{9,6},{10... | collective-permute-start | bytes 294920 | tf_op jit(solution)/shard_map/ppermute | solution.py:28
  37.1 4.8 %collective-permute-start.6 = (bf16[768,256]{1,0:T(8,128)(2,1)S(1)}, bf16[768,256]{1,0:T(8,128)(2,1)S(1)}, u32[]{:S(2)}, u32[]{:S(2)}) collective-permute-start(bf16[768,256]{1,0:T(8,128)(2,1)S(1)} %bitcast.12), channel_id=1, source_target_pairs={{0,29},{1,30},{2,31},{3,0},{4,1},{5,2},{6,3},{7,4},{8,5},{9,6},{10... | collective-permute-start | bytes 1179656 | tf_op jit(solution)/shard_map/ppermute | solution.py:28
  43.5 1.6 %shard_map.97 = (bf16[12,16,256]{2,1,0:T(8,128)(2,1)}, bf16[192,512]{1,0:T(8,128)(2,1)S(1)}, bf16[320,512]{1,0:T(8,128)(2,1)S(1)}, f32[4,64,256]{2,1,0:T(8,128)S(1)}) custom-call(s32[3]{0:T(128)S(1)} %pad_add_fusion.place_ref, f32[192,256]{1,0:T(8,128)S(1)} %get-tuple-element.29.point_ref, f32[192,256]{1,0:T(8,128)S(1)} %get-tuple-element.35.center_ref, ...), custom_call_target="tpu_custom_call" | custom-call | flops 150994944 | bytes 1179648 | tf_op jit(solution)/shard_map/pallas_call | solution.py:286
  45.1 5.1 %collective-permute-start.7 = (bf16[320,512]{1,0:T(8,128)(2,1)S(1)}, bf16[320,512]{1,0:T(8,128)(2,1)S(1)}, u32[]{:S(2)}, u32[]{:S(2)}) collective-permute-start(bf16[320,512]{1,0:T(8,128)(2,1)S(1)} %get-tuple-element.40), channel_id=1, source_target_pairs={{0,32},{32,0},{1,33},{33,1},{2,34},{34,2},{3,35},{35,3},{4,36},{36... | collective-permute-start | bytes 983048 | tf_op jit(solution)/shard_map/ppermute | solution.py:675
  51.0 4.0 %collective-permute-start.10 = (bf16[192,256]{1,0:T(8,128)(2,1)S(1)}, bf16[192,256]{1,0:T(8,128)(2,1)S(1)}, u32[]{:S(2)}, u32[]{:S(2)}) collective-permute-start(bf16[192,256]{1,0:T(8,128)(2,1)S(1)} %slice.18), channel_id=1, source_target_pairs={{0,29},{1,30},{2,31},{3,0},{4,1},{5,2},{6,3},{7,4},{8,5},{9,6},{10... | collective-permute-start | bytes 294920 | tf_op jit(solution)/shard_map/ppermute | solution.py:28
  55.0 7.8 %collective-permute-done.9.refs_2_.east_grad_ref.east_ref = bf16[192,256]{1,0:T(8,128)(2,1)S(1)} collective-permute-done((bf16[192,256]{1,0:T(8,128)(2,1)S(1)}, bf16[192,256]{1,0:T(8,128)(2,1)S(1)}, u32[]{:S(2)}, u32[]{:S(2)}) %collective-permute-start.9) | collective-permute-done | bytes 98336 | tf_op jit(solution)/shard_map/ppermute | solution.py:28
  62.9 1.4 shard_map.98
  64.4 9.2 %all-to-all-start.1 = ((bf16[4,832,256]{2,1,0:T(8,128)(2,1)}), bf16[4,832,256]{2,1,0:T(8,128)(2,1)}, u32[]{:S(2)}, u32[]{:S(2)}) async-start(bf16[4,832,256]{2,1,0:T(8,128)(2,1)} %get-tuple-element.43), calls=%async_computation.1 | async-start | bytes 3407872 | tf_op jit(solution)/shard_map/all_to_all | solution.py:683
  73.6 2.1 %collective-permute-start.11 = (bf16[768,256]{1,0:T(8,128)(2,1)S(1)}, bf16[768,256]{1,0:T(8,128)(2,1)S(1)}, u32[]{:S(2)}, u32[]{:S(2)}) collective-permute-start(bf16[768,256]{1,0:T(8,128)(2,1)S(1)} %get-tuple-element.42), channel_id=1, source_target_pairs={{0,29},{1,30},{2,31},{3,0},{4,1},{5,2},{6,3},{7,4},{8,5},{9,6},{10... | collective-permute-start | bytes 1179656 | tf_op jit(solution)/shard_map/ppermute | solution.py:28
  75.6 12.4 %collective-permute-done.11.east_second_ref = bf16[768,256]{1,0:T(8,128)(2,1)S(1)} collective-permute-done((bf16[768,256]{1,0:T(8,128)(2,1)S(1)}, bf16[768,256]{1,0:T(8,128)(2,1)S(1)}, u32[]{:S(2)}, u32[]{:S(2)}) %collective-permute-start.11) | collective-permute-done | bytes 393248 | tf_op jit(solution)/shard_map/ppermute | solution.py:28
  88.1 5.9 %collective-permute-done.12.west_second_ref = bf16[768,256]{1,0:T(8,128)(2,1)S(1)} collective-permute-done((bf16[768,256]{1,0:T(8,128)(2,1)S(1)}, bf16[768,256]{1,0:T(8,128)(2,1)S(1)}, u32[]{:S(2)}, u32[]{:S(2)}) %collective-permute-start.12) | collective-permute-done | bytes 393248 | tf_op jit(solution)/shard_map/ppermute | solution.py:28
  94.7 7.4 %shard_map.99 = (f32[1536,256]{1,0:T(8,128)}, bf16[1536,256]{1,0:T(8,128)(2,1)}, bf16[192,768]{1,0:T(8,128)(2,1)}) custom-call(s32[3]{0:T(128)} %copy-done.14, bf16[1536,256]{1,0:T(8,128)(2,1)} %bitcast.5.center_in_ref, bf16[768,256]{1,0:T(8,128)(2,1)} %copy-done.9, bf16[768,256]{1,0:T(8,128)(2,1)} %copy-done.18, bf16[768,256]{1,0:T(8,128)(2,1)} %copy-done.10, ...), custom_call_target="tpu_custom_call" | custom-call | flops 2013265920 | bytes 8388608 | tf_op jit(solution)/shard_map/pallas_call | solution.py:454
  102.2 2.5 %collective-permute-done.17.received_ref = bf16[1536,256]{1,0:T(8,128)(2,1)S(1)} collective-permute-done((bf16[1536,256]{1,0:T(8,128)(2,1)}, bf16[1536,256]{1,0:T(8,128)(2,1)S(1)}, u32[]{:S(2)}, u32[]{:S(2)}) %collective-permute-start.17) | collective-permute-done | bytes 786464 | tf_op jit(solution)/shard_map/ppermute | solution.py:694
  104.7 1.4 copy-done.2
  107.1 8.6 %all-to-all-start.2 = ((bf16[16,82,256]{2,1,0:T(8,128)(2,1)}), bf16[16,82,256]{2,1,0:T(8,128)(2,1)S(1)}, u32[]{:S(2)}, u32[]{:S(2)}) async-start(bf16[16,82,256]{2,1,0:T(8,128)(2,1)} %shard_map.102), calls=%async_computation.2 | async-start | bytes 1441792 | tf_op jit(solution)/shard_map/all_to_all | solution.py:702
  115.8 1.3 collective-permute-start.13
  117.1 4.6 %collective-permute-start.15 = (bf16[144,512]{1,0:T(8,128)(2,1)S(1)}, bf16[144,512]{1,0:T(8,128)(2,1)S(1)}, u32[]{:S(2)}, u32[]{:S(2)}) collective-permute-start(bf16[144,512]{1,0:T(8,128)(2,1)S(1)} %get-tuple-element.47), channel_id=1, source_target_pairs={{0,64},{32,96},{64,128},{96,160},{128,192},{160,224},{1,65},{33,97... | collective-permute-start | bytes 442376 | tf_op jit(solution)/shard_map/ppermute | solution.py:24
  121.7 1.3 collective-permute-start.14
  123.0 7.0 %collective-permute-start.16 = (bf16[48,512]{1,0:T(8,128)(2,1)S(1)}, bf16[48,512]{1,0:T(8,128)(2,1)S(1)}, u32[]{:S(2)}, u32[]{:S(2)}) collective-permute-start(bf16[48,512]{1,0:T(8,128)(2,1)S(1)} %get-tuple-element.48), channel_id=1, source_target_pairs={{0,96},{32,128},{64,160},{96,192},{128,224},{1,97},{33,129},{65,16... | collective-permute-start | bytes 147464 | tf_op jit(solution)/shard_map/ppermute | solution.py:24
  131.7 4.1 %all-to-all-done.2.pieces_ref = bf16[16,82,256]{2,1,0:T(8,128)(2,1)S(1)} async-done(((bf16[16,82,256]{2,1,0:T(8,128)(2,1)}), bf16[16,82,256]{2,1,0:T(8,128)(2,1)S(1)}, u32[]{:S(2)}, u32[]{:S(2)}) %all-to-all-start.2) | async-done | bytes 671776 | tf_op jit(solution)/shard_map/all_to_all | solution.py:702
  136.6 5.1 %all-to-all-start.3 = ((bf16[8,82,256]{2,1,0:T(8,128)(2,1)}), bf16[8,82,256]{2,1,0:T(8,128)(2,1)S(1)}, u32[]{:S(2)}, u32[]{:S(2)}) async-start(bf16[8,82,256]{2,1,0:T(8,128)(2,1)} %shard_map.103), calls=%async_computation.3 | async-start | bytes 720896 | tf_op jit(solution)/shard_map/all_to_all | solution.py:704
  141.8 7.4 %shard_map.101 = bf16[12,16,2048]{2,1,0:T(8,128)(2,1)} custom-call(bf16[192,768]{1,0:T(8,128)(2,1)} %get-tuple-element.44.windows_ref, bf16[192,512]{1,0:T(8,128)(2,1)} %copy-done.3, bf16[192,256]{1,0:T(8,128)(2,1)} %copy-done.4, bf16[192,256]{1,0:T(8,128)(2,1)} %copy-done.5, bf16[144,512]{1,0:T(8,128)(2,1)} %copy-done.7, bf16[48,512]{1,0:T(8,128)(2,1)} %copy-done.12, ...), custom_call_target="tpu_custom_call" | custom-call | flops 2013265920 | bytes 20971520 | tf_op jit(solution)/shard_map/pallas_call | solution.py:620
  149.2 1.9 %all-to-all-done.3.parts_ref = bf16[8,82,256]{2,1,0:T(8,128)(2,1)S(1)} async-done(((bf16[8,82,256]{2,1,0:T(8,128)(2,1)}), bf16[8,82,256]{2,1,0:T(8,128)(2,1)S(1)}, u32[]{:S(2)}, u32[]{:S(2)}) %all-to-all-start.3) | async-done | bytes 335904 | tf_op jit(solution)/shard_map/all_to_all | solution.py:704
  (70 shorter events, 10.8 us)
Async XLA Ops:
  3.8 32.2 %all-to-all-start = ((bf16[8,192,256]{2,1,0:T(8,128)(2,1)}), bf16[8,192,256]{2,1,0:T(8,128)(2,1)}, u32[]{:S(2)}, u32[]{:S(2)}) async-start(bf16[8,192,256]{2,1,0:T(8,128)(2,1)} %get-tuple-element.28.after_ref), calls=%async_computation | async-start | bytes 1572864 | tf_op jit(solution)/shard_map/all_to_all | solution.py:653
  14.4 16.5 %copy-start.16 = (s32[16,12]{1,0:T(8,128)S(1)}, s32[16,12]{1,0:T(8,128)}, u32[]{:S(2)}) copy-start(s32[16,12]{1,0:T(8,128)} %param.12) | copy-start | bytes 2308
  14.4 16.5 %copy-start.17 = (f32[3]{0:T(128)S(1)}, f32[3]{0:T(128)}, u32[]{:S(2)}) copy-start(f32[3]{0:T(128)} %param.13) | copy-start | bytes 40
  16.6 25.4 %copy-start.15 = (bf16[16,12,256]{2,0,1:T(8,128)(2,1)S(1)}, bf16[16,12,256]{2,0,1:T(8,128)(2,1)}, u32[]{:S(2)}) copy-start(bf16[16,12,256]{2,0,1:T(8,128)(2,1)} %param.11) | copy-start | bytes 294916
  16.6 26.9 %copy-start.11 = (bf16[2,256,256]{2,1,0:T(8,128)(2,1)S(1)}, bf16[2,256,256]{2,1,0:T(8,128)(2,1)}, u32[]{:S(2)}) copy-start(bf16[2,256,256]{2,1,0:T(8,128)(2,1)} %project_ref.1) | copy-start | bytes 786436
  16.6 16.2 %collective-permute-start = (bf16[144,768]{1,0:T(8,128)(2,1)S(1)}, bf16[144,768]{1,0:T(8,128)(2,1)S(1)}, u32[]{:S(2)}, u32[]{:S(2)}) collective-permute-start(bf16[144,768]{1,0:T(8,128)(2,1)S(1)} %get-tuple-element.31), channel_id=1, source_target_pairs={{64,0},{96,32},{128,64},{160,96},{192,128},{224,160},{65,1},{97,33... | collective-permute-start | bytes 663560 | tf_op jit(solution)/shard_map/ppermute | solution.py:24
  18.0 14.8 %collective-permute-start.2 = (bf16[144,768]{1,0:T(8,128)(2,1)S(1)}, bf16[144,768]{1,0:T(8,128)(2,1)S(1)}, u32[]{:S(2)}, u32[]{:S(2)}) collective-permute-start(bf16[144,768]{1,0:T(8,128)(2,1)S(1)} %get-tuple-element.33), channel_id=1, source_target_pairs={{0,64},{32,96},{64,128},{96,160},{128,192},{160,224},{1,65},{33,97... | collective-permute-start | bytes 663560 | tf_op jit(solution)/shard_map/ppermute | solution.py:24
  22.6 8.7 %collective-permute-start.1 = (bf16[48,768]{1,0:T(8,128)(2,1)S(1)}, bf16[48,768]{1,0:T(8,128)(2,1)S(1)}, u32[]{:S(2)}, u32[]{:S(2)}) collective-permute-start(bf16[48,768]{1,0:T(8,128)(2,1)S(1)} %get-tuple-element.32), channel_id=1, source_target_pairs={{96,0},{128,32},{160,64},{192,96},{224,128},{97,1},{129,33},{161,6... | collective-permute-start | bytes 221192 | tf_op jit(solution)/shard_map/ppermute | solution.py:24
  23.9 8.9 %collective-permute-start.3 = (bf16[48,768]{1,0:T(8,128)(2,1)S(1)}, bf16[48,768]{1,0:T(8,128)(2,1)S(1)}, u32[]{:S(2)}, u32[]{:S(2)}) collective-permute-start(bf16[48,768]{1,0:T(8,128)(2,1)S(1)} %get-tuple-element.34), channel_id=1, source_target_pairs={{0,96},{32,128},{64,160},{96,192},{128,224},{1,97},{33,129},{65,16... | collective-permute-start | bytes 221192 | tf_op jit(solution)/shard_map/ppermute | solution.py:24
  32.9 9.2 %collective-permute-start.4 = (bf16[192,256]{1,0:T(8,128)(2,1)S(1)}, bf16[192,256]{1,0:T(8,128)(2,1)S(1)}, u32[]{:S(2)}, u32[]{:S(2)}) collective-permute-start(bf16[192,256]{1,0:T(8,128)(2,1)S(1)} %get-tuple-element.36), channel_id=1, source_target_pairs={{0,29},{1,30},{2,31},{3,0},{4,1},{5,2},{6,3},{7,4},{8,5},{9,6},{10... | collective-permute-start | bytes 294920 | tf_op jit(solution)/shard_map/ppermute | solution.py:28
  35.9 7.5 %collective-permute-start.5 = (bf16[192,256]{1,0:T(8,128)(2,1)S(1)}, bf16[192,256]{1,0:T(8,128)(2,1)S(1)}, u32[]{:S(2)}, u32[]{:S(2)}) collective-permute-start(bf16[192,256]{1,0:T(8,128)(2,1)S(1)} %get-tuple-element.37), channel_id=1, source_target_pairs={{0,3},{1,4},{2,5},{3,6},{4,7},{5,8},{6,9},{7,10},{8,11},{9,12},{10... | collective-permute-start | bytes 294920 | tf_op jit(solution)/shard_map/ppermute | solution.py:28
  37.1 25.8 %collective-permute-start.6 = (bf16[768,256]{1,0:T(8,128)(2,1)S(1)}, bf16[768,256]{1,0:T(8,128)(2,1)S(1)}, u32[]{:S(2)}, u32[]{:S(2)}) collective-permute-start(bf16[768,256]{1,0:T(8,128)(2,1)S(1)} %bitcast.12), channel_id=1, source_target_pairs={{0,29},{1,30},{2,31},{3,0},{4,1},{5,2},{6,3},{7,4},{8,5},{9,6},{10... | collective-permute-start | bytes 1179656 | tf_op jit(solution)/shard_map/ppermute | solution.py:28
  41.9 21.0 %collective-permute-start.8 = (bf16[768,256]{1,0:T(8,128)(2,1)S(1)}, bf16[768,256]{1,0:T(8,128)(2,1)S(1)}, u32[]{:S(2)}, u32[]{:S(2)}) collective-permute-start(bf16[768,256]{1,0:T(8,128)(2,1)S(1)} %bitcast.13), channel_id=1, source_target_pairs={{0,3},{1,4},{2,5},{3,6},{4,7},{5,8},{6,9},{7,10},{8,11},{9,12},{10... | collective-permute-start | bytes 1179656 | tf_op jit(solution)/shard_map/ppermute | solution.py:28
  42.0 22.3 %copy-start.14 = (s32[3]{0:T(128)}, s32[3]{0:T(128)S(1)}, u32[]{:S(2)}) copy-start(s32[3]{0:T(128)S(1)} %pad_add_fusion.place_ref) | copy-start | bytes 40
  45.1 19.3 %copy-start.3 = (bf16[192,512]{1,0:T(8,128)(2,1)}, bf16[192,512]{1,0:T(8,128)(2,1)S(1)}, u32[]{:S(2)}) copy-start(bf16[192,512]{1,0:T(8,128)(2,1)S(1)} %get-tuple-element.39.grads_ref) | copy-start | bytes 589828
  45.1 17.8 %collective-permute-start.7 = (bf16[320,512]{1,0:T(8,128)(2,1)S(1)}, bf16[320,512]{1,0:T(8,128)(2,1)S(1)}, u32[]{:S(2)}, u32[]{:S(2)}) collective-permute-start(bf16[320,512]{1,0:T(8,128)(2,1)S(1)} %get-tuple-element.40), channel_id=1, source_target_pairs={{0,32},{32,0},{1,33},{33,1},{2,34},{34,2},{3,35},{35,3},{4,36},{36... | collective-permute-start | bytes 983048 | tf_op jit(solution)/shard_map/ppermute | solution.py:675
  50.2 12.7 %collective-permute-start.9 = (bf16[192,256]{1,0:T(8,128)(2,1)S(1)}, bf16[192,256]{1,0:T(8,128)(2,1)S(1)}, u32[]{:S(2)}, u32[]{:S(2)}) collective-permute-start(bf16[192,256]{1,0:T(8,128)(2,1)S(1)} %slice.18), channel_id=1, source_target_pairs={{0,3},{1,4},{2,5},{3,6},{4,7},{5,8},{6,9},{7,10},{8,11},{9,12},{10... | collective-permute-start | bytes 294920 | tf_op jit(solution)/shard_map/ppermute | solution.py:28
  51.0 11.8 %collective-permute-start.10 = (bf16[192,256]{1,0:T(8,128)(2,1)S(1)}, bf16[192,256]{1,0:T(8,128)(2,1)S(1)}, u32[]{:S(2)}, u32[]{:S(2)}) collective-permute-start(bf16[192,256]{1,0:T(8,128)(2,1)S(1)} %slice.18), channel_id=1, source_target_pairs={{0,29},{1,30},{2,31},{3,0},{4,1},{5,2},{6,3},{7,4},{8,5},{9,6},{10... | collective-permute-start | bytes 294920 | tf_op jit(solution)/shard_map/ppermute | solution.py:28
  62.9 52.9 %copy-start.4 = (bf16[192,256]{1,0:T(8,128)(2,1)}, bf16[192,256]{1,0:T(8,128)(2,1)S(1)}, u32[]{:S(2)}) copy-start(bf16[192,256]{1,0:T(8,128)(2,1)S(1)} %collective-permute-done.9.refs_2_.east_grad_ref.east_ref) | copy-start | bytes 294916
  62.9 52.9 %copy-start.5 = (bf16[192,256]{1,0:T(8,128)(2,1)}, bf16[192,256]{1,0:T(8,128)(2,1)S(1)}, u32[]{:S(2)}) copy-start(bf16[192,256]{1,0:T(8,128)(2,1)S(1)} %collective-permute-done.10.refs_3_.west_grad_ref.west_ref) | copy-start | bytes 294916
  64.4 29.6 %all-to-all-start.1 = ((bf16[4,832,256]{2,1,0:T(8,128)(2,1)}), bf16[4,832,256]{2,1,0:T(8,128)(2,1)}, u32[]{:S(2)}, u32[]{:S(2)}) async-start(bf16[4,832,256]{2,1,0:T(8,128)(2,1)} %get-tuple-element.43), calls=%async_computation.1 | async-start | bytes 3407872 | tf_op jit(solution)/shard_map/all_to_all | solution.py:683
  73.6 14.5 %collective-permute-start.11 = (bf16[768,256]{1,0:T(8,128)(2,1)S(1)}, bf16[768,256]{1,0:T(8,128)(2,1)S(1)}, u32[]{:S(2)}, u32[]{:S(2)}) collective-permute-start(bf16[768,256]{1,0:T(8,128)(2,1)S(1)} %get-tuple-element.42), channel_id=1, source_target_pairs={{0,29},{1,30},{2,31},{3,0},{4,1},{5,2},{6,3},{7,4},{8,5},{9,6},{10... | collective-permute-start | bytes 1179656 | tf_op jit(solution)/shard_map/ppermute | solution.py:28
  75.6 18.3 %collective-permute-start.12 = (bf16[768,256]{1,0:T(8,128)(2,1)S(1)}, bf16[768,256]{1,0:T(8,128)(2,1)S(1)}, u32[]{:S(2)}, u32[]{:S(2)}) collective-permute-start(bf16[768,256]{1,0:T(8,128)(2,1)S(1)} %get-tuple-element.42), channel_id=1, source_target_pairs={{0,3},{1,4},{2,5},{3,6},{4,7},{5,8},{6,9},{7,10},{8,11},{9,12},{10... | collective-permute-start | bytes 1179656 | tf_op jit(solution)/shard_map/ppermute | solution.py:28
  102.1 2.6 %collective-permute-start.17 = (bf16[1536,256]{1,0:T(8,128)(2,1)}, bf16[1536,256]{1,0:T(8,128)(2,1)S(1)}, u32[]{:S(2)}, u32[]{:S(2)}) collective-permute-start(bf16[1536,256]{1,0:T(8,128)(2,1)} %get-tuple-element.50), channel_id=1, source_target_pairs={{0,1},{1,0},{2,3},{3,2},{4,5},{5,4},{6,7},{7,6},{8,9},{9,8},{10,11... | collective-permute-start | bytes 2359304 | tf_op jit(solution)/shard_map/ppermute | solution.py:694
  107.1 28.7 %all-to-all-start.2 = ((bf16[16,82,256]{2,1,0:T(8,128)(2,1)}), bf16[16,82,256]{2,1,0:T(8,128)(2,1)S(1)}, u32[]{:S(2)}, u32[]{:S(2)}) async-start(bf16[16,82,256]{2,1,0:T(8,128)(2,1)} %shard_map.102), calls=%async_computation.2 | async-start | bytes 1441792 | tf_op jit(solution)/shard_map/all_to_all | solution.py:702
  115.8 15.9 %collective-permute-start.13 = (bf16[144,512]{1,0:T(8,128)(2,1)S(1)}, bf16[144,512]{1,0:T(8,128)(2,1)S(1)}, u32[]{:S(2)}, u32[]{:S(2)}) collective-permute-start(bf16[144,512]{1,0:T(8,128)(2,1)S(1)} %get-tuple-element.45), channel_id=1, source_target_pairs={{64,0},{96,32},{128,64},{160,96},{192,128},{224,160},{65,1},{97,33... | collective-permute-start | bytes 442376 | tf_op jit(solution)/shard_map/ppermute | solution.py:24
  117.1 14.6 %collective-permute-start.15 = (bf16[144,512]{1,0:T(8,128)(2,1)S(1)}, bf16[144,512]{1,0:T(8,128)(2,1)S(1)}, u32[]{:S(2)}, u32[]{:S(2)}) collective-permute-start(bf16[144,512]{1,0:T(8,128)(2,1)S(1)} %get-tuple-element.47), channel_id=1, source_target_pairs={{0,64},{32,96},{64,128},{96,160},{128,192},{160,224},{1,65},{33,97... | collective-permute-start | bytes 442376 | tf_op jit(solution)/shard_map/ppermute | solution.py:24
  121.7 8.9 %collective-permute-start.14 = (bf16[48,512]{1,0:T(8,128)(2,1)S(1)}, bf16[48,512]{1,0:T(8,128)(2,1)S(1)}, u32[]{:S(2)}, u32[]{:S(2)}) collective-permute-start(bf16[48,512]{1,0:T(8,128)(2,1)S(1)} %get-tuple-element.46), channel_id=1, source_target_pairs={{96,0},{128,32},{160,64},{192,96},{224,128},{97,1},{129,33},{161,6... | collective-permute-start | bytes 147464 | tf_op jit(solution)/shard_map/ppermute | solution.py:24
  123.0 8.7 %collective-permute-start.16 = (bf16[48,512]{1,0:T(8,128)(2,1)S(1)}, bf16[48,512]{1,0:T(8,128)(2,1)S(1)}, u32[]{:S(2)}, u32[]{:S(2)}) collective-permute-start(bf16[48,512]{1,0:T(8,128)(2,1)S(1)} %get-tuple-element.48), channel_id=1, source_target_pairs={{0,96},{32,128},{64,160},{96,192},{128,224},{1,97},{33,129},{65,16... | collective-permute-start | bytes 147464 | tf_op jit(solution)/shard_map/ppermute | solution.py:24
  130.5 11.2 %copy-start.12 = (bf16[48,512]{1,0:T(8,128)(2,1)}, bf16[48,512]{1,0:T(8,128)(2,1)S(1)}, u32[]{:S(2)}) copy-start(bf16[48,512]{1,0:T(8,128)(2,1)S(1)} %collective-permute-done.14.up_far_ref.refs_1_) | copy-start | bytes 147460
  131.7 10.1 %copy-start.8 = (bf16[144,512]{1,0:T(8,128)(2,1)}, bf16[144,512]{1,0:T(8,128)(2,1)S(1)}, u32[]{:S(2)}) copy-start(bf16[144,512]{1,0:T(8,128)(2,1)S(1)} %collective-permute-done.15.down_near_ref.refs_2_) | copy-start | bytes 442372
  136.6 14.4 %all-to-all-start.3 = ((bf16[8,82,256]{2,1,0:T(8,128)(2,1)}), bf16[8,82,256]{2,1,0:T(8,128)(2,1)S(1)}, u32[]{:S(2)}, u32[]{:S(2)}) async-start(bf16[8,82,256]{2,1,0:T(8,128)(2,1)} %shard_map.103), calls=%async_computation.3 | async-start | bytes 720896 | tf_op jit(solution)/shard_map/all_to_all | solution.py:704
  (10 other events, 46.1 us)

commit v6 on v5

--- a/solution.py
+++ b/solution.py
@@ -348,12 +348,13 @@
     west_first_ref,
     west_second_ref,
     message_in_ref,
-    kept_ref,
-    rounded_ref,
+    rounded_kept_ref,
+    rounded_sent_ref,
     windows_ref,
     framed_ref,
     features_ref,
     message_ref,
+    kept_ref,
     sent_ref,
     semaphores,
 ):
@@ -439,7 +440,8 @@
             project_rows = jnp.sum(message_ref[:, 4 * pixels :, :].astype(jnp.float32), axis=0)
             store(9 * width, project_rows)
             store(9 * width + project_rows.shape[0], product[:, 3 * width :])
-    rounded_ref[...] = sent_ref[...].astype(rounded_ref.dtype)
+    rounded_kept_ref[...] = kept_ref[...].astype(rounded_kept_ref.dtype)
+    rounded_sent_ref[...] = sent_ref[...].astype(rounded_sent_ref.dtype)
 
 
 def padded(chunk):
@@ -454,7 +456,7 @@
     return pl.pallas_call(
         functools.partial(weight_terms_kernel, span, chunk),
         out_shape=(
-            like(terms_shape, jnp.float32),
+            like(terms_shape, jnp.bfloat16),
             like(terms_shape, jnp.bfloat16),
             like((pixels, 3 * width), jnp.bfloat16),
         ),
@@ -465,6 +467,7 @@
             pltpu.VMEM((3, total, width), jnp.bfloat16),
             pltpu.VMEM(message.shape, jnp.bfloat16),
             pltpu.VMEM(terms_shape, jnp.float32),
+            pltpu.VMEM(terms_shape, jnp.float32),
             pltpu.SemaphoreType.DMA((6,)),
         ],
         compiler_params=params(60),
@@ -477,7 +480,9 @@
     room = kept_ref.shape[0] // count
     for at in range(count):
         rows = slice(room * at, room * (at + 1))
-        total = kept_ref[rows, :] + received_ref[rows, :].astype(jnp.float32)
+        total = kept_ref[rows, :].astype(jnp.float32) + received_ref[rows, :].astype(
+            jnp.float32
+        )
         out_ref[at] = total[:chunk].astype(jnp.bfloat16)
 
 

time: 153 us -> 153 us (level)
  no operation moved by 1% of the time
where the time goes in v6:
time: 153 us; the launch traced here: 152 us
  starting transfers between devices  78.1 us (51%)
  waiting for transfers between devices  39.6 us (26%)
  Pallas kernels  24.8 us (16%)
  local copies, waits for them, and re-layouts  8.17 us (5%)
    ppermute x8, starting transfers between devices, shift_rows(): return lax.ppermute(value, LAT, pairs)  28.3 us
    ppermute x8, waiting for transfers between devices, shift_columns(): lax.ppermute(value, LON, [(i, (i + by) % LON_COUNT) for i in range(LON_CO...  27.5 us
    ppermute x8, starting transfers between devices, shift_columns(): lax.ppermute(value, LON, [(i, (i + by) % LON_COUNT) for i in range(LON_CO...  14.7 us
    all_to_all x1, starting transfers between devices, shards(): gathered = lax.all_to_all(message, 'y', 0, 0)  9.19 us
    all_to_all x1, starting transfers between devices, shards(): pieces = lax.all_to_all(chip_sum, ('xl', 'z'), 0, 0)  8.63 us
    pallas_call x1, Pallas kernels, input_gradient(): pl.pallas_call(input_gradient_kernel, out_shape=like((pixels // rows, row...  7.37 us
    pallas_call x1, Pallas kernels, weight_terms(): pl.pallas_call(functools.partial(weight_terms_kernel, span, chunk), out_s...  7.25 us
    all_to_all x1, starting transfers between devices, shards(): lax.all_to_all(slices, LAT, 0, 0).reshape(LAT_COUNT * pixels, -1)  6.93 us
  transfers between devices with their start and end apart: 22, of which 11 were waited for; matrix products, arithmetic and copies ran while one was open for 1% of the time, Pallas kernels for 7%

profile of v6, /device:TPU:32, one launch (start us, length us, event | category | flops | bytes accessed | tf_op | source)
XLA Modules:
  0.0 151.7 jit_solution(14542053776801985535)
XLA Ops:
  1.9 1.9 %shard_map.94 = (bf16[192,2048]{1,0:T(8,128)(2,1)S(1)}, bf16[8,192,256]{2,1,0:T(8,128)(2,1)}) custom-call(bf16[12,16,2048]{2,1,0:T(8,128)(2,1)S(1)} %bitcast.10), custom_call_target="tpu_custom_call" | custom-call | flops 201326592 | bytes 2359296 | tf_op jit(solution)/shard_map/pallas_call | solution.py:164
  3.8 6.9 %all-to-all-start = ((bf16[8,192,256]{2,1,0:T(8,128)(2,1)}), bf16[8,192,256]{2,1,0:T(8,128)(2,1)}, u32[]{:S(2)}, u32[]{:S(2)}) async-start(bf16[8,192,256]{2,1,0:T(8,128)(2,1)} %get-tuple-element.28.after_ref), calls=%async_computation | async-start | bytes 1572864 | tf_op jit(solution)/shard_map/all_to_all | solution.py:658
  10.7 3.7 %copy-done = bf16[9,2048,256]{2,1,0:T(8,128)(2,1)S(1)} copy-done((bf16[9,2048,256]{2,1,0:T(8,128)(2,1)S(1)}, bf16[9,2048,256]{2,1,0:T(8,128)(2,1)}, u32[]{:S(2)}) %copy-start) | copy-done | bytes 9437208
  14.4 2.2 %shard_map.95 = (bf16[144,768]{1,0:T(8,128)(2,1)S(1)}, bf16[48,768]{1,0:T(8,128)(2,1)S(1)}, bf16[144,768]{1,0:T(8,128)(2,1)S(1)}, bf16[48,768]{1,0:T(8,128)(2,1)...) custom-call(bf16[192,2048]{1,0:T(8,128)(2,1)S(1)} %get-tuple-element.27.flat_ref, ...), custom_call_target="tpu_custom_call" | custom-call | flops 2013265920 | bytes 10485760 | tf_op jit(solution)/shard_map/pallas_call | solution.py:125
  16.6 1.4 collective-permute-start
  18.0 4.6 %collective-permute-start.2 = (bf16[144,768]{1,0:T(8,128)(2,1)S(1)}, bf16[144,768]{1,0:T(8,128)(2,1)S(1)}, u32[]{:S(2)}, u32[]{:S(2)}) collective-permute-start(bf16[144,768]{1,0:T(8,128)(2,1)S(1)} %get-tuple-element.33), channel_id=1, source_target_pairs={{0,64},{32,96},{64,128},{96,160},{128,192},{160,224},{1,65},{33,97... | collective-permute-start | bytes 663560 | tf_op jit(solution)/shard_map/ppermute | solution.py:24
  22.6 1.3 collective-permute-start.1
  23.9 7.0 %collective-permute-start.3 = (bf16[48,768]{1,0:T(8,128)(2,1)S(1)}, bf16[48,768]{1,0:T(8,128)(2,1)S(1)}, u32[]{:S(2)}, u32[]{:S(2)}) collective-permute-start(bf16[48,768]{1,0:T(8,128)(2,1)S(1)} %get-tuple-element.34), channel_id=1, source_target_pairs={{0,96},{32,128},{64,160},{96,192},{128,224},{1,97},{33,129},{65,16... | collective-permute-start | bytes 221192 | tf_op jit(solution)/shard_map/ppermute | solution.py:24
  31.3 1.6 %collective-permute-done.3.above_far_ref = bf16[48,768]{1,0:T(8,128)(2,1)S(1)} collective-permute-done((bf16[48,768]{1,0:T(8,128)(2,1)S(1)}, bf16[48,768]{1,0:T(8,128)(2,1)S(1)}, u32[]{:S(2)}, u32[]{:S(2)}) %collective-permute-start.3) | collective-permute-done | bytes 73760 | tf_op jit(solution)/shard_map/ppermute | solution.py:24
  32.9 3.0 %collective-permute-start.4 = (bf16[192,256]{1,0:T(8,128)(2,1)S(1)}, bf16[192,256]{1,0:T(8,128)(2,1)S(1)}, u32[]{:S(2)}, u32[]{:S(2)}) collective-permute-start(bf16[192,256]{1,0:T(8,128)(2,1)S(1)} %get-tuple-element.36), channel_id=1, source_target_pairs={{0,29},{1,30},{2,31},{3,0},{4,1},{5,2},{6,3},{7,4},{8,5},{9,6},{10... | collective-permute-start | bytes 294920 | tf_op jit(solution)/shard_map/ppermute | solution.py:28
  37.1 4.8 %collective-permute-start.6 = (bf16[768,256]{1,0:T(8,128)(2,1)S(1)}, bf16[768,256]{1,0:T(8,128)(2,1)S(1)}, u32[]{:S(2)}, u32[]{:S(2)}) collective-permute-start(bf16[768,256]{1,0:T(8,128)(2,1)S(1)} %bitcast.12), channel_id=1, source_target_pairs={{0,29},{1,30},{2,31},{3,0},{4,1},{5,2},{6,3},{7,4},{8,5},{9,6},{10... | collective-permute-start | bytes 1179656 | tf_op jit(solution)/shard_map/ppermute | solution.py:28
  42.2 1.3 collective-permute-done.5.from_west_ref
  43.5 1.6 %shard_map.97 = (bf16[12,16,256]{2,1,0:T(8,128)(2,1)}, bf16[192,512]{1,0:T(8,128)(2,1)S(1)}, bf16[320,512]{1,0:T(8,128)(2,1)S(1)}, f32[4,64,256]{2,1,0:T(8,128)S(1)}) custom-call(s32[3]{0:T(128)S(1)} %pad_add_fusion.place_ref, f32[192,256]{1,0:T(8,128)S(1)} %get-tuple-element.29.point_ref, f32[192,256]{1,0:T(8,128)S(1)} %get-tuple-element.35.center_ref, ...), custom_call_target="tpu_custom_call" | custom-call | flops 150994944 | bytes 1179648 | tf_op jit(solution)/shard_map/pallas_call | solution.py:286
  45.1 5.1 %collective-permute-start.7 = (bf16[320,512]{1,0:T(8,128)(2,1)S(1)}, bf16[320,512]{1,0:T(8,128)(2,1)S(1)}, u32[]{:S(2)}, u32[]{:S(2)}) collective-permute-start(bf16[320,512]{1,0:T(8,128)(2,1)S(1)} %get-tuple-element.40), channel_id=1, source_target_pairs={{0,32},{32,0},{1,33},{33,1},{2,34},{34,2},{3,35},{35,3},{4,36},{36... | collective-permute-start | bytes 983048 | tf_op jit(solution)/shard_map/ppermute | solution.py:680
  51.0 4.0 %collective-permute-start.10 = (bf16[192,256]{1,0:T(8,128)(2,1)S(1)}, bf16[192,256]{1,0:T(8,128)(2,1)S(1)}, u32[]{:S(2)}, u32[]{:S(2)}) collective-permute-start(bf16[192,256]{1,0:T(8,128)(2,1)S(1)} %slice.18), channel_id=1, source_target_pairs={{0,29},{1,30},{2,31},{3,0},{4,1},{5,2},{6,3},{7,4},{8,5},{9,6},{10... | collective-permute-start | bytes 294920 | tf_op jit(solution)/shard_map/ppermute | solution.py:28
  55.0 7.8 %collective-permute-done.9.refs_2_.east_grad_ref.east_ref = bf16[192,256]{1,0:T(8,128)(2,1)S(1)} collective-permute-done((bf16[192,256]{1,0:T(8,128)(2,1)S(1)}, bf16[192,256]{1,0:T(8,128)(2,1)S(1)}, u32[]{:S(2)}, u32[]{:S(2)}) %collective-permute-start.9) | collective-permute-done | bytes 98336 | tf_op jit(solution)/shard_map/ppermute | solution.py:28
  62.9 1.4 shard_map.98
  64.4 9.2 %all-to-all-start.1 = ((bf16[4,832,256]{2,1,0:T(8,128)(2,1)}), bf16[4,832,256]{2,1,0:T(8,128)(2,1)}, u32[]{:S(2)}, u32[]{:S(2)}) async-start(bf16[4,832,256]{2,1,0:T(8,128)(2,1)} %get-tuple-element.43), calls=%async_computation.1 | async-start | bytes 3407872 | tf_op jit(solution)/shard_map/all_to_all | solution.py:688
  73.6 2.1 %collective-permute-start.11 = (bf16[768,256]{1,0:T(8,128)(2,1)S(1)}, bf16[768,256]{1,0:T(8,128)(2,1)S(1)}, u32[]{:S(2)}, u32[]{:S(2)}) collective-permute-start(bf16[768,256]{1,0:T(8,128)(2,1)S(1)} %get-tuple-element.42), channel_id=1, source_target_pairs={{0,29},{1,30},{2,31},{3,0},{4,1},{5,2},{6,3},{7,4},{8,5},{9,6},{10... | collective-permute-start | bytes 1179656 | tf_op jit(solution)/shard_map/ppermute | solution.py:28
  75.6 12.4 %collective-permute-done.11.east_second_ref = bf16[768,256]{1,0:T(8,128)(2,1)S(1)} collective-permute-done((bf16[768,256]{1,0:T(8,128)(2,1)S(1)}, bf16[768,256]{1,0:T(8,128)(2,1)S(1)}, u32[]{:S(2)}, u32[]{:S(2)}) %collective-permute-start.11) | collective-permute-done | bytes 393248 | tf_op jit(solution)/shard_map/ppermute | solution.py:28
  88.1 5.9 %collective-permute-done.12.west_second_ref = bf16[768,256]{1,0:T(8,128)(2,1)S(1)} collective-permute-done((bf16[768,256]{1,0:T(8,128)(2,1)S(1)}, bf16[768,256]{1,0:T(8,128)(2,1)S(1)}, u32[]{:S(2)}, u32[]{:S(2)}) %collective-permute-start.12) | collective-permute-done | bytes 393248 | tf_op jit(solution)/shard_map/ppermute | solution.py:28
  94.7 7.3 %shard_map.99 = (bf16[1536,256]{1,0:T(8,128)(2,1)}, bf16[1536,256]{1,0:T(8,128)(2,1)}, bf16[192,768]{1,0:T(8,128)(2,1)}) custom-call(s32[3]{0:T(128)} %copy-done.14, bf16[1536,256]{1,0:T(8,128)(2,1)} %bitcast.5.center_in_ref, bf16[768,256]{1,0:T(8,128)(2,1)} %copy-done.9, bf16[768,256]{1,0:T(8,128)(2,1)} %copy-done.18, bf16[768,256]{1,0:T(8,128)(2,1)} %copy-done.10, ...), custom_call_target="tpu_custom_call" | custom-call | flops 2013265920 | bytes 8388608 | tf_op jit(solution)/shard_map/pallas_call | solution.py:456
  102.1 2.5 %collective-permute-done.17.received_ref = bf16[1536,256]{1,0:T(8,128)(2,1)S(1)} collective-permute-done((bf16[1536,256]{1,0:T(8,128)(2,1)}, bf16[1536,256]{1,0:T(8,128)(2,1)S(1)}, u32[]{:S(2)}, u32[]{:S(2)}) %collective-permute-start.17) | collective-permute-done | bytes 786464 | tf_op jit(solution)/shard_map/ppermute | solution.py:699
  106.7 8.6 %all-to-all-start.2 = ((bf16[16,82,256]{2,1,0:T(8,128)(2,1)}), bf16[16,82,256]{2,1,0:T(8,128)(2,1)S(1)}, u32[]{:S(2)}, u32[]{:S(2)}) async-start(bf16[16,82,256]{2,1,0:T(8,128)(2,1)} %shard_map.102), calls=%async_computation.2 | async-start | bytes 1441792 | tf_op jit(solution)/shard_map/all_to_all | solution.py:707
  115.4 1.3 collective-permute-start.13
  116.7 4.6 %collective-permute-start.15 = (bf16[144,512]{1,0:T(8,128)(2,1)S(1)}, bf16[144,512]{1,0:T(8,128)(2,1)S(1)}, u32[]{:S(2)}, u32[]{:S(2)}) collective-permute-start(bf16[144,512]{1,0:T(8,128)(2,1)S(1)} %get-tuple-element.47), channel_id=1, source_target_pairs={{0,64},{32,96},{64,128},{96,160},{128,192},{160,224},{1,65},{33,97... | collective-permute-start | bytes 442376 | tf_op jit(solution)/shard_map/ppermute | solution.py:24
  121.3 1.3 collective-permute-start.14
  122.6 7.0 %collective-permute-start.16 = (bf16[48,512]{1,0:T(8,128)(2,1)S(1)}, bf16[48,512]{1,0:T(8,128)(2,1)S(1)}, u32[]{:S(2)}, u32[]{:S(2)}) collective-permute-start(bf16[48,512]{1,0:T(8,128)(2,1)S(1)} %get-tuple-element.48), channel_id=1, source_target_pairs={{0,96},{32,128},{64,160},{96,192},{128,224},{1,97},{33,129},{65,16... | collective-permute-start | bytes 147464 | tf_op jit(solution)/shard_map/ppermute | solution.py:24
  131.3 4.1 %all-to-all-done.2.pieces_ref = bf16[16,82,256]{2,1,0:T(8,128)(2,1)S(1)} async-done(((bf16[16,82,256]{2,1,0:T(8,128)(2,1)}), bf16[16,82,256]{2,1,0:T(8,128)(2,1)S(1)}, u32[]{:S(2)}, u32[]{:S(2)}) %all-to-all-start.2) | async-done | bytes 671776 | tf_op jit(solution)/shard_map/all_to_all | solution.py:707
  136.2 5.1 %all-to-all-start.3 = ((bf16[8,82,256]{2,1,0:T(8,128)(2,1)}), bf16[8,82,256]{2,1,0:T(8,128)(2,1)S(1)}, u32[]{:S(2)}, u32[]{:S(2)}) async-start(bf16[8,82,256]{2,1,0:T(8,128)(2,1)} %shard_map.103), calls=%async_computation.3 | async-start | bytes 720896 | tf_op jit(solution)/shard_map/all_to_all | solution.py:709
  141.4 7.4 %shard_map.101 = bf16[12,16,2048]{2,1,0:T(8,128)(2,1)} custom-call(bf16[192,768]{1,0:T(8,128)(2,1)} %get-tuple-element.44.windows_ref, bf16[192,512]{1,0:T(8,128)(2,1)} %copy-done.2, bf16[192,256]{1,0:T(8,128)(2,1)} %copy-done.3, bf16[192,256]{1,0:T(8,128)(2,1)} %copy-done.4, bf16[144,512]{1,0:T(8,128)(2,1)} %copy-done.7, bf16[48,512]{1,0:T(8,128)(2,1)} %copy-done.12, ...), custom_call_target="tpu_custom_call" | custom-call | flops 2013265920 | bytes 20971520 | tf_op jit(solution)/shard_map/pallas_call | solution.py:625
  148.8 1.9 %all-to-all-done.3.parts_ref = bf16[8,82,256]{2,1,0:T(8,128)(2,1)S(1)} async-done(((bf16[8,82,256]{2,1,0:T(8,128)(2,1)}), bf16[8,82,256]{2,1,0:T(8,128)(2,1)S(1)}, u32[]{:S(2)}, u32[]{:S(2)}) %all-to-all-start.3) | async-done | bytes 335904 | tf_op jit(solution)/shard_map/all_to_all | solution.py:709
  (70 shorter events, 10.7 us)
Async XLA Ops:
  3.8 32.2 %all-to-all-start = ((bf16[8,192,256]{2,1,0:T(8,128)(2,1)}), bf16[8,192,256]{2,1,0:T(8,128)(2,1)}, u32[]{:S(2)}, u32[]{:S(2)}) async-start(bf16[8,192,256]{2,1,0:T(8,128)(2,1)} %get-tuple-element.28.after_ref), calls=%async_computation | async-start | bytes 1572864 | tf_op jit(solution)/shard_map/all_to_all | solution.py:658
  14.4 16.5 %copy-start.16 = (s32[16,12]{1,0:T(8,128)S(1)}, s32[16,12]{1,0:T(8,128)}, u32[]{:S(2)}) copy-start(s32[16,12]{1,0:T(8,128)} %param.12) | copy-start | bytes 2308
  14.4 16.5 %copy-start.17 = (f32[3]{0:T(128)S(1)}, f32[3]{0:T(128)}, u32[]{:S(2)}) copy-start(f32[3]{0:T(128)} %param.13) | copy-start | bytes 40
  16.6 25.4 %copy-start.15 = (bf16[16,12,256]{2,0,1:T(8,128)(2,1)S(1)}, bf16[16,12,256]{2,0,1:T(8,128)(2,1)}, u32[]{:S(2)}) copy-start(bf16[16,12,256]{2,0,1:T(8,128)(2,1)} %param.11) | copy-start | bytes 294916
  16.6 26.9 %copy-start.11 = (bf16[2,256,256]{2,1,0:T(8,128)(2,1)S(1)}, bf16[2,256,256]{2,1,0:T(8,128)(2,1)}, u32[]{:S(2)}) copy-start(bf16[2,256,256]{2,1,0:T(8,128)(2,1)} %project_ref.1) | copy-start | bytes 786436
  16.6 16.2 %collective-permute-start = (bf16[144,768]{1,0:T(8,128)(2,1)S(1)}, bf16[144,768]{1,0:T(8,128)(2,1)S(1)}, u32[]{:S(2)}, u32[]{:S(2)}) collective-permute-start(bf16[144,768]{1,0:T(8,128)(2,1)S(1)} %get-tuple-element.31), channel_id=1, source_target_pairs={{64,0},{96,32},{128,64},{160,96},{192,128},{224,160},{65,1},{97,33... | collective-permute-start | bytes 663560 | tf_op jit(solution)/shard_map/ppermute | solution.py:24
  18.0 14.8 %collective-permute-start.2 = (bf16[144,768]{1,0:T(8,128)(2,1)S(1)}, bf16[144,768]{1,0:T(8,128)(2,1)S(1)}, u32[]{:S(2)}, u32[]{:S(2)}) collective-permute-start(bf16[144,768]{1,0:T(8,128)(2,1)S(1)} %get-tuple-element.33), channel_id=1, source_target_pairs={{0,64},{32,96},{64,128},{96,160},{128,192},{160,224},{1,65},{33,97... | collective-permute-start | bytes 663560 | tf_op jit(solution)/shard_map/ppermute | solution.py:24
  22.6 8.7 %collective-permute-start.1 = (bf16[48,768]{1,0:T(8,128)(2,1)S(1)}, bf16[48,768]{1,0:T(8,128)(2,1)S(1)}, u32[]{:S(2)}, u32[]{:S(2)}) collective-permute-start(bf16[48,768]{1,0:T(8,128)(2,1)S(1)} %get-tuple-element.32), channel_id=1, source_target_pairs={{96,0},{128,32},{160,64},{192,96},{224,128},{97,1},{129,33},{161,6... | collective-permute-start | bytes 221192 | tf_op jit(solution)/shard_map/ppermute | solution.py:24
  23.9 8.9 %collective-permute-start.3 = (bf16[48,768]{1,0:T(8,128)(2,1)S(1)}, bf16[48,768]{1,0:T(8,128)(2,1)S(1)}, u32[]{:S(2)}, u32[]{:S(2)}) collective-permute-start(bf16[48,768]{1,0:T(8,128)(2,1)S(1)} %get-tuple-element.34), channel_id=1, source_target_pairs={{0,96},{32,128},{64,160},{96,192},{128,224},{1,97},{33,129},{65,16... | collective-permute-start | bytes 221192 | tf_op jit(solution)/shard_map/ppermute | solution.py:24
  32.9 9.2 %collective-permute-start.4 = (bf16[192,256]{1,0:T(8,128)(2,1)S(1)}, bf16[192,256]{1,0:T(8,128)(2,1)S(1)}, u32[]{:S(2)}, u32[]{:S(2)}) collective-permute-start(bf16[192,256]{1,0:T(8,128)(2,1)S(1)} %get-tuple-element.36), channel_id=1, source_target_pairs={{0,29},{1,30},{2,31},{3,0},{4,1},{5,2},{6,3},{7,4},{8,5},{9,6},{10... | collective-permute-start | bytes 294920 | tf_op jit(solution)/shard_map/ppermute | solution.py:28
  35.9 7.5 %collective-permute-start.5 = (bf16[192,256]{1,0:T(8,128)(2,1)S(1)}, bf16[192,256]{1,0:T(8,128)(2,1)S(1)}, u32[]{:S(2)}, u32[]{:S(2)}) collective-permute-start(bf16[192,256]{1,0:T(8,128)(2,1)S(1)} %get-tuple-element.37), channel_id=1, source_target_pairs={{0,3},{1,4},{2,5},{3,6},{4,7},{5,8},{6,9},{7,10},{8,11},{9,12},{10... | collective-permute-start | bytes 294920 | tf_op jit(solution)/shard_map/ppermute | solution.py:28
  37.1 25.8 %collective-permute-start.6 = (bf16[768,256]{1,0:T(8,128)(2,1)S(1)}, bf16[768,256]{1,0:T(8,128)(2,1)S(1)}, u32[]{:S(2)}, u32[]{:S(2)}) collective-permute-start(bf16[768,256]{1,0:T(8,128)(2,1)S(1)} %bitcast.12), channel_id=1, source_target_pairs={{0,29},{1,30},{2,31},{3,0},{4,1},{5,2},{6,3},{7,4},{8,5},{9,6},{10... | collective-permute-start | bytes 1179656 | tf_op jit(solution)/shard_map/ppermute | solution.py:28
  41.9 21.0 %collective-permute-start.8 = (bf16[768,256]{1,0:T(8,128)(2,1)S(1)}, bf16[768,256]{1,0:T(8,128)(2,1)S(1)}, u32[]{:S(2)}, u32[]{:S(2)}) collective-permute-start(bf16[768,256]{1,0:T(8,128)(2,1)S(1)} %bitcast.13), channel_id=1, source_target_pairs={{0,3},{1,4},{2,5},{3,6},{4,7},{5,8},{6,9},{7,10},{8,11},{9,12},{10... | collective-permute-start | bytes 1179656 | tf_op jit(solution)/shard_map/ppermute | solution.py:28
  42.0 22.3 %copy-start.14 = (s32[3]{0:T(128)}, s32[3]{0:T(128)S(1)}, u32[]{:S(2)}) copy-start(s32[3]{0:T(128)S(1)} %pad_add_fusion.place_ref) | copy-start | bytes 40
  45.1 19.3 %copy-start.2 = (bf16[192,512]{1,0:T(8,128)(2,1)}, bf16[192,512]{1,0:T(8,128)(2,1)S(1)}, u32[]{:S(2)}) copy-start(bf16[192,512]{1,0:T(8,128)(2,1)S(1)} %get-tuple-element.39.grads_ref) | copy-start | bytes 589828
  45.1 17.8 %collective-permute-start.7 = (bf16[320,512]{1,0:T(8,128)(2,1)S(1)}, bf16[320,512]{1,0:T(8,128)(2,1)S(1)}, u32[]{:S(2)}, u32[]{:S(2)}) collective-permute-start(bf16[320,512]{1,0:T(8,128)(2,1)S(1)} %get-tuple-element.40), channel_id=1, source_target_pairs={{0,32},{32,0},{1,33},{33,1},{2,34},{34,2},{3,35},{35,3},{4,36},{36... | collective-permute-start | bytes 983048 | tf_op jit(solution)/shard_map/ppermute | solution.py:680
  50.2 12.7 %collective-permute-start.9 = (bf16[192,256]{1,0:T(8,128)(2,1)S(1)}, bf16[192,256]{1,0:T(8,128)(2,1)S(1)}, u32[]{:S(2)}, u32[]{:S(2)}) collective-permute-start(bf16[192,256]{1,0:T(8,128)(2,1)S(1)} %slice.18), channel_id=1, source_target_pairs={{0,3},{1,4},{2,5},{3,6},{4,7},{5,8},{6,9},{7,10},{8,11},{9,12},{10... | collective-permute-start | bytes 294920 | tf_op jit(solution)/shard_map/ppermute | solution.py:28
  51.0 11.8 %collective-permute-start.10 = (bf16[192,256]{1,0:T(8,128)(2,1)S(1)}, bf16[192,256]{1,0:T(8,128)(2,1)S(1)}, u32[]{:S(2)}, u32[]{:S(2)}) collective-permute-start(bf16[192,256]{1,0:T(8,128)(2,1)S(1)} %slice.18), channel_id=1, source_target_pairs={{0,29},{1,30},{2,31},{3,0},{4,1},{5,2},{6,3},{7,4},{8,5},{9,6},{10... | collective-permute-start | bytes 294920 | tf_op jit(solution)/shard_map/ppermute | solution.py:28
  62.9 52.5 %copy-start.3 = (bf16[192,256]{1,0:T(8,128)(2,1)}, bf16[192,256]{1,0:T(8,128)(2,1)S(1)}, u32[]{:S(2)}) copy-start(bf16[192,256]{1,0:T(8,128)(2,1)S(1)} %collective-permute-done.9.refs_2_.east_grad_ref.east_ref) | copy-start | bytes 294916
  62.9 52.5 %copy-start.4 = (bf16[192,256]{1,0:T(8,128)(2,1)}, bf16[192,256]{1,0:T(8,128)(2,1)S(1)}, u32[]{:S(2)}) copy-start(bf16[192,256]{1,0:T(8,128)(2,1)S(1)} %collective-permute-done.10.refs_3_.west_grad_ref.west_ref) | copy-start | bytes 294916
  64.4 29.6 %all-to-all-start.1 = ((bf16[4,832,256]{2,1,0:T(8,128)(2,1)}), bf16[4,832,256]{2,1,0:T(8,128)(2,1)}, u32[]{:S(2)}, u32[]{:S(2)}) async-start(bf16[4,832,256]{2,1,0:T(8,128)(2,1)} %get-tuple-element.43), calls=%async_computation.1 | async-start | bytes 3407872 | tf_op jit(solution)/shard_map/all_to_all | solution.py:688
  73.6 14.5 %collective-permute-start.11 = (bf16[768,256]{1,0:T(8,128)(2,1)S(1)}, bf16[768,256]{1,0:T(8,128)(2,1)S(1)}, u32[]{:S(2)}, u32[]{:S(2)}) collective-permute-start(bf16[768,256]{1,0:T(8,128)(2,1)S(1)} %get-tuple-element.42), channel_id=1, source_target_pairs={{0,29},{1,30},{2,31},{3,0},{4,1},{5,2},{6,3},{7,4},{8,5},{9,6},{10... | collective-permute-start | bytes 1179656 | tf_op jit(solution)/shard_map/ppermute | solution.py:28
  75.6 18.3 %collective-permute-start.12 = (bf16[768,256]{1,0:T(8,128)(2,1)S(1)}, bf16[768,256]{1,0:T(8,128)(2,1)S(1)}, u32[]{:S(2)}, u32[]{:S(2)}) collective-permute-start(bf16[768,256]{1,0:T(8,128)(2,1)S(1)} %get-tuple-element.42), channel_id=1, source_target_pairs={{0,3},{1,4},{2,5},{3,6},{4,7},{5,8},{6,9},{7,10},{8,11},{9,12},{10... | collective-permute-start | bytes 1179656 | tf_op jit(solution)/shard_map/ppermute | solution.py:28
  102.0 2.6 %collective-permute-start.17 = (bf16[1536,256]{1,0:T(8,128)(2,1)}, bf16[1536,256]{1,0:T(8,128)(2,1)S(1)}, u32[]{:S(2)}, u32[]{:S(2)}) collective-permute-start(bf16[1536,256]{1,0:T(8,128)(2,1)} %get-tuple-element.50), channel_id=1, source_target_pairs={{0,1},{1,0},{2,3},{3,2},{4,5},{5,4},{6,7},{7,6},{8,9},{9,8},{10,11... | collective-permute-start | bytes 2359304 | tf_op jit(solution)/shard_map/ppermute | solution.py:699
  106.7 28.7 %all-to-all-start.2 = ((bf16[16,82,256]{2,1,0:T(8,128)(2,1)}), bf16[16,82,256]{2,1,0:T(8,128)(2,1)S(1)}, u32[]{:S(2)}, u32[]{:S(2)}) async-start(bf16[16,82,256]{2,1,0:T(8,128)(2,1)} %shard_map.102), calls=%async_computation.2 | async-start | bytes 1441792 | tf_op jit(solution)/shard_map/all_to_all | solution.py:707
  115.4 15.9 %collective-permute-start.13 = (bf16[144,512]{1,0:T(8,128)(2,1)S(1)}, bf16[144,512]{1,0:T(8,128)(2,1)S(1)}, u32[]{:S(2)}, u32[]{:S(2)}) collective-permute-start(bf16[144,512]{1,0:T(8,128)(2,1)S(1)} %get-tuple-element.45), channel_id=1, source_target_pairs={{64,0},{96,32},{128,64},{160,96},{192,128},{224,160},{65,1},{97,33... | collective-permute-start | bytes 442376 | tf_op jit(solution)/shard_map/ppermute | solution.py:24
  116.7 14.6 %collective-permute-start.15 = (bf16[144,512]{1,0:T(8,128)(2,1)S(1)}, bf16[144,512]{1,0:T(8,128)(2,1)S(1)}, u32[]{:S(2)}, u32[]{:S(2)}) collective-permute-start(bf16[144,512]{1,0:T(8,128)(2,1)S(1)} %get-tuple-element.47), channel_id=1, source_target_pairs={{0,64},{32,96},{64,128},{96,160},{128,192},{160,224},{1,65},{33,97... | collective-permute-start | bytes 442376 | tf_op jit(solution)/shard_map/ppermute | solution.py:24
  121.3 8.9 %collective-permute-start.14 = (bf16[48,512]{1,0:T(8,128)(2,1)S(1)}, bf16[48,512]{1,0:T(8,128)(2,1)S(1)}, u32[]{:S(2)}, u32[]{:S(2)}) collective-permute-start(bf16[48,512]{1,0:T(8,128)(2,1)S(1)} %get-tuple-element.46), channel_id=1, source_target_pairs={{96,0},{128,32},{160,64},{192,96},{224,128},{97,1},{129,33},{161,6... | collective-permute-start | bytes 147464 | tf_op jit(solution)/shard_map/ppermute | solution.py:24
  122.6 8.7 %collective-permute-start.16 = (bf16[48,512]{1,0:T(8,128)(2,1)S(1)}, bf16[48,512]{1,0:T(8,128)(2,1)S(1)}, u32[]{:S(2)}, u32[]{:S(2)}) collective-permute-start(bf16[48,512]{1,0:T(8,128)(2,1)S(1)} %get-tuple-element.48), channel_id=1, source_target_pairs={{0,96},{32,128},{64,160},{96,192},{128,224},{1,97},{33,129},{65,16... | collective-permute-start | bytes 147464 | tf_op jit(solution)/shard_map/ppermute | solution.py:24
  130.1 11.2 %copy-start.12 = (bf16[48,512]{1,0:T(8,128)(2,1)}, bf16[48,512]{1,0:T(8,128)(2,1)S(1)}, u32[]{:S(2)}) copy-start(bf16[48,512]{1,0:T(8,128)(2,1)S(1)} %collective-permute-done.14.up_far_ref.refs_1_) | copy-start | bytes 147460
  131.3 10.1 %copy-start.8 = (bf16[144,512]{1,0:T(8,128)(2,1)}, bf16[144,512]{1,0:T(8,128)(2,1)S(1)}, u32[]{:S(2)}) copy-start(bf16[144,512]{1,0:T(8,128)(2,1)S(1)} %collective-permute-done.15.down_near_ref.refs_2_) | copy-start | bytes 442372
  136.2 14.4 %all-to-all-start.3 = ((bf16[8,82,256]{2,1,0:T(8,128)(2,1)}), bf16[8,82,256]{2,1,0:T(8,128)(2,1)S(1)}, u32[]{:S(2)}, u32[]{:S(2)}) async-start(bf16[8,82,256]{2,1,0:T(8,128)(2,1)} %shard_map.103), calls=%async_computation.3 | async-start | bytes 720896 | tf_op jit(solution)/shard_map/all_to_all | solution.py:709
  (10 other events, 45.8 us)
